TPU v7x, 256 devices: a whole 4x4x8 slice. The times are simulated.
256 devices in a mesh: leaf: 16 (over y_hi, z), panel: 16 (over x, y_lo, core).
Axes of the slice: x: 4, y: 4 (y_hi: 2, y_lo: 2; y = y_hi * 2 + y_lo), z: 8, core: 2. Of those that a mesh axis runs over, the one named last changes fastest.
Arguments:
- a21: bfloat16 [16, 16384, 256], P('leaf', 'panel'), may hold values from -1.5 to 1.5
- l11_inv: bfloat16 [16, 256, 256], P('leaf'), as said below
- a22: bfloat16 [16, 16384, 2048], P('leaf', 'panel'), may hold values from -6 to 6
- tasks: int32 [16, 128], P('leaf', 'panel'), may hold values from 0 to 16
- emap: int32 [16, 128], P('leaf', 'panel'), may hold values from 0 to 7, as said below
- parent_in: float32 [16384, 2048], P('panel', 'leaf'), may hold values from -6 to 6
Outputs:
- l21: bfloat16 [16, 16384, 256], P('leaf', 'panel')
- parent_out: float32 [16384, 2048], P('panel', 'leaf')
Inputs may be any that keep to these rules, and one draw needn't show every extreme that they name: `l11_inv`: lower triangular with positive diagonal. `emap`: the 8 row tiles of one front on one device go to the 8 parent tiles of that device in some order (a permutation of 0 to 7).
All inputs are finite; a program needn't handle non-finite values.
Results may differ from a plain program's by a relative error of at most 0.017.
Values may be sent and summed in bfloat16 or wider, within the bound.
No kernel may reach another device: no remote copies, remote signals or barrier semaphores. Data moves between devices by JAX's collectives and lax.ppermute only.
A program may use at most 64 MiB of HBM per device.

v0:
```python
import jax
import jax.numpy as jnp
from jax import lax
from jax.sharding import PartitionSpec as P

TILE = 128
WIN_DEV = 128
PT_DEV = 8


def on_device(a21, l11_inv, a22, tasks, emap, parent_in):
    factor = lax.dot_general(
        a21[0], l11_inv[0], (((1,), (1,)), ((), ())), preferred_element_type=jnp.float32
    ).astype(jnp.bfloat16)
    row_count = factor.shape[0]
    tiles_dev = row_count // TILE
    leading = factor[:WIN_DEV]
    limits = jnp.repeat(tasks[0] * TILE, TILE)
    trailing = a22[0]
    column_span = trailing.shape[1]
    window_piece = lax.all_gather(leading, "panel", axis=0, tiled=True)
    columns = jnp.arange(window_piece.shape[0])
    values = lax.dot_general(
        factor, window_piece, (((1,), (1,)), ((), ())), preferred_element_type=jnp.float32
    )
    update = jnp.where(columns[None, :] < limits[:, None], values, 0.0)
    contribution = (trailing.astype(jnp.float32) - update).astype(jnp.bfloat16)
    onehot = (emap[0][:, None] == jnp.arange(PT_DEV)[None, :]).astype(jnp.bfloat16)
    blocks = contribution.reshape(tiles_dev, TILE, column_span)
    placed = jnp.einsum("tk,trw->krw", onehot, blocks, preferred_element_type=jnp.float32)
    arrivals = lax.psum_scatter(
        placed.reshape(PT_DEV * TILE, column_span).astype(jnp.bfloat16),
        "leaf",
        scatter_dimension=1,
        tiled=True,
    ).astype(jnp.float32)
    return (factor[None], parent_in + arrivals)


def solution(mesh):
    return jax.shard_map(
        on_device,
        mesh=mesh,
        in_specs=(
            P("leaf", "panel", None),
            P("leaf", None, None),
            P("leaf", "panel", None),
            P("leaf", "panel"),
            P("leaf", "panel"),
            P("panel", "leaf"),
        ),
        out_specs=(P("leaf", "panel", None), P("panel", "leaf")),
        check_vma=False,
    )
```

profile of v0, /device:TPU:6, one launch (start us, length us, event | category | flops | bytes accessed | tf_op | source)
XLA Modules:
  0.0 283.2 jit_solution(12639009565058784309)
XLA Ops:
  7.2 0.0 copy-start
  7.2 0.0 all-gather.2.cloned.1.call-start
  7.2 1.0 copy-done
  8.2 1.2 convolution_convert_fusion
  9.5 0.0 copy-start.1
  9.5 0.7 slice.4
  10.2 0.0 all-gather.2.cloned.1.call-update
  10.2 0.0 reduce-scatter.4.cloned.1.call-start
  10.2 0.7 multiply_bitcast_fusion
  10.9 0.1 broadcast_bitcast_fusion
  11.0 0.0 copy-start.3
  11.0 36.5 %all-gather.2.cloned.1.call-done = bf16[2048,256]{1,0:T(8,128)(2,1)} async-done(((bf16[128,256]{1,0:T(8,128)(2,1)}), bf16[2048,256]{1,0:T(8,128)(2,1)}) %all-gather.2.cloned.1.call-update) | async-done | bytes 1048592 | tf_op jit(solution)/shard_map/all_gather | solution.py:21
  47.4 3.8 %fusion = bf16[1024,2048]{1,0:T(8,128)(2,1)S(1)} fusion(bf16[1024,256]{1,0:T(8,128)(2,1)S(1)} %convolution_convert_fusion, bf16[2048,256]{1,0:T(8,128)(2,1)} %all-gather.2.cloned.1.call-done, bf16[1,1024,2048]{2,1,0:T(8,128)(2,1)} %param.8, s32[1024]{0:T(1024)S(1)} %broadcast_bitcast_fusion), kind=kOutput, calls=%fused_computation.1 | convolution fusion | flops 1084227584 | bytes 9965568 | tf_op jit(solution)/shard_map/dot_general | solution.py:23
  51.3 0.0 copy-done.1
  51.3 0.0 copy-done.3
  51.3 2.9 %fusion.3 = bf16[8,128,2048]{2,0,1:T(8,128)(2,1)S(1)} fusion(bf16[8,128,2048]{2,1,0:T(8,128)(2,1)S(1)} %bitcast.26, s32[8]{0:T(128)S(1)} %bitcast.29), kind=kOutput, calls=%fused_computation.5 | convolution fusion | flops 35651648 | bytes 8388640 | tf_op jit(solution)/shard_map/tk,trw->krw/dot_general | solution.py:30
  54.2 4.3 %copy.12 = bf16[8,128,2048]{2,1,0:T(8,128)(2,1)} copy(bf16[8,128,2048]{2,0,1:T(8,128)(2,1)S(1)} %fusion.3) | data formatting | bytes 8388608 | tf_op jit(solution)/shard_map/convert_element_type | solution.py:32
  58.5 6.4 %copy.13 = bf16[1024,2048]{0,1:T(8,128)(2,1)} copy(bf16[1024,2048]{1,0:T(8,128)(2,1)} %bitcast.25) | data formatting | bytes 8388608
  64.8 0.0 copy-start.2
  64.9 0.0 reduce-scatter.4.cloned.1.call-update
  64.9 209.6 %reduce-scatter.4.cloned.1.call-done = bf16[128,1024]{1,0:T(8,128)(2,1)} async-done(((bf16[2048,1024]{1,0:T(8,128)(2,1)}), bf16[128,1024]{1,0:T(8,128)(2,1)}) %reduce-scatter.4.cloned.1.call-update) | async-done | bytes 262160
  274.4 1.1 copy.14
  275.6 0.0 copy-done.2
  275.6 0.8 convert_add_fusion
Async XLA Ops:
  7.2 1.0 copy-start
  7.2 40.3 %all-gather.2.cloned.1.call-start = ((), (), s32[]{:S(2)}) async-start(), calls=%async_computation.1 | async-start | bytes 1114112 | tf_op jit(solution)/shard_map/all_gather | solution.py:21
  9.5 41.8 %copy-start.1 = (bf16[1024,256]{1,0:T(8,128)(2,1)}, bf16[1024,256]{1,0:T(8,128)(2,1)S(1)}, u32[]{:S(2)}) copy-start(bf16[1024,256]{1,0:T(8,128)(2,1)S(1)} %convolution_convert_fusion) | copy-start | bytes 1572868
  10.2 264.3 %reduce-scatter.4.cloned.1.call-start = ((), (), s32[]{:S(2)}) async-start(), calls=%async_computation.2 | async-start | bytes 4456448
  11.0 40.3 %copy-start.3 = (s32[1,8]{1,0:T(1,128)S(1)}, s32[1,8]{1,0:T(1,128)}, u32[]{:S(2)}) copy-start(s32[1,8]{1,0:T(1,128)} %param.10) | copy-start | bytes 100
  64.8 210.7 %copy-start.2 = (f32[1024,128]{1,0:T(8,128)S(1)}, f32[1024,128]{1,0:T(8,128)}, u32[]{:S(2)}) copy-start(f32[1024,128]{1,0:T(8,128)} %param.11) | copy-start | bytes 1572868
Sparse Core Ops, SparseCore 0:
  10.4 36.9 all-gather.1
  65.0 209.3 reduce-scatter.3
where the time goes:
time: 284 us; the launch traced here: 283 us
  waiting for transfers between devices  246 us (87%)
  between operations  14.1 us (5%)
  local copies, waits for them, and re-layouts  13.6 us (5%)
  matrix products  7.94 us (3%)
    unnamed x3, waiting for transfers between devices  210 us
    all_gather x1, waiting for transfers between devices, on_device(): window_piece = lax.all_gather(leading, 'panel', axis=0, tiled=True)  36.5 us
    unnamed x10, local copies, waits for them, and re-layouts  8.51 us
  transfers between devices with their start and end apart: 2, of which 2 were waited for; matrix products, arithmetic and copies ran while one was open for 0% of the time, Pallas kernels for 0%

commit v1 on v0

v1 whole, which is shorter than its diff:
```python
import jax
import jax.numpy as jnp
from jax import lax
from jax.experimental import pallas as pl
from jax.experimental.pallas import tpu as pltpu
from jax.sharding import PartitionSpec as P

TILE = 128
TILES_DEV = 8
ROWS_DEV = TILES_DEV * TILE
PW = 256
STREAMS = 2
BF16 = jnp.bfloat16
F32 = jnp.float32


def leaf_perm(dz, dy):
    pairs = []
    for y in range(2):
        for z in range(8):
            pairs.append((y * 8 + z, (y ^ dy) * 8 + (z + dz) % 8))
    return pairs


def panel_perm(dx, dl, dc):
    pairs = []
    for x in range(4):
        for low in range(2):
            for core in range(2):
                target = ((x + dx) % 4) * 4 + (low ^ dl) * 2 + (core ^ dc)
                pairs.append((x * 4 + low * 2 + core, target))
    return pairs


def to_leaf(value, dz, dy=0):
    return lax.ppermute(value, "leaf", leaf_perm(dz, dy))


def to_panel(value, dx=0, dl=0, dc=0):
    return lax.ppermute(value, "panel", panel_perm(dx, dl, dc))


def destination(scalars, step, other):
    leaf = scalars[0]
    return ((leaf // 8) ^ other) * 8 + (leaf + step + 8) % 8


def window_slot(scalars, step, other):
    tile = destination(scalars, step, other)
    panel = scalars[1]
    ahead = (tile // 4 - panel // 4 + 4) % 4
    place = jnp.where(ahead == 0, 0, jnp.where(ahead == 3, 1, ahead + 1))
    return place * 2 + ((tile // 2) % 2 ^ (panel // 2) % 2)


def contribution_kernel(steps, sinks, scalars, factor, *refs):
    count = len(steps)
    trailing = refs[: 2 * count]
    own = refs[2 * count : 4 * count]
    across = refs[4 * count : 6 * count]
    outs = refs[6 * count :]
    core = scalars[1] % 2
    for at, step in enumerate(steps):
        pieces = []
        limits = []
        for other in range(2):
            tile = destination(scalars, step, other)
            mine = (tile % 2) == core
            pieces.append(jnp.where(mine, own[2 * at + other][0], across[2 * at + other][0]))
            limits.append(tile)
        weights = jnp.concatenate(pieces, axis=0)
        for k in range(TILES_DEV):
            child = scalars[2 + k]
            planned = scalars[10 + child]
            rows = pl.ds(pl.multiple_of(child * TILE, TILE), TILE)
            update = lax.dot_general(
                factor[rows, :], weights, (((1,), (1,)), ((), ())), preferred_element_type=F32
            )
            for other in range(2):
                part = update[:, other * TILE : (other + 1) * TILE]
                part = jnp.where(limits[other] < planned, part, 0.0)
                value = (trailing[2 * at + other][rows, :].astype(F32) - part).astype(BF16)
                sinks[(step, other)](outs, k, value)


def contributions(steps, out_shapes, sinks, scalars, factor, trailing, own, across):
    def column(step, other):
        return pl.BlockSpec((ROWS_DEV, TILE), lambda i, s: (0, destination(s, step, other)))

    def piece(step, other):
        return pl.BlockSpec((1, TILE, PW), lambda i, s: (window_slot(s, step, other), 0, 0))

    pairs = [(step, other) for step in steps for other in range(2)]

    def body(s, f, *refs):
        contribution_kernel(steps, sinks, s, f, *refs)

    return pl.pallas_call(
        body,
        out_shape=[jax.ShapeDtypeStruct(shape, BF16) for shape in out_shapes],
        grid_spec=pltpu.PrefetchScalarGridSpec(
            num_scalar_prefetch=1,
            grid=(1,),
            in_specs=[pl.BlockSpec((ROWS_DEV, PW), lambda i, s: (0, 0))]
            + [column(*pair) for pair in pairs]
            + [piece(*pair) for pair in pairs]
            + [piece(*pair) for pair in pairs],
            out_specs=[
                pl.BlockSpec(shape, lambda i, s, rank=len(shape): (0,) * rank) for shape in out_shapes
            ],
        ),
        compiler_params=pltpu.CompilerParams(vmem_limit_bytes=24 * 1024 * 1024),
        cost_estimate=pl.CostEstimate(
            flops=2 * ROWS_DEV * PW * 2 * TILE * len(steps),
            bytes_accessed=(1 + 2 * len(steps)) * ROWS_DEV * PW * 2,
            transcendentals=0,
        ),
    )(scalars, factor, *([trailing] * len(pairs)), *([own] * len(pairs)), *([across] * len(pairs)))


def into(slot, lead=None):
    def sink(outs, k, value):
        per = TILES_DEV // STREAMS
        group, inner = divmod(k, per)
        rows = pl.ds(inner * TILE, TILE)
        per_stream = len(outs) // STREAMS
        out = outs[group * per_stream + slot]
        if lead is None:
            out[rows, :] = value
        else:
            out[lead, rows, :] = value

    return sink


def add(*terms):
    total = terms[0].astype(F32)
    for term in terms[1:]:
        total = total + term.astype(F32)
    return total


def on_device(a21, l11_inv, a22, tasks, emap, parent_in):
    a21, l11_inv, a22 = a21[0], l11_inv[0], a22[0]

    def solve(rows):
        return lax.dot_general(
            rows, l11_inv, (((1,), (1,)), ((), ())), preferred_element_type=F32
        ).astype(BF16)

    lead = solve(a21[:TILE])
    pair = jnp.stack([lead, to_panel(lead, dl=1)])
    own = jnp.concatenate([pair, to_panel(pair, dx=1), to_panel(pair, dx=-1), to_panel(pair, dx=2)])
    across = to_panel(own, dc=1)

    factor = solve(a21)
    order = jnp.arange(TILES_DEV, dtype=jnp.int32)
    children = jnp.sum(jnp.where(emap[0][None, :] == order[:, None], order[None, :], 0), axis=1)
    scalars = jnp.concatenate(
        [
            lax.axis_index("leaf").astype(jnp.int32)[None],
            lax.axis_index("panel").astype(jnp.int32)[None],
            children.astype(jnp.int32),
            tasks[0],
        ]
    )
    rows = ROWS_DEV // STREAMS
    one, two, three = (rows, TILE), (2, rows, TILE), (3, rows, TILE)

    def run(steps, shapes, sinks):
        flat = contributions(steps, shapes * STREAMS, sinks, scalars, factor, a22, own, across)
        return [flat[g * len(shapes) : (g + 1) * len(shapes)] for g in range(STREAMS)]

    far = run([4], [one, one], {(4, 0): into(0), (4, 1): into(1)})
    up, down = [], []
    for g in range(STREAMS):
        up.append(to_leaf(far[g][0], 1))
        down.append(to_leaf(far[g][1], -1))
    third = run(
        [3, -3],
        [two, two],
        {(3, 0): into(0, 0), (3, 1): into(0, 1), (-3, 0): into(1, 0), (-3, 1): into(1, 1)},
    )
    near = run(
        [1, -1, 0],
        [one, one, one, three],
        {
            (1, 0): into(0),
            (-1, 0): into(1),
            (0, 0): into(2),
            (1, 1): into(3, 0),
            (-1, 1): into(3, 1),
            (0, 1): into(3, 2),
        },
    )
    direct = [to_leaf(near[g][3], 0, 1) for g in range(STREAMS)]
    second = run(
        [2, -2],
        [one, one, one, one],
        {(2, 0): into(0), (2, 1): into(1), (-2, 0): into(2), (-2, 1): into(3)},
    )
    for g in range(STREAMS):
        c3p, c3m = third[g]
        up[g] = to_leaf(jnp.stack([add(c3p[0], up[g]).astype(BF16), c3p[1]]), 1)
        down[g] = to_leaf(jnp.stack([c3m[0], add(c3m[1], down[g]).astype(BF16)]), -1)
    for g in range(STREAMS):
        c2ps, c2po, c2ms, c2mo = second[g]
        up[g] = (
            to_leaf(add(c2ps, up[g][0]).astype(BF16), 1),
            to_leaf(add(c2po, up[g][1]).astype(BF16), 1, 1),
        )
        down[g] = (
            to_leaf(add(c2ms, down[g][0]).astype(BF16), -1),
            to_leaf(add(c2mo, down[g][1]).astype(BF16), -1, 1),
        )
    total = []
    for g in range(STREAMS):
        c1p, c1m, c0, _ = near[g]
        up[g] = to_leaf(add(c1p, direct[g][0], *up[g]).astype(BF16), 1)
        down[g] = to_leaf(add(c1m, direct[g][1], *down[g]).astype(BF16), -1)
        total.append(add(c0, direct[g][2], up[g], down[g]))
    return (factor[None], parent_in + jnp.concatenate(total))


def solution(mesh):
    return jax.shard_map(
        on_device,
        mesh=mesh,
        in_specs=(
            P("leaf", "panel", None),
            P("leaf", None, None),
            P("leaf", "panel", None),
            P("leaf", "panel"),
            P("leaf", "panel"),
            P("panel", "leaf"),
        ),
        out_specs=(P("leaf", "panel", None), P("panel", "leaf")),
        check_vma=False,
    )
```

time: 284 us -> 93.3 us (0.33)
  waiting for transfers between devices: 246 us -> 25.8 us
  starting transfers between devices: 0.08 us -> 50.6 us
  between operations: 14.1 us -> 1.01 us
  local copies, waits for them, and re-layouts: 13.6 us -> 3.36 us
  Pallas kernels: 0 us -> 6.18 us
  matrix products: 7.94 us -> 2.4 us
    unnamed x3 -> x0, waiting for transfers between devices: 210 us -> none
    ppermute x0 -> x27, starting transfers between devices: none -> 50.6 us  [the longest x22 44.1 us: to_leaf(): return lax.ppermute(value, 'leaf', leaf_perm(dz, dy))]
    all_gather x1 -> x0, waiting for transfers between devices: 36.5 us -> none  [on_device(): window_piece = lax.all_gather(leading, 'panel', axis=0, tiled=True)]
    ppermute x0 -> x27, waiting for transfers between devices: none -> 25.8 us  [the longest x22 19.4 us: to_leaf(): return lax.ppermute(value, 'leaf', leaf_perm(dz, dy))]
    pallas_call x0 -> x4, Pallas kernels: none -> 6.18 us  [contributions(): pl.pallas_call(body, out_shape=[jax.ShapeDtypeStruct(shape, BF16) for sha...]
    dot_general x3 -> x2, matrix products: 7.94 us -> 2.4 us  [solve(): lax.dot_general(rows, l11_inv, (((1,), (1,)), ((), ())), preferred_elemen...]
    unnamed x10 -> x11, local copies, waits for them, and re-layouts: 8.51 us -> 3.31 us
    convert_element_type x1 -> x0, local copies, waits for them, and re-layouts: 4.28 us -> none  [on_device(): placed.reshape(PT_DEV * TILE, column_span).astype(jnp.bfloat16)]
  transfers between devices with their start and end apart: 2 -> 27, of which waited for: 2 -> 10; matrix products, arithmetic and copies ran while one was open for 0% -> 4% of each run, Pallas kernels for 0% -> 5%
where the time goes in v1:
time: 93.3 us; the launch traced here: 92.7 us
  starting transfers between devices  50.6 us (54%)
  waiting for transfers between devices  25.8 us (28%)
  Pallas kernels  6.18 us (7%)
  local copies, waits for them, and re-layouts  3.36 us (4%)
  other arithmetic  3.34 us (4%)
  matrix products  2.4 us (3%)
  between operations  1.01 us (1%)
    ppermute x22, starting transfers between devices, to_leaf(): return lax.ppermute(value, 'leaf', leaf_perm(dz, dy))  44.1 us
    ppermute x22, waiting for transfers between devices, to_leaf(): return lax.ppermute(value, 'leaf', leaf_perm(dz, dy))  19.4 us
    ppermute x5, starting transfers between devices, to_panel(): return lax.ppermute(value, 'panel', panel_perm(dx, dl, dc))  6.48 us
    ppermute x5, waiting for transfers between devices, to_panel(): return lax.ppermute(value, 'panel', panel_perm(dx, dl, dc))  6.43 us
    pallas_call x4, Pallas kernels, contributions(): pl.pallas_call(body, out_shape=[jax.ShapeDtypeStruct(shape, BF16) for sha...  6.18 us
    unnamed x11, local copies, waits for them, and re-layouts  3.31 us
    dot_general x2, matrix products, solve(): lax.dot_general(rows, l11_inv, (((1,), (1,)), ((), ())), preferred_elemen...  2.4 us
  transfers between devices with their start and end apart: 27, of which 10 were waited for; matrix products, arithmetic and copies ran while one was open for 4% of the time, Pallas kernels for 5%

profile of v1, /device:TPU:6, one launch (start us, length us, event | category | flops | bytes accessed | tf_op | source)
XLA Modules:
  0.0 92.7 jit_solution(10396879356767430160)
XLA Ops:
  2.6 1.7 %collective-permute-start = (bf16[128,256]{1,0:T(8,128)(2,1)S(1)}, bf16[128,256]{1,0:T(8,128)(2,1)S(1)}, u32[]{:S(2)}, u32[]{:S(2)}) collective-permute-start(bf16[128,256]{1,0:T(8,128)(2,1)S(1)} %get-tuple-element.63), channel_id=1, source_target_pairs={{0,2},{1,3},{2,0},{3,1},{4,6},{5,7},{6,4},{7,5},{8,10},{9,11},{10,... | collective-permute-start | bytes 196616 | tf_op jit(solution)/shard_map/ppermute | solution.py:40
  4.2 2.7 %collective-permute-done = bf16[128,256]{1,0:T(8,128)(2,1)S(1)} collective-permute-done((bf16[128,256]{1,0:T(8,128)(2,1)S(1)}, bf16[128,256]{1,0:T(8,128)(2,1)S(1)}, u32[]{:S(2)}, u32[]{:S(2)}) %collective-permute-start) | collective-permute-done | bytes 65568 | tf_op jit(solution)/shard_map/ppermute | solution.py:40
  8.4 1.7 %collective-permute-start.2 = (bf16[2,128,256]{2,1,0:T(8,128)(2,1)S(1)}, bf16[2,128,256]{2,1,0:T(8,128)(2,1)S(1)}, u32[]{:S(2)}, u32[]{:S(2)}) collective-permute-start(bf16[2,128,256]{2,1,0:T(8,128)(2,1)S(1)} %pad_maximum_fusion.4), channel_id=1, source_target_pairs={{0,12},{1,13},{2,14},{3,15},{4,0},{5,1},{6,2},{7,3},{8,4},{9,5},{1... | collective-permute-start | bytes 393224 | tf_op jit(solution)/shard_map/ppermute | solution.py:40
  10.1 1.6 %collective-permute-start.1 = (bf16[2,128,256]{2,1,0:T(8,128)(2,1)S(1)}, bf16[2,128,256]{2,1,0:T(8,128)(2,1)S(1)}, u32[]{:S(2)}, u32[]{:S(2)}) collective-permute-start(bf16[2,128,256]{2,1,0:T(8,128)(2,1)S(1)} %pad_maximum_fusion.4), channel_id=1, source_target_pairs={{0,4},{1,5},{2,6},{3,7},{4,8},{5,9},{6,10},{7,11},{8,12},{9,13},{1... | collective-permute-start | bytes 393224 | tf_op jit(solution)/shard_map/ppermute | solution.py:40
  11.7 3.4 %collective-permute-done.1 = bf16[2,128,256]{2,1,0:T(8,128)(2,1)S(1)} collective-permute-done((bf16[2,128,256]{2,1,0:T(8,128)(2,1)S(1)}, bf16[2,128,256]{2,1,0:T(8,128)(2,1)S(1)}, u32[]{:S(2)}, u32[]{:S(2)}) %collective-permute-start.1) | collective-permute-done | bytes 131104 | tf_op jit(solution)/shard_map/ppermute | solution.py:40
  18.5 2.4 %copy-done.1 = bf16[1,1024,2048]{2,1,0:T(8,128)(2,1)S(1)} copy-done((bf16[1,1024,2048]{2,1,0:T(8,128)(2,1)S(1)}, bf16[1,1024,2048]{2,1,0:T(8,128)(2,1)}, u32[]{:S(2)}) %copy-start.1) | copy-done | bytes 4194328
  22.0 5.9 %collective-permute-start.22 = (bf16[512,128]{1,0:T(8,128)(2,1)S(1)}, bf16[512,128]{1,0:T(8,128)(2,1)S(1)}, u32[]{:S(2)}, u32[]{:S(2)}) collective-permute-start(bf16[512,128]{1,0:T(8,128)(2,1)S(1)} %get-tuple-element.48), channel_id=1, source_target_pairs={{0,112},{16,0},{32,16},{48,32},{64,48},{80,64},{96,80},{112,96},{1... | collective-permute-start | bytes 393224 | tf_op jit(solution)/shard_map/ppermute | solution.py:36
  27.9 3.2 %collective-permute-start.11 = (bf16[512,128]{1,0:T(8,128)(2,1)S(1)}, bf16[512,128]{1,0:T(8,128)(2,1)S(1)}, u32[]{:S(2)}, u32[]{:S(2)}) collective-permute-start(bf16[512,128]{1,0:T(8,128)(2,1)S(1)} %get-tuple-element.36), channel_id=1, source_target_pairs={{0,112},{16,0},{32,16},{48,32},{64,48},{80,64},{96,80},{112,96},{1... | collective-permute-start | bytes 393224 | tf_op jit(solution)/shard_map/ppermute | solution.py:36
  31.2 1.5 %shard_map.79 = (bf16[2,512,128]{2,1,0:T(8,128)(2,1)S(1)}, bf16[2,512,128]{2,1,0:T(8,128)(2,1)S(1)}, bf16[2,512,128]{2,1,0:T(8,128)(2,1)S(1)}, bf16[2,512,128]{2,1,0:T(8,128)(2,1)S(1)}) custom-call(s32[18]{0:T(128)S(1)} %pad_add_fusion.s, bf16[1024,256]{1,0:T(8,128)(2,1)S(1)} %convolution_convert_fusion.f, bf16[1024,2048]{1,0:T(8,128)(2,1)S(1)} %bitcast.117, ...), custom_call_target="tpu_custom_call" | custom-call | flops 268435456 | bytes 2621440 | tf_op jit(solution)/shard_map/pallas_call | solution.py:98
  32.8 2.0 %shard_map.77 = (bf16[512,128]{1,0:T(8,128)(2,1)S(1)}, bf16[512,128]{1,0:T(8,128)(2,1)S(1)}, bf16[512,128]{1,0:T(8,128)(2,1)S(1)}, bf16[3,512,128]{2,1,0:T(8,128...) custom-call(s32[18]{0:T(128)S(1)} %pad_add_fusion.s, ...), custom_call_target="tpu_custom_call" | custom-call | flops 402653184 | bytes 3670016 | tf_op jit(solution)/shard_map/pallas_call | solution.py:98
  34.8 3.3 %collective-permute-start.5 = (bf16[3,512,128]{2,1,0:T(8,128)(2,1)S(1)}, bf16[3,512,128]{2,1,0:T(8,128)(2,1)S(1)}, u32[]{:S(2)}, u32[]{:S(2)}) collective-permute-start(bf16[3,512,128]{2,1,0:T(8,128)(2,1)S(1)} %get-tuple-element.27), channel_id=1, source_target_pairs={{0,128},{16,144},{32,160},{48,176},{64,192},{80,208},{96,224},{112... | collective-permute-start | bytes 1179656 | tf_op jit(solution)/shard_map/ppermute | solution.py:36
  38.1 1.5 %shard_map.78 = (bf16[512,128]{1,0:T(8,128)(2,1)S(1)}, bf16[512,128]{1,0:T(8,128)(2,1)S(1)}, bf16[512,128]{1,0:T(8,128)(2,1)S(1)}, bf16[512,128]{1,0:T(8,128)(2,...) custom-call(s32[18]{0:T(128)S(1)} %pad_add_fusion.s, ...), custom_call_target="tpu_custom_call" | custom-call | flops 268435456 | bytes 2621440 | tf_op jit(solution)/shard_map/pallas_call | solution.py:98
  40.1 3.3 %collective-permute-start.23 = (bf16[2,512,128]{2,1,0:T(8,128)(2,1)S(1)}, bf16[2,512,128]{2,1,0:T(8,128)(2,1)S(1)}, u32[]{:S(2)}, u32[]{:S(2)}) collective-permute-start(bf16[2,512,128]{2,1,0:T(8,128)(2,1)S(1)} %pad_maximum_fusion.3), channel_id=1, source_target_pairs={{0,112},{16,0},{32,16},{48,32},{64,48},{80,64},{96,80},{112,96},{1... | collective-permute-start | bytes 786440 | tf_op jit(solution)/shard_map/ppermute | solution.py:36
  43.9 3.3 %collective-permute-start.12 = (bf16[2,512,128]{2,1,0:T(8,128)(2,1)S(1)}, bf16[2,512,128]{2,1,0:T(8,128)(2,1)S(1)}, u32[]{:S(2)}, u32[]{:S(2)}) collective-permute-start(bf16[2,512,128]{2,1,0:T(8,128)(2,1)S(1)} %pad_maximum_fusion.1), channel_id=1, source_target_pairs={{0,112},{16,0},{32,16},{48,32},{64,48},{80,64},{96,80},{112,96},{1... | collective-permute-start | bytes 786440 | tf_op jit(solution)/shard_map/ppermute | solution.py:36
  47.3 6.3 %collective-permute-done.12 = bf16[2,512,128]{2,1,0:T(8,128)(2,1)S(1)} collective-permute-done((bf16[2,512,128]{2,1,0:T(8,128)(2,1)S(1)}, bf16[2,512,128]{2,1,0:T(8,128)(2,1)S(1)}, u32[]{:S(2)}, u32[]{:S(2)}) %collective-permute-start.12) | collective-permute-done | bytes 262176 | tf_op jit(solution)/shard_map/ppermute | solution.py:36
  53.7 3.8 %collective-permute-start.13 = (bf16[512,128]{1,0:T(8,128)(2,1)S(1)}, bf16[512,128]{1,0:T(8,128)(2,1)S(1)}, u32[]{:S(2)}, u32[]{:S(2)}) collective-permute-start(bf16[512,128]{1,0:T(8,128)(2,1)S(1)} %get-tuple-element.56), channel_id=1, source_target_pairs={{0,112},{16,0},{32,16},{48,32},{64,48},{80,64},{96,80},{112,96},{1... | collective-permute-start | bytes 393224 | tf_op jit(solution)/shard_map/ppermute | solution.py:36
  57.5 4.1 %collective-permute-done.7 = bf16[2,512,128]{2,1,0:T(8,128)(2,1)S(1)} collective-permute-done((bf16[2,512,128]{2,1,0:T(8,128)(2,1)S(1)}, bf16[2,512,128]{2,1,0:T(8,128)(2,1)S(1)}, u32[]{:S(2)}, u32[]{:S(2)}) %collective-permute-start.7) | collective-permute-done | bytes 262176 | tf_op jit(solution)/shard_map/ppermute | solution.py:36
  61.7 5.1 %collective-permute-start.14 = (bf16[512,128]{1,0:T(8,128)(2,1)S(1)}, bf16[512,128]{1,0:T(8,128)(2,1)S(1)}, u32[]{:S(2)}, u32[]{:S(2)}) collective-permute-start(bf16[512,128]{1,0:T(8,128)(2,1)S(1)} %get-tuple-element.57), channel_id=1, source_target_pairs={{0,240},{16,128},{32,144},{48,160},{64,176},{80,192},{96,208},{112... | collective-permute-start | bytes 393224 | tf_op jit(solution)/shard_map/ppermute | solution.py:36
  67.1 3.2 %collective-permute-start.24 = (bf16[512,128]{1,0:T(8,128)(2,1)S(1)}, bf16[512,128]{1,0:T(8,128)(2,1)S(1)}, u32[]{:S(2)}, u32[]{:S(2)}) collective-permute-start(bf16[512,128]{1,0:T(8,128)(2,1)S(1)} %get-tuple-element.60), channel_id=1, source_target_pairs={{0,112},{16,0},{32,16},{48,32},{64,48},{80,64},{96,80},{112,96},{1... | collective-permute-start | bytes 393224 | tf_op jit(solution)/shard_map/ppermute | solution.py:36
  70.4 4.9 %collective-permute-start.25 = (bf16[512,128]{1,0:T(8,128)(2,1)S(1)}, bf16[512,128]{1,0:T(8,128)(2,1)S(1)}, u32[]{:S(2)}, u32[]{:S(2)}) collective-permute-start(bf16[512,128]{1,0:T(8,128)(2,1)S(1)} %get-tuple-element.61), channel_id=1, source_target_pairs={{0,240},{16,128},{32,144},{48,160},{64,176},{80,192},{96,208},{112... | collective-permute-start | bytes 393224 | tf_op jit(solution)/shard_map/ppermute | solution.py:36
  77.1 3.9 %collective-permute-start.15 = (bf16[512,128]{1,0:T(8,128)(2,1)S(1)}, bf16[512,128]{1,0:T(8,128)(2,1)S(1)}, u32[]{:S(2)}, u32[]{:S(2)}) collective-permute-start(bf16[512,128]{1,0:T(8,128)(2,1)S(1)} %get-tuple-element.51), channel_id=1, source_target_pairs={{0,112},{16,0},{32,16},{48,32},{64,48},{80,64},{96,80},{112,96},{1... | collective-permute-start | bytes 393224 | tf_op jit(solution)/shard_map/ppermute | solution.py:36
  81.5 3.9 %collective-permute-done.20 = bf16[512,128]{1,0:T(8,128)(2,1)S(1)} collective-permute-done((bf16[512,128]{1,0:T(8,128)(2,1)S(1)}, bf16[512,128]{1,0:T(8,128)(2,1)S(1)}, u32[]{:S(2)}, u32[]{:S(2)}) %collective-permute-start.20) | collective-permute-done | bytes 131104 | tf_op jit(solution)/shard_map/ppermute | solution.py:36
  85.6 3.2 %collective-permute-start.26 = (bf16[512,128]{1,0:T(8,128)(2,1)S(1)}, bf16[512,128]{1,0:T(8,128)(2,1)S(1)}, u32[]{:S(2)}, u32[]{:S(2)}) collective-permute-start(bf16[512,128]{1,0:T(8,128)(2,1)S(1)} %get-tuple-element.53), channel_id=1, source_target_pairs={{0,112},{16,0},{32,16},{48,32},{64,48},{80,64},{96,80},{112,96},{1... | collective-permute-start | bytes 393224 | tf_op jit(solution)/shard_map/ppermute | solution.py:36
  88.9 2.9 %collective-permute-done.21 = bf16[512,128]{1,0:T(8,128)(2,1)S(1)} collective-permute-done((bf16[512,128]{1,0:T(8,128)(2,1)S(1)}, bf16[512,128]{1,0:T(8,128)(2,1)S(1)}, u32[]{:S(2)}, u32[]{:S(2)}) %collective-permute-start.21) | collective-permute-done | bytes 131104 | tf_op jit(solution)/shard_map/ppermute | solution.py:36
  (72 shorter events, 13.0 us)
Async XLA Ops:
  7.0 8.5 %collective-permute-start.3 = (bf16[2,128,256]{2,1,0:T(8,128)(2,1)S(1)}, bf16[2,128,256]{2,1,0:T(8,128)(2,1)S(1)}, u32[]{:S(2)}, u32[]{:S(2)}) collective-permute-start(bf16[2,128,256]{2,1,0:T(8,128)(2,1)S(1)} %pad_maximum_fusion.4), channel_id=1, source_target_pairs={{0,8},{1,9},{2,10},{3,11},{4,12},{5,13},{6,14},{7,15},{8,0},{9,1},... | collective-permute-start | bytes 393224 | tf_op jit(solution)/shard_map/ppermute | solution.py:40
  8.4 7.0 %collective-permute-start.2 = (bf16[2,128,256]{2,1,0:T(8,128)(2,1)S(1)}, bf16[2,128,256]{2,1,0:T(8,128)(2,1)S(1)}, u32[]{:S(2)}, u32[]{:S(2)}) collective-permute-start(bf16[2,128,256]{2,1,0:T(8,128)(2,1)S(1)} %pad_maximum_fusion.4), channel_id=1, source_target_pairs={{0,12},{1,13},{2,14},{3,15},{4,0},{5,1},{6,2},{7,3},{8,4},{9,5},{1... | collective-permute-start | bytes 393224 | tf_op jit(solution)/shard_map/ppermute | solution.py:40
  22.0 17.6 %collective-permute-start.22 = (bf16[512,128]{1,0:T(8,128)(2,1)S(1)}, bf16[512,128]{1,0:T(8,128)(2,1)S(1)}, u32[]{:S(2)}, u32[]{:S(2)}) collective-permute-start(bf16[512,128]{1,0:T(8,128)(2,1)S(1)} %get-tuple-element.48), channel_id=1, source_target_pairs={{0,112},{16,0},{32,16},{48,32},{64,48},{80,64},{96,80},{112,96},{1... | collective-permute-start | bytes 393224 | tf_op jit(solution)/shard_map/ppermute | solution.py:36
  27.9 16.0 %collective-permute-start.6 = (bf16[512,128]{1,0:T(8,128)(2,1)S(1)}, bf16[512,128]{1,0:T(8,128)(2,1)S(1)}, u32[]{:S(2)}, u32[]{:S(2)}) collective-permute-start(bf16[512,128]{1,0:T(8,128)(2,1)S(1)} %get-tuple-element.31), channel_id=1, source_target_pairs={{0,16},{16,32},{32,48},{48,64},{64,80},{80,96},{96,112},{112,0},{1... | collective-permute-start | bytes 393224 | tf_op jit(solution)/shard_map/ppermute | solution.py:36
  27.9 15.6 %collective-permute-start.11 = (bf16[512,128]{1,0:T(8,128)(2,1)S(1)}, bf16[512,128]{1,0:T(8,128)(2,1)S(1)}, u32[]{:S(2)}, u32[]{:S(2)}) collective-permute-start(bf16[512,128]{1,0:T(8,128)(2,1)S(1)} %get-tuple-element.36), channel_id=1, source_target_pairs={{0,112},{16,0},{32,16},{48,32},{64,48},{80,64},{96,80},{112,96},{1... | collective-permute-start | bytes 393224 | tf_op jit(solution)/shard_map/ppermute | solution.py:36
  31.2 9.0 %collective-permute-start.17 = (bf16[512,128]{1,0:T(8,128)(2,1)S(1)}, bf16[512,128]{1,0:T(8,128)(2,1)S(1)}, u32[]{:S(2)}, u32[]{:S(2)}) collective-permute-start(bf16[512,128]{1,0:T(8,128)(2,1)S(1)} %get-tuple-element.43), channel_id=1, source_target_pairs={{0,16},{16,32},{32,48},{48,64},{64,80},{80,96},{96,112},{112,0},{1... | collective-permute-start | bytes 393224 | tf_op jit(solution)/shard_map/ppermute | solution.py:36
  34.8 32.1 %collective-permute-start.5 = (bf16[3,512,128]{2,1,0:T(8,128)(2,1)S(1)}, bf16[3,512,128]{2,1,0:T(8,128)(2,1)S(1)}, u32[]{:S(2)}, u32[]{:S(2)}) collective-permute-start(bf16[3,512,128]{2,1,0:T(8,128)(2,1)S(1)} %get-tuple-element.27), channel_id=1, source_target_pairs={{0,128},{16,144},{32,160},{48,176},{64,192},{80,208},{96,224},{112... | collective-permute-start | bytes 1179656 | tf_op jit(solution)/shard_map/ppermute | solution.py:36
  39.6 37.3 %collective-permute-start.16 = (bf16[3,512,128]{2,1,0:T(8,128)(2,1)S(1)}, bf16[3,512,128]{2,1,0:T(8,128)(2,1)S(1)}, u32[]{:S(2)}, u32[]{:S(2)}) collective-permute-start(bf16[3,512,128]{2,1,0:T(8,128)(2,1)S(1)} %get-tuple-element.39), channel_id=1, source_target_pairs={{0,128},{16,144},{32,160},{48,176},{64,192},{80,208},{96,224},{112... | collective-permute-start | bytes 1179656 | tf_op jit(solution)/shard_map/ppermute | solution.py:36
  40.1 13.5 %collective-permute-start.23 = (bf16[2,512,128]{2,1,0:T(8,128)(2,1)S(1)}, bf16[2,512,128]{2,1,0:T(8,128)(2,1)S(1)}, u32[]{:S(2)}, u32[]{:S(2)}) collective-permute-start(bf16[2,512,128]{2,1,0:T(8,128)(2,1)S(1)} %pad_maximum_fusion.3), channel_id=1, source_target_pairs={{0,112},{16,0},{32,16},{48,32},{64,48},{80,64},{96,80},{112,96},{1... | collective-permute-start | bytes 786440 | tf_op jit(solution)/shard_map/ppermute | solution.py:36
  43.5 23.3 %collective-permute-start.18 = (bf16[2,512,128]{2,1,0:T(8,128)(2,1)S(1)}, bf16[2,512,128]{2,1,0:T(8,128)(2,1)S(1)}, u32[]{:S(2)}, u32[]{:S(2)}) collective-permute-start(bf16[2,512,128]{2,1,0:T(8,128)(2,1)S(1)} %pad_maximum_fusion.2), channel_id=1, source_target_pairs={{0,16},{16,32},{32,48},{48,64},{64,80},{80,96},{96,112},{112,0},{1... | collective-permute-start | bytes 786440 | tf_op jit(solution)/shard_map/ppermute | solution.py:36
  43.9 9.7 %collective-permute-start.12 = (bf16[2,512,128]{2,1,0:T(8,128)(2,1)S(1)}, bf16[2,512,128]{2,1,0:T(8,128)(2,1)S(1)}, u32[]{:S(2)}, u32[]{:S(2)}) collective-permute-start(bf16[2,512,128]{2,1,0:T(8,128)(2,1)S(1)} %pad_maximum_fusion.1), channel_id=1, source_target_pairs={{0,112},{16,0},{32,16},{48,32},{64,48},{80,64},{96,80},{112,96},{1... | collective-permute-start | bytes 786440 | tf_op jit(solution)/shard_map/ppermute | solution.py:36
  53.6 8.1 %collective-permute-start.7 = (bf16[2,512,128]{2,1,0:T(8,128)(2,1)S(1)}, bf16[2,512,128]{2,1,0:T(8,128)(2,1)S(1)}, u32[]{:S(2)}, u32[]{:S(2)}) collective-permute-start(bf16[2,512,128]{2,1,0:T(8,128)(2,1)S(1)} %pad_maximum_fusion), channel_id=1, source_target_pairs={{0,16},{16,32},{32,48},{48,64},{64,80},{80,96},{96,112},{112,0},{1... | collective-permute-start | bytes 786440 | tf_op jit(solution)/shard_map/ppermute | solution.py:36
  53.7 13.4 %collective-permute-start.13 = (bf16[512,128]{1,0:T(8,128)(2,1)S(1)}, bf16[512,128]{1,0:T(8,128)(2,1)S(1)}, u32[]{:S(2)}, u32[]{:S(2)}) collective-permute-start(bf16[512,128]{1,0:T(8,128)(2,1)S(1)} %get-tuple-element.56), channel_id=1, source_target_pairs={{0,112},{16,0},{32,16},{48,32},{64,48},{80,64},{96,80},{112,96},{1... | collective-permute-start | bytes 393224 | tf_op jit(solution)/shard_map/ppermute | solution.py:36
  61.7 8.7 %collective-permute-start.14 = (bf16[512,128]{1,0:T(8,128)(2,1)S(1)}, bf16[512,128]{1,0:T(8,128)(2,1)S(1)}, u32[]{:S(2)}, u32[]{:S(2)}) collective-permute-start(bf16[512,128]{1,0:T(8,128)(2,1)S(1)} %get-tuple-element.57), channel_id=1, source_target_pairs={{0,240},{16,128},{32,144},{48,160},{64,176},{80,192},{96,208},{112... | collective-permute-start | bytes 393224 | tf_op jit(solution)/shard_map/ppermute | solution.py:36
  66.8 8.5 %collective-permute-start.8 = (bf16[512,128]{1,0:T(8,128)(2,1)S(1)}, bf16[512,128]{1,0:T(8,128)(2,1)S(1)}, u32[]{:S(2)}, u32[]{:S(2)}) collective-permute-start(bf16[512,128]{1,0:T(8,128)(2,1)S(1)} %get-tuple-element.54), channel_id=1, source_target_pairs={{0,16},{16,32},{32,48},{48,64},{64,80},{80,96},{96,112},{112,0},{1... | collective-permute-start | bytes 393224 | tf_op jit(solution)/shard_map/ppermute | solution.py:36
  66.9 9.9 %collective-permute-start.9 = (bf16[512,128]{1,0:T(8,128)(2,1)S(1)}, bf16[512,128]{1,0:T(8,128)(2,1)S(1)}, u32[]{:S(2)}, u32[]{:S(2)}) collective-permute-start(bf16[512,128]{1,0:T(8,128)(2,1)S(1)} %get-tuple-element.55), channel_id=1, source_target_pairs={{0,144},{16,160},{32,176},{48,192},{64,208},{80,224},{96,240},{112... | collective-permute-start | bytes 393224 | tf_op jit(solution)/shard_map/ppermute | solution.py:36
  67.1 9.9 %collective-permute-start.24 = (bf16[512,128]{1,0:T(8,128)(2,1)S(1)}, bf16[512,128]{1,0:T(8,128)(2,1)S(1)}, u32[]{:S(2)}, u32[]{:S(2)}) collective-permute-start(bf16[512,128]{1,0:T(8,128)(2,1)S(1)} %get-tuple-element.60), channel_id=1, source_target_pairs={{0,112},{16,0},{32,16},{48,32},{64,48},{80,64},{96,80},{112,96},{1... | collective-permute-start | bytes 393224 | tf_op jit(solution)/shard_map/ppermute | solution.py:36
  70.4 10.5 %collective-permute-start.25 = (bf16[512,128]{1,0:T(8,128)(2,1)S(1)}, bf16[512,128]{1,0:T(8,128)(2,1)S(1)}, u32[]{:S(2)}, u32[]{:S(2)}) collective-permute-start(bf16[512,128]{1,0:T(8,128)(2,1)S(1)} %get-tuple-element.61), channel_id=1, source_target_pairs={{0,240},{16,128},{32,144},{48,160},{64,176},{80,192},{96,208},{112... | collective-permute-start | bytes 393224 | tf_op jit(solution)/shard_map/ppermute | solution.py:36
  75.3 6.2 %collective-permute-start.19 = (bf16[512,128]{1,0:T(8,128)(2,1)S(1)}, bf16[512,128]{1,0:T(8,128)(2,1)S(1)}, u32[]{:S(2)}, u32[]{:S(2)}) collective-permute-start(bf16[512,128]{1,0:T(8,128)(2,1)S(1)} %get-tuple-element.58), channel_id=1, source_target_pairs={{0,16},{16,32},{32,48},{48,64},{64,80},{80,96},{96,112},{112,0},{1... | collective-permute-start | bytes 393224 | tf_op jit(solution)/shard_map/ppermute | solution.py:36
  76.8 8.6 %collective-permute-start.20 = (bf16[512,128]{1,0:T(8,128)(2,1)S(1)}, bf16[512,128]{1,0:T(8,128)(2,1)S(1)}, u32[]{:S(2)}, u32[]{:S(2)}) collective-permute-start(bf16[512,128]{1,0:T(8,128)(2,1)S(1)} %get-tuple-element.59), channel_id=1, source_target_pairs={{0,144},{16,160},{32,176},{48,192},{64,208},{80,224},{96,240},{112... | collective-permute-start | bytes 393224 | tf_op jit(solution)/shard_map/ppermute | solution.py:36
  77.0 11.9 %collective-permute-start.10 = (bf16[512,128]{1,0:T(8,128)(2,1)S(1)}, bf16[512,128]{1,0:T(8,128)(2,1)S(1)}, u32[]{:S(2)}, u32[]{:S(2)}) collective-permute-start(bf16[512,128]{1,0:T(8,128)(2,1)S(1)} %get-tuple-element.50), channel_id=1, source_target_pairs={{0,16},{16,32},{32,48},{48,64},{64,80},{80,96},{96,112},{112,0},{1... | collective-permute-start | bytes 393224 | tf_op jit(solution)/shard_map/ppermute | solution.py:36
  77.1 11.8 %collective-permute-start.15 = (bf16[512,128]{1,0:T(8,128)(2,1)S(1)}, bf16[512,128]{1,0:T(8,128)(2,1)S(1)}, u32[]{:S(2)}, u32[]{:S(2)}) collective-permute-start(bf16[512,128]{1,0:T(8,128)(2,1)S(1)} %get-tuple-element.51), channel_id=1, source_target_pairs={{0,112},{16,0},{32,16},{48,32},{64,48},{80,64},{96,80},{112,96},{1... | collective-permute-start | bytes 393224 | tf_op jit(solution)/shard_map/ppermute | solution.py:36
  85.5 6.3 %collective-permute-start.21 = (bf16[512,128]{1,0:T(8,128)(2,1)S(1)}, bf16[512,128]{1,0:T(8,128)(2,1)S(1)}, u32[]{:S(2)}, u32[]{:S(2)}) collective-permute-start(bf16[512,128]{1,0:T(8,128)(2,1)S(1)} %get-tuple-element.52), channel_id=1, source_target_pairs={{0,16},{16,32},{32,48},{48,64},{64,80},{80,96},{96,112},{112,0},{1... | collective-permute-start | bytes 393224 | tf_op jit(solution)/shard_map/ppermute | solution.py:36
  85.6 6.2 %collective-permute-start.26 = (bf16[512,128]{1,0:T(8,128)(2,1)S(1)}, bf16[512,128]{1,0:T(8,128)(2,1)S(1)}, u32[]{:S(2)}, u32[]{:S(2)}) collective-permute-start(bf16[512,128]{1,0:T(8,128)(2,1)S(1)} %get-tuple-element.53), channel_id=1, source_target_pairs={{0,112},{16,0},{32,16},{48,32},{64,48},{80,64},{96,80},{112,96},{1... | collective-permute-start | bytes 393224 | tf_op jit(solution)/shard_map/ppermute | solution.py:36
  (7 other events, 83.2 us)

commit v2 on v0

v2 whole, which is shorter than its diff:
```python
import jax
import jax.numpy as jnp
from jax import lax
from jax.experimental import pallas as pl
from jax.experimental.pallas import tpu as pltpu
from jax.sharding import PartitionSpec as P

TILE = 128
TILES_DEV = 8
ROWS_DEV = TILES_DEV * TILE
PW = 256
BF16 = jnp.bfloat16
F32 = jnp.float32
AXES = ("leaf", "panel")
VMEM_LIMIT = 16 * 1024 * 1024


def place(value, move):
    pairs = []
    for y in range(2):
        for z in range(8):
            for x in range(4):
                for low in range(2):
                    for core in range(2):
                        ny, nz, nx, nlow, ncore = move(y, z, x, low, core)
                        target = ny * 8 + nz % 8, (nx % 4) * 4 + nlow * 2 + ncore
                        pairs.append(((y * 8 + z) * 16 + x * 4 + low * 2 + core, target[0] * 16 + target[1]))
    return lax.ppermute(value, AXES, pairs)


def to_sibling(value):
    return place(value, lambda y, z, x, low, core: (y, z, x, low, 1 - core))


def across_y(value):
    return place(value, lambda y, z, x, low, core: (1 - y, z, x, low, core))


def along(value):
    return place(value, lambda y, z, x, low, core: (y, z + 1 - 2 * core, x, low, core))


def along_crossing(value):
    return place(value, lambda y, z, x, low, core: (y, z + 1 - 2 * core, x, low, 1 - core))


def along_first(value):
    return place(value, lambda y, z, x, low, core: (y ^ core, z + 1 - 2 * core, x, low, core))


def along_second(value):
    return place(value, lambda y, z, x, low, core: (1 - (y ^ core), z + 1 - 2 * core, x, low, core))


def position():
    return lax.axis_index("leaf"), lax.axis_index("panel")


def destination(step, kind):
    leaf, panel = position()
    core = panel % 2
    other = {0: 0, 1: 1, 2: core, 3: 1 - core}[kind]
    z = leaf + step * (1 - 2 * core) + 8
    return ((leaf // 8) ^ other) * 8 + z % 8


def window_slot(step, kind):
    tile = destination(step, kind)
    panel = position()[1]
    ahead = (tile // 4 - panel // 4 + 4) % 4
    slot = jnp.where(ahead == 0, 0, jnp.where(ahead == 2, 1, jnp.where(ahead == 1, 2, 3)))
    return slot * 2 + ((tile // 2) % 2 ^ (panel // 2) % 2)


def contributions(items, out_shapes, maps, factors, trailings, window, inverse, after=None):
    tiles = []
    for _, step, kind, _, _ in items:
        if (step, kind) not in tiles:
            tiles.append((step, kind))
    panels = []
    for panel, *_ in items:
        if panel not in panels:
            panels.append(panel)
    groups = []
    for panel in panels:
        work = [item for item in items if item[0] == panel]
        groups += [(panel, work[first : first + 2]) for first in range(0, len(work), 2)]
    count = len(panels)

    def body(*refs):
        maps_ref = dict(zip(panels, refs[:count]))
        factor = dict(zip(panels, refs[count : 2 * count]))
        trailing = dict(zip(panels, refs[2 * count : 3 * count]))
        own, far, inverse_ref = refs[3 * count : 3 * count + 3]
        outs = refs[len(refs) - len(out_shapes) :]
        core = position()[1] % 2
        weights = {}
        for tile in tiles:
            mine = (destination(*tile) % 2) == core
            slot = window_slot(*tile)
            rows = jnp.where(mine, own[slot], far[slot])
            weights[tile] = lax.dot_general(
                rows, inverse_ref[...], (((1,), (1,)), ((), ())), preferred_element_type=F32
            ).astype(BF16)
        for panel, group in groups:
            weight = jnp.concatenate([weights[item[1:3]] for item in group], axis=0)
            for pair in range(TILES_DEV // 2):
                update = lax.dot_general(
                    factor[panel][pair * 2 * TILE : (pair + 1) * 2 * TILE, :], weight,
                    (((1,), (1,)), ((), ())), preferred_element_type=F32,
                )
                for t in (2 * pair, 2 * pair + 1):
                    rows = slice(t * TILE, (t + 1) * TILE)
                    inner = (t % 2) * TILE
                    target = pl.ds(pl.multiple_of(maps_ref[panel][0, t] * TILE, TILE), TILE)
                    for m, (_, step, kind, out, lead) in enumerate(group):
                        tile = destination(step, kind)
                        part = update[inner : inner + TILE, m * TILE : (m + 1) * TILE]
                        part = jnp.where(tile < maps_ref[panel][0, TILES_DEV + t], part, 0.0)
                        column = pl.ds(pl.multiple_of(tile * TILE, TILE), TILE)
                        value = (trailing[panel][rows, column].astype(F32) - part).astype(BF16)
                        outs[out][(*lead, target, slice(None))] = value

    here = pl.BlockSpec(memory_space=pltpu.VMEM)
    extra = [] if after is None else [after]
    return pl.pallas_call(
        body,
        out_shape=[jax.ShapeDtypeStruct(shape, BF16) for shape in out_shapes],
        in_specs=[pl.BlockSpec(memory_space=pltpu.SMEM)] * count + [here] * (2 * count + 3 + len(extra)),
        out_specs=[here] * len(out_shapes),
        compiler_params=pltpu.CompilerParams(vmem_limit_bytes=VMEM_LIMIT),
        cost_estimate=pl.CostEstimate(
            flops=2 * ROWS_DEV * PW * TILE * len(items),
            bytes_accessed=(count * PW + 2 * len(items) * TILE) * ROWS_DEV * 2,
            transcendentals=0,
        ),
    )(
        *[maps[panel] for panel in panels],
        *[factors[panel] for panel in panels],
        *[trailings[panel] for panel in panels],
        *window,
        inverse,
        *extra,
    )


def solve_kernel(a21, inverse, emap, tasks, out, kept):
    out[:ROWS_DEV, :] = lax.dot_general(
        a21[...], inverse[...], (((1,), (1,)), ((), ())), preferred_element_type=F32
    ).astype(BF16)
    kept[...] = inverse[...]
    row = lax.broadcasted_iota(jnp.int32, (2 * TILES_DEV, PW), 0)
    rows = jnp.zeros((2 * TILES_DEV, PW), F32)
    for t in range(TILES_DEV):
        rows = jnp.where(row == t, emap[0, t].astype(F32), rows)
        rows = jnp.where(row == TILES_DEV + t, tasks[0, t].astype(F32), rows)
    out[ROWS_DEV:, :] = rows.astype(BF16)


def solve(a21, inverse, emap, tasks):
    here = pl.BlockSpec(memory_space=pltpu.VMEM)
    scalars = pl.BlockSpec(memory_space=pltpu.SMEM)
    rows = (ROWS_DEV + 2 * TILES_DEV, PW)
    return pl.pallas_call(
        solve_kernel,
        out_shape=[jax.ShapeDtypeStruct(rows, BF16), jax.ShapeDtypeStruct(inverse.shape, BF16)],
        in_specs=[here] * 2 + [scalars] * 2,
        out_specs=[here] * 2,
        compiler_params=pltpu.CompilerParams(vmem_limit_bytes=VMEM_LIMIT),
        cost_estimate=pl.CostEstimate(
            flops=2 * ROWS_DEV * PW * PW, bytes_accessed=4 * ROWS_DEV * PW, transcendentals=0
        ),
    )(a21, inverse, emap, tasks)


def bring_kernel(trailing, pair, out):
    out[...] = trailing[:TILE, :TILE] + pair[0, :, :TILE]


def bring(trailing, pair):
    here = pl.BlockSpec(memory_space=pltpu.VMEM)
    return pl.pallas_call(
        bring_kernel,
        out_shape=jax.ShapeDtypeStruct((TILE, TILE), BF16),
        in_specs=[here] * 2,
        out_specs=here,
        compiler_params=pltpu.CompilerParams(vmem_limit_bytes=VMEM_LIMIT),
    )(trailing, pair)


def add(*terms):
    total = terms[0].astype(F32)
    for term in terms[1:]:
        total = total + term.astype(F32)
    return total


def on_device(a21, l11_inv, a22, tasks, emap, parent_in):
    a21, l11_inv, a22 = a21[0], l11_inv[0], a22[0]
    a22_other = to_sibling(a22)
    lead = a21[:TILE]
    pair = jnp.stack([lead, place(lead, lambda y, z, x, low, core: (y, z, x, 1 - low, core))])
    factor, inverse = solve(a21, l11_inv, emap, tasks)
    pair, factor, inverse = lax.optimization_barrier((pair, factor, inverse))
    factor_other = to_sibling(factor)
    own = jnp.concatenate(
        [pair]
        + [
            place(pair, lambda y, z, x, low, core, dx=dx: (y, z, x + dx, low, core))
            for dx in (2, -1, 1)
        ]
    )
    brought = bring(a22, pair)
    maps_other = factor_other[ROWS_DEV:, 0].astype(jnp.int32)[None]
    own, a22_other, factor_other, maps_other, brought = lax.optimization_barrier(
        (own, a22_other, factor_other, maps_other, brought)
    )
    window = (own, to_sibling(own))
    maps = (jnp.concatenate([emap, tasks], axis=1), maps_other)
    factors, trailings = (factor, factor_other), (a22, a22_other)

    def run(items, shapes, after=None):
        return contributions(items, shapes, maps, factors, trailings, window, inverse, after)

    one, two, three = (ROWS_DEV, TILE), (2, ROWS_DEV, TILE), (3, ROWS_DEV, TILE)
    (far,) = run([(0, 4, 2, 0, (0,)), (1, 4, 2, 0, (1,))], [two], brought)
    first = along(far)
    sib1, own1, own0, near = run(
        [
            (0, 1, 1, 3, (1,)), (0, 0, 1, 3, (2,)), (0, 1, 0, 1, ()), (0, 0, 0, 2, ()),
            (1, 1, 1, 3, (0,)), (1, 1, 0, 0, ()),
        ],
        [one, one, one, three],
        far,
    )
    beside = across_y(near)
    third = run(
        [(1, 3, 2, 0, (0,)), (1, 3, 3, 0, (1,)), (0, 3, 2, 1, (0,)), (0, 3, 3, 1, (1,))],
        [two, two],
        near,
    )
    second = run(
        [(1, 2, 2, 0, ()), (1, 2, 3, 1, ()), (0, 2, 2, 2, ()), (0, 2, 3, 3, ())],
        [one] * 4,
        third[0],
    )
    moving = []
    for g in range(2):
        moving.append(along(jnp.stack([add(third[g][0], first[1 - g]).astype(BF16), third[g][1]])))
    for g in range(2):
        if g == 0:
            moving[g], beside = lax.optimization_barrier((moving[g], beside))
        moving[g] = (
            along_first(add(second[2 * g], moving[g][0]).astype(BF16)),
            along_second(add(second[2 * g + 1], moving[g][1]).astype(BF16)),
        )
    for g, base in enumerate((sib1, own1)):
        total = add(base, beside[g], *moving[g]).astype(BF16)
        moving[g] = along(total) if g else along_crossing(total)
    arrivals = add(own0, beside[2], *moving)
    return (factor[None, :ROWS_DEV], parent_in + arrivals)


def solution(mesh):
    return jax.shard_map(
        on_device,
        mesh=mesh,
        in_specs=(
            P("leaf", "panel", None),
            P("leaf", None, None),
            P("leaf", "panel", None),
            P("leaf", "panel"),
            P("leaf", "panel"),
            P("panel", "leaf"),
        ),
        out_specs=(P("leaf", "panel", None), P("panel", "leaf")),
        check_vma=False,
    )
```

time: 284 us -> 76.2 us (0.27)
  the two profiles are of different devices: /device:TPU:6 before, /device:TPU:1 now
where the time goes in v2:
time: 76.2 us; the launch traced here: 76 us
  starting transfers between devices  36.2 us (48%)
  waiting for transfers between devices  23.6 us (31%)
  local copies, waits for them, and re-layouts  7.17 us (9%)
  Pallas kernels  6.11 us (8%)
  other arithmetic  2 us (3%)
  between operations  0.81 us (1%)
    ppermute x17, starting transfers between devices, place(): return lax.ppermute(value, AXES, pairs)  36.2 us
    ppermute x17, waiting for transfers between devices, place(): return lax.ppermute(value, AXES, pairs)  23.6 us
    unnamed x18, local copies, waits for them, and re-layouts  5.46 us
    pallas_call x4, Pallas kernels, contributions(): pl.pallas_call(body, out_shape=[jax.ShapeDtypeStruct(shape, BF16) for sha...  5.23 us
  transfers between devices with their start and end apart: 17, of which 11 were waited for; matrix products, arithmetic and copies ran while one was open for 3% of the time, Pallas kernels for 6%

profile of v2, /device:TPU:1, one launch (start us, length us, event | category | flops | bytes accessed | tf_op | source)
XLA Modules:
  0.0 76.0 jit_solution(10611841808087424759)
XLA Ops:
  0.7 3.3 %collective-permute-start.4 = (bf16[1024,2048]{1,0:T(8,128)(2,1)}, bf16[1024,2048]{1,0:T(8,128)(2,1)S(1)}, u32[]{:S(2)}, u32[]{:S(2)}) collective-permute-start(bf16[1024,2048]{1,0:T(8,128)(2,1)} %bitcast.34), channel_id=1, source_target_pairs={{0,1},{1,0},{2,3},{3,2},{4,5},{5,4},{6,7},{7,6},{8,9},{9,8},{10,11... | collective-permute-start | bytes 12582920 | tf_op jit(solution)/shard_map/ppermute | solution.py:28
  4.9 1.0 %copy-done.2 = bf16[1,1024,256]{2,1,0:T(8,128)(2,1)S(1)} copy-done((bf16[1,1024,256]{2,1,0:T(8,128)(2,1)S(1)}, bf16[1,1024,256]{2,1,0:T(8,128)(2,1)}, u32[]{:S(2)}) %copy-start.2) | copy-done | bytes 524312
  6.0 0.9 %copy-done.3 = bf16[1,256,256]{2,1,0:T(8,128)(2,1)S(1)} copy-done((bf16[1,256,256]{2,1,0:T(8,128)(2,1)S(1)}, bf16[1,256,256]{2,1,0:T(8,128)(2,1)}, u32[]{:S(2)}) %copy-start.3) | copy-done | bytes 131096
  9.5 2.2 %collective-permute-start.1 = (bf16[2,128,256]{2,1,0:T(8,128)(2,1)S(1)}, bf16[2,128,256]{2,1,0:T(8,128)(2,1)S(1)}, u32[]{:S(2)}, u32[]{:S(2)}) collective-permute-start(bf16[2,128,256]{2,1,0:T(8,128)(2,1)S(1)} %pad_maximum_fusion.3.pair), channel_id=1, source_target_pairs={{0,8},{1,9},{2,10},{3,11},{4,12},{5,13},{6,14},{7,15},{8,0},{9,1},... | collective-permute-start | bytes 393224 | tf_op jit(solution)/shard_map/ppermute | solution.py:28
  13.2 2.2 %copy-done = bf16[1,1024,2048]{2,1,0:T(8,128)(2,1)S(1)} copy-done((bf16[1,1024,2048]{2,1,0:T(8,128)(2,1)S(1)}, bf16[1,1024,2048]{2,1,0:T(8,128)(2,1)}, u32[]{:S(2)}) %copy-start) | copy-done | bytes 4194328
  16.0 2.3 %collective-permute-done.2 = bf16[2,128,256]{2,1,0:T(8,128)(2,1)S(1)} collective-permute-done((bf16[2,128,256]{2,1,0:T(8,128)(2,1)S(1)}, bf16[2,128,256]{2,1,0:T(8,128)(2,1)S(1)}, u32[]{:S(2)}, u32[]{:S(2)}) %collective-permute-start.2) | collective-permute-done | bytes 131104 | tf_op jit(solution)/shard_map/ppermute | solution.py:28
  18.9 1.5 %collective-permute-start.6 = (bf16[8,128,256]{2,1,0:T(8,128)(2,1)S(1)}, bf16[8,128,256]{2,1,0:T(8,128)(2,1)S(1)}, u32[]{:S(2)}, u32[]{:S(2)}) collective-permute-start(bf16[8,128,256]{2,1,0:T(8,128)(2,1)S(1)} %pad_maximum_fusion.refs_6_), channel_id=1, source_target_pairs={{0,1},{1,0},{2,3},{3,2},{4,5},{5,4},{6,7},{7,6},{8,9},{9,8},{10,11... | collective-permute-start | bytes 1572872 | tf_op jit(solution)/shard_map/ppermute | solution.py:28
  20.4 1.5 %collective-permute-done.6.refs_7_ = bf16[8,128,256]{2,1,0:T(8,128)(2,1)S(1)} collective-permute-done((bf16[8,128,256]{2,1,0:T(8,128)(2,1)S(1)}, bf16[8,128,256]{2,1,0:T(8,128)(2,1)S(1)}, u32[]{:S(2)}, u32[]{:S(2)}) %collective-permute-start.6) | collective-permute-done | bytes 524320 | tf_op jit(solution)/shard_map/ppermute | solution.py:28
  21.9 1.2 %shard_map.79.refs_9_ = bf16[2,1024,128]{2,1,0:T(8,128)(2,1)S(1)} custom-call(s32[1,16]{1,0:T(1,128)S(1)} %pad_add_fusion.refs_0_.refs_1_, s32[1,16]{1,0:T(1,128)S(1)} %bitcast.42, bf16[1040,256]{1,0:T(8,128)(2,1)S(1)} %get-tuple-element.26.refs_2_.refs_3_, bf16[1040,256]{1,0:T(8,128)(2,1)S(1)} %collective-permute-done.5.refs_3_.refs_2_, ...), custom_call_target="tpu_custom_call" | custom-call | flops 134217728 | bytes 2097152 | tf_op jit(solution)/shard_map/pallas_call | solution.py:126
  23.1 5.4 %collective-permute-start.7 = (bf16[2,1024,128]{2,1,0:T(8,128)(2,1)S(1)}, bf16[2,1024,128]{2,1,0:T(8,128)(2,1)S(1)}, u32[]{:S(2)}, u32[]{:S(2)}) collective-permute-start(bf16[2,1024,128]{2,1,0:T(8,128)(2,1)S(1)} %shard_map.79.refs_9_), channel_id=1, source_target_pairs={{0,16},{1,113},{2,18},{3,115},{4,20},{5,117},{6,22},{7,119},{8,24}... | collective-permute-start | bytes 1572872 | tf_op jit(solution)/shard_map/ppermute | solution.py:28
  28.5 1.5 %shard_map.80 = (bf16[1024,128]{1,0:T(8,128)(2,1)S(1)}, bf16[1024,128]{1,0:T(8,128)(2,1)S(1)}, bf16[1024,128]{1,0:T(8,128)(2,1)S(1)}, bf16[3,1024,128]{2,1,0:T(8,128)(2,1)S(1)}) custom-call(s32[1,16]{1,0:T(1,128)S(1)} %pad_add_fusion.refs_0_.refs_1_, s32[1,16]{1,0:T(1,128)S(1)} %bitcast.43, bf16[1040,256]{1,0:T(8,128)(2,1)S(1)} %get-tuple-element.26.refs_2_.refs_3_, ...), custom_call_target="tpu_custom_call" | custom-call | flops 402653184 | bytes 4194304 | tf_op jit(solution)/shard_map/pallas_call | solution.py:126
  30.0 2.7 %collective-permute-start.9 = (bf16[3,1024,128]{2,1,0:T(8,128)(2,1)S(1)}, bf16[3,1024,128]{2,1,0:T(8,128)(2,1)S(1)}, u32[]{:S(2)}, u32[]{:S(2)}) collective-permute-start(bf16[3,1024,128]{2,1,0:T(8,128)(2,1)S(1)} %get-tuple-element.35.refs_9_), channel_id=1, source_target_pairs={{0,128},{1,129},{2,130},{3,131},{4,132},{5,133},{6,134},{7,135},{8... | collective-permute-start | bytes 2359304 | tf_op jit(solution)/shard_map/ppermute | solution.py:28
  32.7 1.3 %shard_map.81 = (bf16[2,1024,128]{2,1,0:T(8,128)(2,1)S(1)}, bf16[2,1024,128]{2,1,0:T(8,128)(2,1)S(1)}) custom-call(s32[1,16]{1,0:T(1,128)S(1)} %bitcast.44, s32[1,16]{1,0:T(1,128)S(1)} %pad_add_fusion.refs_0_.refs_1_, bf16[1040,256]{1,0:T(8,128)(2,1)S(1)} %collective-permute-done.5.refs_3_.refs_2_, bf16[1040,256]{1,0:T(8,128)(2,1)S(1)} %get-tuple-element.26.refs_2_.refs_3_, ...), custom_call_target="tpu_custom_call" | custom-call | flops 268435456 | bytes 3145728 | tf_op jit(solution)/shard_map/pallas_call | solution.py:126
  34.8 3.5 %collective-permute-start.13 = (bf16[2,1024,128]{2,1,0:T(8,128)(2,1)S(1)}, bf16[2,1024,128]{2,1,0:T(8,128)(2,1)S(1)}, u32[]{:S(2)}, u32[]{:S(2)}) collective-permute-start(bf16[2,1024,128]{2,1,0:T(8,128)(2,1)S(1)} %pad_maximum_fusion.2), channel_id=1, source_target_pairs={{0,16},{1,113},{2,18},{3,115},{4,20},{5,117},{6,22},{7,119},{8,24}... | collective-permute-start | bytes 1572872 | tf_op jit(solution)/shard_map/ppermute | solution.py:28
  38.5 1.3 %shard_map.82 = (bf16[1024,128]{1,0:T(8,128)(2,1)S(1)}, bf16[1024,128]{1,0:T(8,128)(2,1)S(1)}, bf16[1024,128]{1,0:T(8,128)(2,1)S(1)}, bf16[1024,128]{1,0:T(8,128)(2,1)S(1)}) custom-call(s32[1,16]{1,0:T(1,128)S(1)} %bitcast.45, s32[1,16]{1,0:T(1,128)S(1)} %pad_add_fusion.refs_0_.refs_1_, bf16[1040,256]{1,0:T(8,128)(2,1)S(1)} %collective-permute-done.5.refs_3_.refs_2_, ...), custom_call_target="tpu_custom_call" | custom-call | flops 268435456 | bytes 3145728 | tf_op jit(solution)/shard_map/pallas_call | solution.py:126
  39.8 4.7 %collective-permute-done.13 = bf16[2,1024,128]{2,1,0:T(8,128)(2,1)S(1)} collective-permute-done((bf16[2,1024,128]{2,1,0:T(8,128)(2,1)S(1)}, bf16[2,1024,128]{2,1,0:T(8,128)(2,1)S(1)}, u32[]{:S(2)}, u32[]{:S(2)}) %collective-permute-start.13) | collective-permute-done | bytes 524320 | tf_op jit(solution)/shard_map/ppermute | solution.py:28
  44.6 5.5 %collective-permute-start.14 = (bf16[1024,128]{1,0:T(8,128)(2,1)S(1)}, bf16[1024,128]{1,0:T(8,128)(2,1)S(1)}, u32[]{:S(2)}, u32[]{:S(2)}) collective-permute-start(bf16[1024,128]{1,0:T(8,128)(2,1)S(1)} %get-tuple-element.52), channel_id=1, source_target_pairs={{0,16},{1,241},{2,18},{3,243},{4,20},{5,245},{6,22},{7,247},{8,24}... | collective-permute-start | bytes 786440 | tf_op jit(solution)/shard_map/ppermute | solution.py:28
  50.3 5.3 %collective-permute-start.10 = (bf16[1024,128]{1,0:T(8,128)(2,1)S(1)}, bf16[1024,128]{1,0:T(8,128)(2,1)S(1)}, u32[]{:S(2)}, u32[]{:S(2)}) collective-permute-start(bf16[1024,128]{1,0:T(8,128)(2,1)S(1)} %get-tuple-element.48), channel_id=1, source_target_pairs={{0,16},{1,241},{2,18},{3,243},{4,20},{5,245},{6,22},{7,247},{8,24}... | collective-permute-start | bytes 786440 | tf_op jit(solution)/shard_map/ppermute | solution.py:28
  56.2 5.9 %collective-permute-done.10 = bf16[1024,128]{1,0:T(8,128)(2,1)S(1)} collective-permute-done((bf16[1024,128]{1,0:T(8,128)(2,1)S(1)}, bf16[1024,128]{1,0:T(8,128)(2,1)S(1)}, u32[]{:S(2)}, u32[]{:S(2)}) %collective-permute-start.10) | collective-permute-done | bytes 262176 | tf_op jit(solution)/shard_map/ppermute | solution.py:28
  62.1 1.0 %collective-permute-done.11 = bf16[1024,128]{1,0:T(8,128)(2,1)S(1)} collective-permute-done((bf16[1024,128]{1,0:T(8,128)(2,1)S(1)}, bf16[1024,128]{1,0:T(8,128)(2,1)S(1)}, u32[]{:S(2)}, u32[]{:S(2)}) %collective-permute-start.11) | collective-permute-done | bytes 262176 | tf_op jit(solution)/shard_map/ppermute | solution.py:28
  63.4 4.2 %collective-permute-start.12 = (bf16[1024,128]{1,0:T(8,128)(2,1)S(1)}, bf16[1024,128]{1,0:T(8,128)(2,1)S(1)}, u32[]{:S(2)}, u32[]{:S(2)}) collective-permute-start(bf16[1024,128]{1,0:T(8,128)(2,1)S(1)} %get-tuple-element.46), channel_id=1, source_target_pairs={{0,17},{1,112},{2,19},{3,114},{4,21},{5,116},{6,23},{7,118},{8,25}... | collective-permute-start | bytes 786440 | tf_op jit(solution)/shard_map/ppermute | solution.py:28
  68.9 2.7 %collective-permute-done.12 = bf16[1024,128]{1,0:T(8,128)(2,1)S(1)} collective-permute-done((bf16[1024,128]{1,0:T(8,128)(2,1)S(1)}, bf16[1024,128]{1,0:T(8,128)(2,1)S(1)}, u32[]{:S(2)}, u32[]{:S(2)}) %collective-permute-start.12) | collective-permute-done | bytes 262176 | tf_op jit(solution)/shard_map/ppermute | solution.py:28
  71.6 3.4 %collective-permute-done.16 = bf16[1024,128]{1,0:T(8,128)(2,1)S(1)} collective-permute-done((bf16[1024,128]{1,0:T(8,128)(2,1)S(1)}, bf16[1024,128]{1,0:T(8,128)(2,1)S(1)}, u32[]{:S(2)}, u32[]{:S(2)}) %collective-permute-start.16) | collective-permute-done | bytes 262176 | tf_op jit(solution)/shard_map/ppermute | solution.py:28
  75.0 0.9 %fusion.12 = f32[1024,128]{1,0:T(8,128)} fusion(f32[1024,128]{1,0:T(8,128)S(1)} %copy-done.8, bf16[1024,128]{1,0:T(8,128)(2,1)S(1)} %collective-permute-done.16, bf16[1024,128]{1,0:T(8,128)(2,1)S(1)} %collective-permute-done.12, bf16[1024,128]{1,0:T(8,128)(2,1)S(1)} %get-tuple-element.34, bf16[3,1024,128]{2,1,0:T(8,128)(2,1)S(1)} %collective-permute-done.9), kind=kLoop, calls=%fused_computation.22 | loop fusion | flops 1048576 | bytes 2097152 | tf_op jit(solution)/shard_map/add | solution.py:261
  (49 shorter events, 9.8 us)
Async XLA Ops:
  0.6 19.7 %copy-start.5 = (s32[1,8]{1,0:T(1,128)S(1)}, s32[1,8]{1,0:T(1,128)}, u32[]{:S(2)}) copy-start(s32[1,8]{1,0:T(1,128)} %emap.1) | copy-start | bytes 100
  0.6 19.7 %copy-start.7 = (s32[1,8]{1,0:T(1,128)S(1)}, s32[1,8]{1,0:T(1,128)}, u32[]{:S(2)}) copy-start(s32[1,8]{1,0:T(1,128)} %tasks.1) | copy-start | bytes 100
  0.7 18.2 %collective-permute-start.4 = (bf16[1024,2048]{1,0:T(8,128)(2,1)}, bf16[1024,2048]{1,0:T(8,128)(2,1)S(1)}, u32[]{:S(2)}, u32[]{:S(2)}) collective-permute-start(bf16[1024,2048]{1,0:T(8,128)(2,1)} %bitcast.34), channel_id=1, source_target_pairs={{0,1},{1,0},{2,3},{3,2},{4,5},{5,4},{6,7},{7,6},{8,9},{9,8},{10,11... | collective-permute-start | bytes 12582920 | tf_op jit(solution)/shard_map/ppermute | solution.py:28
  4.8 4.2 %collective-permute-start = (bf16[128,256]{1,0:T(8,128)(2,1)S(1)}, bf16[128,256]{1,0:T(8,128)(2,1)S(1)}, u32[]{:S(2)}, u32[]{:S(2)}) collective-permute-start(bf16[128,256]{1,0:T(8,128)(2,1)S(1)} %get-tuple-element.55), channel_id=1, source_target_pairs={{0,2},{1,3},{2,0},{3,1},{4,6},{5,7},{6,4},{7,5},{8,10},{9,11},{10,... | collective-permute-start | bytes 196616 | tf_op jit(solution)/shard_map/ppermute | solution.py:28
  4.9 1.0 %copy-start.2 = (bf16[1,1024,256]{2,1,0:T(8,128)(2,1)S(1)}, bf16[1,1024,256]{2,1,0:T(8,128)(2,1)}, u32[]{:S(2)}) copy-start(bf16[1,1024,256]{2,1,0:T(8,128)(2,1)} %param.6) | copy-start | bytes 1572868
  6.0 0.9 %copy-start.3 = (bf16[1,256,256]{2,1,0:T(8,128)(2,1)S(1)}, bf16[1,256,256]{2,1,0:T(8,128)(2,1)}, u32[]{:S(2)}) copy-start(bf16[1,256,256]{2,1,0:T(8,128)(2,1)} %param.7) | copy-start | bytes 393220
  9.1 9.7 %collective-permute-start.5 = (bf16[1040,256]{1,0:T(8,128)(2,1)S(1)}, bf16[1040,256]{1,0:T(8,128)(2,1)S(1)}, u32[]{:S(2)}, u32[]{:S(2)}) collective-permute-start(bf16[1040,256]{1,0:T(8,128)(2,1)S(1)} %get-tuple-element.26.refs_2_.refs_3_), channel_id=1, source_target_pairs={{0,1},{1,0},{2,3},{3,2},{4,5},{5,4},{6,7},{7,6},{8,9},{9,8},{10,11... | collective-permute-start | bytes 1597448 | tf_op jit(solution)/shard_map/ppermute | solution.py:28
  9.5 6.5 %collective-permute-start.1 = (bf16[2,128,256]{2,1,0:T(8,128)(2,1)S(1)}, bf16[2,128,256]{2,1,0:T(8,128)(2,1)S(1)}, u32[]{:S(2)}, u32[]{:S(2)}) collective-permute-start(bf16[2,128,256]{2,1,0:T(8,128)(2,1)S(1)} %pad_maximum_fusion.3.pair), channel_id=1, source_target_pairs={{0,8},{1,9},{2,10},{3,11},{4,12},{5,13},{6,14},{7,15},{8,0},{9,1},... | collective-permute-start | bytes 393224 | tf_op jit(solution)/shard_map/ppermute | solution.py:28
  11.8 6.6 %collective-permute-start.2 = (bf16[2,128,256]{2,1,0:T(8,128)(2,1)S(1)}, bf16[2,128,256]{2,1,0:T(8,128)(2,1)S(1)}, u32[]{:S(2)}, u32[]{:S(2)}) collective-permute-start(bf16[2,128,256]{2,1,0:T(8,128)(2,1)S(1)} %pad_maximum_fusion.3.pair), channel_id=1, source_target_pairs={{0,12},{1,13},{2,14},{3,15},{4,0},{5,1},{6,2},{7,3},{8,4},{9,5},{1... | collective-permute-start | bytes 393224 | tf_op jit(solution)/shard_map/ppermute | solution.py:28
  12.6 6.0 %collective-permute-start.3 = (bf16[2,128,256]{2,1,0:T(8,128)(2,1)S(1)}, bf16[2,128,256]{2,1,0:T(8,128)(2,1)S(1)}, u32[]{:S(2)}, u32[]{:S(2)}) collective-permute-start(bf16[2,128,256]{2,1,0:T(8,128)(2,1)S(1)} %pad_maximum_fusion.3.pair), channel_id=1, source_target_pairs={{0,4},{1,5},{2,6},{3,7},{4,8},{5,9},{6,10},{7,11},{8,12},{9,13},{1... | collective-permute-start | bytes 393224 | tf_op jit(solution)/shard_map/ppermute | solution.py:28
  13.2 2.2 %copy-start = (bf16[1,1024,2048]{2,1,0:T(8,128)(2,1)S(1)}, bf16[1,1024,2048]{2,1,0:T(8,128)(2,1)}, u32[]{:S(2)}) copy-start(bf16[1,1024,2048]{2,1,0:T(8,128)(2,1)} %param.8) | copy-start | bytes 12582916
  15.4 6.4 %copy-start.1 = (bf16[1,1024,2048]{2,1,0:T(8,128)(2,1)S(1)}, bf16[1,1024,2048]{2,1,0:T(8,128)(2,1)}, u32[]{:S(2)}) copy-start(bf16[1,1024,2048]{2,1,0:T(8,128)(2,1)} %param.8) | copy-start | bytes 12582916
  18.9 3.0 %collective-permute-start.6 = (bf16[8,128,256]{2,1,0:T(8,128)(2,1)S(1)}, bf16[8,128,256]{2,1,0:T(8,128)(2,1)S(1)}, u32[]{:S(2)}, u32[]{:S(2)}) collective-permute-start(bf16[8,128,256]{2,1,0:T(8,128)(2,1)S(1)} %pad_maximum_fusion.refs_6_), channel_id=1, source_target_pairs={{0,1},{1,0},{2,3},{3,2},{4,5},{5,4},{6,7},{7,6},{8,9},{9,8},{10,11... | collective-permute-start | bytes 1572872 | tf_op jit(solution)/shard_map/ppermute | solution.py:28
  23.1 11.6 %collective-permute-start.7 = (bf16[2,1024,128]{2,1,0:T(8,128)(2,1)S(1)}, bf16[2,1024,128]{2,1,0:T(8,128)(2,1)S(1)}, u32[]{:S(2)}, u32[]{:S(2)}) collective-permute-start(bf16[2,1024,128]{2,1,0:T(8,128)(2,1)S(1)} %shard_map.79.refs_9_), channel_id=1, source_target_pairs={{0,16},{1,113},{2,18},{3,115},{4,20},{5,117},{6,22},{7,119},{8,24}... | collective-permute-start | bytes 1572872 | tf_op jit(solution)/shard_map/ppermute | solution.py:28
  30.0 20.1 %collective-permute-start.9 = (bf16[3,1024,128]{2,1,0:T(8,128)(2,1)S(1)}, bf16[3,1024,128]{2,1,0:T(8,128)(2,1)S(1)}, u32[]{:S(2)}, u32[]{:S(2)}) collective-permute-start(bf16[3,1024,128]{2,1,0:T(8,128)(2,1)S(1)} %get-tuple-element.35.refs_9_), channel_id=1, source_target_pairs={{0,128},{1,129},{2,130},{3,131},{4,132},{5,133},{6,134},{7,135},{8... | collective-permute-start | bytes 2359304 | tf_op jit(solution)/shard_map/ppermute | solution.py:28
  34.8 9.6 %collective-permute-start.13 = (bf16[2,1024,128]{2,1,0:T(8,128)(2,1)S(1)}, bf16[2,1024,128]{2,1,0:T(8,128)(2,1)S(1)}, u32[]{:S(2)}, u32[]{:S(2)}) collective-permute-start(bf16[2,1024,128]{2,1,0:T(8,128)(2,1)S(1)} %pad_maximum_fusion.2), channel_id=1, source_target_pairs={{0,16},{1,113},{2,18},{3,115},{4,20},{5,117},{6,22},{7,119},{8,24}... | collective-permute-start | bytes 1572872 | tf_op jit(solution)/shard_map/ppermute | solution.py:28
  38.4 11.7 %collective-permute-start.8 = (bf16[2,1024,128]{2,1,0:T(8,128)(2,1)S(1)}, bf16[2,1024,128]{2,1,0:T(8,128)(2,1)S(1)}, u32[]{:S(2)}, u32[]{:S(2)}) collective-permute-start(bf16[2,1024,128]{2,1,0:T(8,128)(2,1)S(1)} %pad_maximum_fusion.1), channel_id=1, source_target_pairs={{0,16},{1,113},{2,18},{3,115},{4,20},{5,117},{6,22},{7,119},{8,24}... | collective-permute-start | bytes 1572872 | tf_op jit(solution)/shard_map/ppermute | solution.py:28
  39.8 35.3 %copy-start.8 = (f32[1024,128]{1,0:T(8,128)S(1)}, f32[1024,128]{1,0:T(8,128)}, u32[]{:S(2)}) copy-start(f32[1024,128]{1,0:T(8,128)} %param.11) | copy-start | bytes 1572868
  44.6 11.0 %collective-permute-start.14 = (bf16[1024,128]{1,0:T(8,128)(2,1)S(1)}, bf16[1024,128]{1,0:T(8,128)(2,1)S(1)}, u32[]{:S(2)}, u32[]{:S(2)}) collective-permute-start(bf16[1024,128]{1,0:T(8,128)(2,1)S(1)} %get-tuple-element.52), channel_id=1, source_target_pairs={{0,16},{1,241},{2,18},{3,243},{4,20},{5,245},{6,22},{7,247},{8,24}... | collective-permute-start | bytes 786440 | tf_op jit(solution)/shard_map/ppermute | solution.py:28
  50.1 6.1 %collective-permute-start.15 = (bf16[1024,128]{1,0:T(8,128)(2,1)S(1)}, bf16[1024,128]{1,0:T(8,128)(2,1)S(1)}, u32[]{:S(2)}, u32[]{:S(2)}) collective-permute-start(bf16[1024,128]{1,0:T(8,128)(2,1)S(1)} %get-tuple-element.53), channel_id=1, source_target_pairs={{0,144},{1,113},{2,146},{3,115},{4,148},{5,117},{6,150},{7,119},{8... | collective-permute-start | bytes 786440 | tf_op jit(solution)/shard_map/ppermute | solution.py:28
  50.3 11.9 %collective-permute-start.10 = (bf16[1024,128]{1,0:T(8,128)(2,1)S(1)}, bf16[1024,128]{1,0:T(8,128)(2,1)S(1)}, u32[]{:S(2)}, u32[]{:S(2)}) collective-permute-start(bf16[1024,128]{1,0:T(8,128)(2,1)S(1)} %get-tuple-element.48), channel_id=1, source_target_pairs={{0,16},{1,241},{2,18},{3,243},{4,20},{5,245},{6,22},{7,247},{8,24}... | collective-permute-start | bytes 786440 | tf_op jit(solution)/shard_map/ppermute | solution.py:28
  55.6 7.5 %collective-permute-start.11 = (bf16[1024,128]{1,0:T(8,128)(2,1)S(1)}, bf16[1024,128]{1,0:T(8,128)(2,1)S(1)}, u32[]{:S(2)}, u32[]{:S(2)}) collective-permute-start(bf16[1024,128]{1,0:T(8,128)(2,1)S(1)} %get-tuple-element.49), channel_id=1, source_target_pairs={{0,144},{1,113},{2,146},{3,115},{4,148},{5,117},{6,150},{7,119},{8... | collective-permute-start | bytes 786440 | tf_op jit(solution)/shard_map/ppermute | solution.py:28
  63.4 8.2 %collective-permute-start.12 = (bf16[1024,128]{1,0:T(8,128)(2,1)S(1)}, bf16[1024,128]{1,0:T(8,128)(2,1)S(1)}, u32[]{:S(2)}, u32[]{:S(2)}) collective-permute-start(bf16[1024,128]{1,0:T(8,128)(2,1)S(1)} %get-tuple-element.46), channel_id=1, source_target_pairs={{0,17},{1,112},{2,19},{3,114},{4,21},{5,116},{6,23},{7,118},{8,25}... | collective-permute-start | bytes 786440 | tf_op jit(solution)/shard_map/ppermute | solution.py:28
  67.5 7.5 %collective-permute-start.16 = (bf16[1024,128]{1,0:T(8,128)(2,1)S(1)}, bf16[1024,128]{1,0:T(8,128)(2,1)S(1)}, u32[]{:S(2)}, u32[]{:S(2)}) collective-permute-start(bf16[1024,128]{1,0:T(8,128)(2,1)S(1)} %get-tuple-element.47), channel_id=1, source_target_pairs={{0,16},{1,113},{2,18},{3,115},{4,20},{5,117},{6,22},{7,119},{8,24}... | collective-permute-start | bytes 786440 | tf_op jit(solution)/shard_map/ppermute | solution.py:28
  (2 other events, 1.3 us)

commit v3 on v0

v3 whole, which is shorter than its diff:
```python
import jax
import jax.numpy as jnp
from jax import lax
from jax.experimental import pallas as pl
from jax.experimental.pallas import tpu as pltpu
from jax.sharding import PartitionSpec as P

TILE = 128
TILES_DEV = 8
ROWS_DEV = TILES_DEV * TILE
PW = 256
BF16 = jnp.bfloat16
F32 = jnp.float32
AXES = ("leaf", "panel")
VMEM_LIMIT = 16 * 1024 * 1024


def place(value, move):
    pairs = []
    for y in range(2):
        for z in range(8):
            for x in range(4):
                for low in range(2):
                    for core in range(2):
                        ny, nz, nx, nlow, ncore = move(y, z, x, low, core)
                        target = ny * 8 + nz % 8, (nx % 4) * 4 + nlow * 2 + ncore
                        pairs.append(((y * 8 + z) * 16 + x * 4 + low * 2 + core, target[0] * 16 + target[1]))
    return lax.ppermute(value, AXES, pairs)


def to_sibling(value):
    return place(value, lambda y, z, x, low, core: (y, z, x, low, 1 - core))


def across_y(value):
    return place(value, lambda y, z, x, low, core: (1 - y, z, x, low, core))


def along(value, way):
    return place(value, lambda y, z, x, low, core: (y, z + way, x, low, core))


def along_y(value, way):
    return place(value, lambda y, z, x, low, core: (1 - y, z + way, x, low, core))


def position():
    return lax.axis_index("leaf"), lax.axis_index("panel")


def destination(step, other):
    leaf = position()[0]
    return ((leaf // 8) ^ other) * 8 + (leaf + step + 8) % 8


def window_slot(step, other):
    tile = destination(step, other)
    panel = position()[1]
    ahead = (tile // 4 - panel // 4 + 4) % 4
    slot = jnp.where(ahead == 0, 0, jnp.where(ahead == 2, 1, jnp.where(ahead == 1, 2, 3)))
    return slot * 2 + ((tile // 2) % 2 ^ (panel // 2) % 2)


def contributions(items, out_shapes, prepared, window, after):
    def body(factor, trailing, limits, inverse, own, far, after, *outs):
        core = position()[1] % 2
        for first in range(0, len(items), 2):
            group = items[first : first + 2]
            tiles = [destination(step, other) for step, other, _, _ in group]
            columns = [pl.ds(pl.multiple_of(tile * TILE, TILE), TILE) for tile in tiles]
            weights = []
            for tile, (step, other, _, _) in zip(tiles, group):
                mine = (tile % 2) == core
                slot = window_slot(step, other)
                rows = jnp.where(mine, own[slot], far[slot])
                weights.append(
                    lax.dot_general(
                        rows, inverse[...], (((1,), (1,)), ((), ())), preferred_element_type=F32
                    ).astype(BF16)
                )
            weight = jnp.concatenate(weights, axis=0)
            for pair in range(TILES_DEV // 2):
                update = lax.dot_general(
                    factor[pair * 2 * TILE : (pair + 1) * 2 * TILE, :], weight,
                    (((1,), (1,)), ((), ())), preferred_element_type=F32,
                )
                for k in (2 * pair, 2 * pair + 1):
                    rows = slice(k * TILE, (k + 1) * TILE)
                    inner = (k % 2) * TILE
                    for m, (_, _, out, lead) in enumerate(group):
                        part = update[inner : inner + TILE, m * TILE : (m + 1) * TILE]
                        part = jnp.where(limits[k : k + 1, :] > tiles[m], part, 0.0)
                        value = (trailing[rows, columns[m]].astype(F32) - part).astype(BF16)
                        outs[out][(*lead, rows, slice(None))] = value

    here = pl.BlockSpec(memory_space=pltpu.VMEM)
    return pl.pallas_call(
        body,
        out_shape=[jax.ShapeDtypeStruct(shape, BF16) for shape in out_shapes],
        in_specs=[here] * 7,
        out_specs=[here] * len(out_shapes),
        compiler_params=pltpu.CompilerParams(vmem_limit_bytes=VMEM_LIMIT),
        cost_estimate=pl.CostEstimate(
            flops=2 * ROWS_DEV * PW * TILE * len(items),
            bytes_accessed=(PW + 2 * len(items) * TILE) * ROWS_DEV * 2,
            transcendentals=0,
        ),
    )(*prepared, *window, after)


def prepare_kernel(maps, a21, inverse, trailing, out, factor, ordered, limits, kept):
    out[...] = lax.dot_general(
        a21[...], inverse[...], (((1,), (1,)), ((), ())), preferred_element_type=F32
    ).astype(BF16)
    kept[...] = inverse[...]
    for t in range(TILES_DEV):
        rows = slice(t * TILE, (t + 1) * TILE)
        target = pl.ds(pl.multiple_of(maps[0, t] * TILE, TILE), TILE)
        factor[target, :] = out[rows, :]
        ordered[target, :] = trailing[rows, :]
        limits[pl.ds(maps[0, t], 1), :] = jnp.full((1, TILE), maps[0, TILES_DEV + t], jnp.int32)


def prepare(maps, a21, inverse, trailing):
    here = pl.BlockSpec(memory_space=pltpu.VMEM)
    like = [jax.ShapeDtypeStruct(value.shape, BF16) for value in (a21, a21, trailing)]
    return pl.pallas_call(
        prepare_kernel,
        out_shape=like
        + [
            jax.ShapeDtypeStruct((TILES_DEV, TILE), jnp.int32),
            jax.ShapeDtypeStruct(inverse.shape, BF16),
        ],
        in_specs=[pl.BlockSpec(memory_space=pltpu.SMEM)] + [here] * 3,
        out_specs=[here] * 5,
        compiler_params=pltpu.CompilerParams(vmem_limit_bytes=VMEM_LIMIT),
        cost_estimate=pl.CostEstimate(
            flops=2 * ROWS_DEV * PW * PW, bytes_accessed=8 * 1024 * 1024, transcendentals=0
        ),
    )(maps, a21, inverse, trailing)


def bring_kernel(trailing, lead, out):
    out[...] = trailing[:TILE, :TILE] + lead[:, :TILE]


def bring(trailing, lead):
    here = pl.BlockSpec(memory_space=pltpu.VMEM)
    return pl.pallas_call(
        bring_kernel,
        out_shape=jax.ShapeDtypeStruct((TILE, TILE), BF16),
        in_specs=[here] * 2,
        out_specs=here,
        compiler_params=pltpu.CompilerParams(vmem_limit_bytes=VMEM_LIMIT),
    )(trailing, lead)


def add(*terms):
    total = terms[0].astype(F32)
    for term in terms[1:]:
        total = total + term.astype(F32)
    return total


def on_device(a21, l11_inv, a22, tasks, emap, parent_in):
    a21, l11_inv, a22 = a21[0], l11_inv[0], a22[0]
    lead = a21[:TILE]
    pair = jnp.stack([lead, place(lead, lambda y, z, x, low, core: (y, z, x, 1 - low, core))])
    pair, brought, a21, l11_inv = lax.optimization_barrier((pair, bring(a22, lead), a21, l11_inv))
    own = jnp.concatenate(
        [pair]
        + [
            place(pair, lambda y, z, x, low, core, dx=dx: (y, z, x + dx, low, core))
            for dx in (2, -1, 1)
        ]
    )
    maps = jnp.concatenate([emap, tasks], axis=1)
    l21, *prepared = prepare(maps, a21, l11_inv, a22)
    own, prepared = lax.optimization_barrier((own, prepared))
    window = (own, to_sibling(own))

    def run(items, shapes, after):
        return contributions(items, shapes, prepared, window, after)

    one, two = (ROWS_DEV, TILE), (2, ROWS_DEV, TILE)
    def bf16(*terms):
        return add(*terms).astype(BF16)

    far, far_y = run([(4, 0, 0, ()), (4, 1, 1, ())], [one, one], brought)
    up4, down4_y = along(far, 1), along(far_y, -1)
    near1, up3_y, down3 = run(
        [(3, 1, 1, ()), (-3, 0, 2, ()), (1, 1, 0, (0,)), (-1, 1, 0, (1,))], [two, one, one], far
    )
    up3, down3_y, near0 = run([(3, 0, 0, ()), (-3, 1, 1, ()), (0, 1, 2, ())], [one] * 3, up3_y)
    up3_y, down3 = along(up3_y, 1), along(down3, -1)
    near1 = across_y(near1)
    up = along(bf16(up3, up4), 1)
    down3_y = bf16(down3_y, down4_y)
    down_y = along(down3_y, -1)
    up2_y, down2, up2, down2_y = run(
        [(2, 1, 0, ()), (-2, 0, 1, ()), (2, 0, 2, ()), (-2, 1, 3, ())], [one] * 4, down3_y
    )
    up_y = along_y(bf16(up2_y, up3_y), 1)
    down = along(bf16(down2, down3), -1)
    up1, down1, own0 = run([(1, 0, 0, ()), (-1, 0, 1, ()), (0, 0, 2, ())], [one] * 3, up2)
    up = along(bf16(up2, up), 1)
    down_y = along_y(bf16(down2_y, down_y), -1)
    near1, near0 = lax.optimization_barrier((near1, near0))
    near0 = across_y(near0)
    up = along(bf16(up1, up, up_y, near1[0]), 1)
    down = along(bf16(down1, down, down_y, near1[1]), -1)
    arrivals = add(own0, near0, up, down)
    return (l21[None], parent_in + arrivals)


def solution(mesh):
    return jax.shard_map(
        on_device,
        mesh=mesh,
        in_specs=(
            P("leaf", "panel", None),
            P("leaf", None, None),
            P("leaf", "panel", None),
            P("leaf", "panel"),
            P("leaf", "panel"),
            P("panel", "leaf"),
        ),
        out_specs=(P("leaf", "panel", None), P("panel", "leaf")),
        check_vma=False,
    )
```

time: 284 us -> 69.1 us (0.24)
  waiting for transfers between devices: 246 us -> 20.3 us
  starting transfers between devices: 0.08 us -> 35.9 us
  between operations: 14.1 us -> 0.8 us
  local copies, waits for them, and re-layouts: 13.6 us -> 4.14 us
  matrix products: 7.94 us -> 0 us
  Pallas kernels: 0 us -> 5.91 us
    unnamed x3 -> x0, waiting for transfers between devices: 210 us -> none
    all_gather x1 -> x0, waiting for transfers between devices: 36.5 us -> none  [on_device(): window_piece = lax.all_gather(leading, 'panel', axis=0, tiled=True)]
    ppermute x0 -> x19, starting transfers between devices: none -> 35.9 us  [place(): return lax.ppermute(value, AXES, pairs)]
    ppermute x0 -> x19, waiting for transfers between devices: none -> 20.3 us  [place(): return lax.ppermute(value, AXES, pairs)]
    dot_general x3 -> x0, matrix products: 7.94 us -> none  [the longest x1 3.84 us: on_device(): lax.dot_general(factor, window_piece, (((1,), (1,)), ((), ())), preferred...]
    pallas_call x0 -> x7, Pallas kernels: none -> 5.91 us  [the longest x5 3.99 us: contributions(): pl.pallas_call(body, out_shape=[jax.ShapeDtypeStruct(shape, BF16) for sha...]
    unnamed x10 -> x14, local copies, waits for them, and re-layouts: 8.51 us -> 3.25 us
    convert_element_type x1 -> x0, local copies, waits for them, and re-layouts: 4.28 us -> none  [on_device(): placed.reshape(PT_DEV * TILE, column_span).astype(jnp.bfloat16)]
  transfers between devices with their start and end apart: 2 -> 19, of which waited for: 2 -> 12; matrix products, arithmetic and copies ran while one was open for 0% -> 1% of each run, Pallas kernels for 0% -> 8%
where the time goes in v3:
time: 69.1 us; the launch traced here: 68.8 us
  starting transfers between devices  35.9 us (52%)
  waiting for transfers between devices  20.3 us (29%)
  Pallas kernels  5.91 us (9%)
  local copies, waits for them, and re-layouts  4.14 us (6%)
  other arithmetic  1.79 us (3%)
  between operations  0.8 us (1%)
    ppermute x19, starting transfers between devices, place(): return lax.ppermute(value, AXES, pairs)  35.9 us
    ppermute x19, waiting for transfers between devices, place(): return lax.ppermute(value, AXES, pairs)  20.3 us
    pallas_call x5, Pallas kernels, contributions(): pl.pallas_call(body, out_shape=[jax.ShapeDtypeStruct(shape, BF16) for sha...  3.99 us
    unnamed x14, local copies, waits for them, and re-layouts  3.25 us
    pallas_call x1, Pallas kernels, prepare(): pl.pallas_call(prepare_kernel, out_shape=like + [jax.ShapeDtypeStruct((TI...  1.91 us
  transfers between devices with their start and end apart: 19, of which 12 were waited for; matrix products, arithmetic and copies ran while one was open for 1% of the time, Pallas kernels for 8%

profile of v3, /device:TPU:6, one launch (start us, length us, event | category | flops | bytes accessed | tf_op | source)
XLA Modules:
  0.0 68.8 jit_solution(9279278723338618456)
XLA Ops:
  1.5 1.7 %collective-permute-start = (bf16[128,256]{1,0:T(8,128)(2,1)S(1)}, bf16[128,256]{1,0:T(8,128)(2,1)S(1)}, u32[]{:S(2)}, u32[]{:S(2)}) collective-permute-start(bf16[128,256]{1,0:T(8,128)(2,1)S(1)} %get-tuple-element.67.lead), channel_id=1, source_target_pairs={{0,2},{1,3},{2,0},{3,1},{4,6},{5,7},{6,4},{7,5},{8,10},{9,11},{10,... | collective-permute-start | bytes 196616 | tf_op jit(solution)/shard_map/ppermute | solution.py:28
  3.2 2.2 %copy-done = bf16[1,1024,2048]{2,1,0:T(8,128)(2,1)S(1)} copy-done((bf16[1,1024,2048]{2,1,0:T(8,128)(2,1)S(1)}, bf16[1,1024,2048]{2,1,0:T(8,128)(2,1)}, u32[]{:S(2)}) %copy-start) | copy-done | bytes 4194328
  5.9 2.3 %collective-permute-start.3 = (bf16[2,128,256]{2,1,0:T(8,128)(2,1)S(1)}, bf16[2,128,256]{2,1,0:T(8,128)(2,1)S(1)}, u32[]{:S(2)}, u32[]{:S(2)}) collective-permute-start(bf16[2,128,256]{2,1,0:T(8,128)(2,1)S(1)} %pad_maximum_fusion.1), channel_id=1, source_target_pairs={{0,4},{1,5},{2,6},{3,7},{4,8},{5,9},{6,10},{7,11},{8,12},{9,13},{1... | collective-permute-start | bytes 393224 | tf_op jit(solution)/shard_map/ppermute | solution.py:28
  8.2 1.6 %collective-permute-start.1 = (bf16[2,128,256]{2,1,0:T(8,128)(2,1)S(1)}, bf16[2,128,256]{2,1,0:T(8,128)(2,1)S(1)}, u32[]{:S(2)}, u32[]{:S(2)}) collective-permute-start(bf16[2,128,256]{2,1,0:T(8,128)(2,1)S(1)} %pad_maximum_fusion.1), channel_id=1, source_target_pairs={{0,8},{1,9},{2,10},{3,11},{4,12},{5,13},{6,14},{7,15},{8,0},{9,1},... | collective-permute-start | bytes 393224 | tf_op jit(solution)/shard_map/ppermute | solution.py:28
  9.8 1.0 %copy-done.2 = bf16[1,1024,256]{2,1,0:T(8,128)(2,1)S(1)} copy-done((bf16[1,1024,256]{2,1,0:T(8,128)(2,1)S(1)}, bf16[1,1024,256]{2,1,0:T(8,128)(2,1)}, u32[]{:S(2)}) %copy-start.2) | copy-done | bytes 524312
  10.9 1.9 %shard_map.78 = (bf16[1024,256]{1,0:T(8,128)(2,1)}, bf16[1024,256]{1,0:T(8,128)(2,1)S(1)}, bf16[1024,2048]{1,0:T(8,128)(2,1)S(1)}, s32[8,128]{1,0:T(8,128)S(1)}, bf16[256,256]{1,0:T(8,128)(2,1)S(1)}) custom-call(s32[1,16]{1,0:T(1,128)S(1)} %pad_add_fusion.maps, bf16[1024,256]{1,0:T(8,128)(2,1)S(1)} %bitcast.15, bf16[256,256]{1,0:T(8,128)(2,1)S(1)} %bitcast.16, ...), custom_call_target="tpu_custom_call" | custom-call | flops 134217728 | bytes 8388608 | tf_op jit(solution)/shard_map/pallas_call | solution.py:127
  12.8 3.0 %collective-permute-done.2 = bf16[2,128,256]{2,1,0:T(8,128)(2,1)S(1)} collective-permute-done((bf16[2,128,256]{2,1,0:T(8,128)(2,1)S(1)}, bf16[2,128,256]{2,1,0:T(8,128)(2,1)S(1)}, u32[]{:S(2)}, u32[]{:S(2)}) %collective-permute-start.2) | collective-permute-done | bytes 131104 | tf_op jit(solution)/shard_map/ppermute | solution.py:28
  16.0 1.9 %collective-permute-done.4.far = bf16[8,128,256]{2,1,0:T(8,128)(2,1)S(1)} collective-permute-done((bf16[8,128,256]{2,1,0:T(8,128)(2,1)S(1)}, bf16[8,128,256]{2,1,0:T(8,128)(2,1)S(1)}, u32[]{:S(2)}, u32[]{:S(2)}) %collective-permute-start.4) | collective-permute-done | bytes 524320 | tf_op jit(solution)/shard_map/ppermute | solution.py:28
  18.4 1.2 %collective-permute-start.8 = (bf16[1024,128]{1,0:T(8,128)(2,1)S(1)}, bf16[1024,128]{1,0:T(8,128)(2,1)S(1)}, u32[]{:S(2)}, u32[]{:S(2)}) collective-permute-start(bf16[1024,128]{1,0:T(8,128)(2,1)S(1)} %get-tuple-element.47.after), channel_id=1, source_target_pairs={{0,16},{1,17},{2,18},{3,19},{4,20},{5,21},{6,22},{7,23},{8,24},{9,... | collective-permute-start | bytes 786440 | tf_op jit(solution)/shard_map/ppermute | solution.py:28
  20.5 2.0 %collective-permute-start.11 = (bf16[1024,128]{1,0:T(8,128)(2,1)S(1)}, bf16[1024,128]{1,0:T(8,128)(2,1)S(1)}, u32[]{:S(2)}, u32[]{:S(2)}) collective-permute-start(bf16[1024,128]{1,0:T(8,128)(2,1)S(1)} %get-tuple-element.48.after), channel_id=1, source_target_pairs={{0,16},{1,17},{2,18},{3,19},{4,20},{5,21},{6,22},{7,23},{8,24},{9,... | collective-permute-start | bytes 786440 | tf_op jit(solution)/shard_map/ppermute | solution.py:28
  22.5 2.1 %collective-permute-start.5 = (bf16[1024,128]{1,0:T(8,128)(2,1)S(1)}, bf16[1024,128]{1,0:T(8,128)(2,1)S(1)}, u32[]{:S(2)}, u32[]{:S(2)}) collective-permute-start(bf16[1024,128]{1,0:T(8,128)(2,1)S(1)} %get-tuple-element.50), channel_id=1, source_target_pairs={{0,112},{1,113},{2,114},{3,115},{4,116},{5,117},{6,118},{7,119},{8... | collective-permute-start | bytes 786440 | tf_op jit(solution)/shard_map/ppermute | solution.py:28
  24.6 2.9 %collective-permute-start.6 = (bf16[2,1024,128]{2,1,0:T(8,128)(2,1)S(1)}, bf16[2,1024,128]{2,1,0:T(8,128)(2,1)S(1)}, u32[]{:S(2)}, u32[]{:S(2)}) collective-permute-start(bf16[2,1024,128]{2,1,0:T(8,128)(2,1)S(1)} %get-tuple-element.53), channel_id=1, source_target_pairs={{0,128},{1,129},{2,130},{3,131},{4,132},{5,133},{6,134},{7,135},{8... | collective-permute-start | bytes 1572872 | tf_op jit(solution)/shard_map/ppermute | solution.py:28
  27.5 2.0 %collective-permute-start.14 = (bf16[1024,128]{1,0:T(8,128)(2,1)S(1)}, bf16[1024,128]{1,0:T(8,128)(2,1)S(1)}, u32[]{:S(2)}, u32[]{:S(2)}) collective-permute-start(bf16[1024,128]{1,0:T(8,128)(2,1)S(1)} %get-tuple-element.62), channel_id=1, source_target_pairs={{0,112},{1,113},{2,114},{3,115},{4,116},{5,117},{6,118},{7,119},{8... | collective-permute-start | bytes 786440 | tf_op jit(solution)/shard_map/ppermute | solution.py:28
  31.4 3.8 %collective-permute-start.16 = (bf16[1024,128]{1,0:T(8,128)(2,1)S(1)}, bf16[1024,128]{1,0:T(8,128)(2,1)S(1)}, u32[]{:S(2)}, u32[]{:S(2)}) collective-permute-start(bf16[1024,128]{1,0:T(8,128)(2,1)S(1)} %add_convert_fusion.5.after), channel_id=1, source_target_pairs={{0,112},{1,113},{2,114},{3,115},{4,116},{5,117},{6,118},{7,119},{8... | collective-permute-start | bytes 786440 | tf_op jit(solution)/shard_map/ppermute | solution.py:28
  36.3 2.1 %collective-permute-start.12 = (bf16[1024,128]{1,0:T(8,128)(2,1)S(1)}, bf16[1024,128]{1,0:T(8,128)(2,1)S(1)}, u32[]{:S(2)}, u32[]{:S(2)}) collective-permute-start(bf16[1024,128]{1,0:T(8,128)(2,1)S(1)} %add_convert_fusion.2), channel_id=1, source_target_pairs={{0,144},{1,145},{2,146},{3,147},{4,148},{5,149},{6,150},{7,151},{8... | collective-permute-start | bytes 786440 | tf_op jit(solution)/shard_map/ppermute | solution.py:28
  38.6 3.8 %collective-permute-start.15 = (bf16[1024,128]{1,0:T(8,128)(2,1)S(1)}, bf16[1024,128]{1,0:T(8,128)(2,1)S(1)}, u32[]{:S(2)}, u32[]{:S(2)}) collective-permute-start(bf16[1024,128]{1,0:T(8,128)(2,1)S(1)} %add_convert_fusion.1), channel_id=1, source_target_pairs={{0,112},{1,113},{2,114},{3,115},{4,116},{5,117},{6,118},{7,119},{8... | collective-permute-start | bytes 786440 | tf_op jit(solution)/shard_map/ppermute | solution.py:28
  42.6 6.1 %collective-permute-start.17 = (bf16[1024,128]{1,0:T(8,128)(2,1)S(1)}, bf16[1024,128]{1,0:T(8,128)(2,1)S(1)}, u32[]{:S(2)}, u32[]{:S(2)}) collective-permute-start(bf16[1024,128]{1,0:T(8,128)(2,1)S(1)} %add_convert_fusion), channel_id=1, source_target_pairs={{0,240},{1,241},{2,242},{3,243},{4,244},{5,245},{6,246},{7,247},{8... | collective-permute-start | bytes 786440 | tf_op jit(solution)/shard_map/ppermute | solution.py:28
  50.1 3.0 %collective-permute-done.10 = bf16[1024,128]{1,0:T(8,128)(2,1)S(1)} collective-permute-done((bf16[1024,128]{1,0:T(8,128)(2,1)S(1)}, bf16[1024,128]{1,0:T(8,128)(2,1)S(1)}, u32[]{:S(2)}, u32[]{:S(2)}) %collective-permute-start.10) | collective-permute-done | bytes 262176 | tf_op jit(solution)/shard_map/ppermute | solution.py:28
  53.1 2.3 %collective-permute-done.17 = bf16[1024,128]{1,0:T(8,128)(2,1)S(1)} collective-permute-done((bf16[1024,128]{1,0:T(8,128)(2,1)S(1)}, bf16[1024,128]{1,0:T(8,128)(2,1)S(1)}, u32[]{:S(2)}, u32[]{:S(2)}) %collective-permute-start.17) | collective-permute-done | bytes 262176 | tf_op jit(solution)/shard_map/ppermute | solution.py:28
  55.7 3.8 %collective-permute-start.18 = (bf16[1024,128]{1,0:T(8,128)(2,1)S(1)}, bf16[1024,128]{1,0:T(8,128)(2,1)S(1)}, u32[]{:S(2)}, u32[]{:S(2)}) collective-permute-start(bf16[1024,128]{1,0:T(8,128)(2,1)S(1)} %get-tuple-element.65), channel_id=1, source_target_pairs={{0,112},{1,113},{2,114},{3,115},{4,116},{5,117},{6,118},{7,119},{8... | collective-permute-start | bytes 786440 | tf_op jit(solution)/shard_map/ppermute | solution.py:28
  59.5 1.4 %collective-permute-done.7 = bf16[1024,128]{1,0:T(8,128)(2,1)S(1)} collective-permute-done((bf16[1024,128]{1,0:T(8,128)(2,1)S(1)}, bf16[1024,128]{1,0:T(8,128)(2,1)S(1)}, u32[]{:S(2)}, u32[]{:S(2)}) %collective-permute-start.7) | collective-permute-done | bytes 262176 | tf_op jit(solution)/shard_map/ppermute | solution.py:28
  60.9 3.5 %collective-permute-done.18 = bf16[1024,128]{1,0:T(8,128)(2,1)S(1)} collective-permute-done((bf16[1024,128]{1,0:T(8,128)(2,1)S(1)}, bf16[1024,128]{1,0:T(8,128)(2,1)S(1)}, u32[]{:S(2)}, u32[]{:S(2)}) %collective-permute-start.18) | collective-permute-done | bytes 262176 | tf_op jit(solution)/shard_map/ppermute | solution.py:28
  64.5 3.4 %collective-permute-done.13 = bf16[1024,128]{1,0:T(8,128)(2,1)S(1)} collective-permute-done((bf16[1024,128]{1,0:T(8,128)(2,1)S(1)}, bf16[1024,128]{1,0:T(8,128)(2,1)S(1)}, u32[]{:S(2)}, u32[]{:S(2)}) %collective-permute-start.13) | collective-permute-done | bytes 262176 | tf_op jit(solution)/shard_map/ppermute | solution.py:28
  67.9 0.9 %add_add_fusion = f32[1024,128]{1,0:T(8,128)} fusion(f32[1024,128]{1,0:T(8,128)S(1)} %copy-done.4, bf16[1024,128]{1,0:T(8,128)(2,1)S(1)} %collective-permute-done.18, bf16[1024,128]{1,0:T(8,128)(2,1)S(1)} %collective-permute-done.13, bf16[1024,128]{1,0:T(8,128)(2,1)S(1)} %collective-permute-done.7, bf16[1024,128]{1,0:T(8,128)(2,1)S(1)} %get-tuple-element.52), kind=kLoop, calls=%fused_computation.5 | loop fusion | flops 1048576 | bytes 2097152 | tf_op jit(solution)/shard_map/add | solution.py:213
  (47 shorter events, 7.9 us)
Async XLA Ops:
  0.6 9.2 %copy-start.3 = (bf16[1,256,256]{2,1,0:T(8,128)(2,1)S(1)}, bf16[1,256,256]{2,1,0:T(8,128)(2,1)}, u32[]{:S(2)}) copy-start(bf16[1,256,256]{2,1,0:T(8,128)(2,1)} %param.7) | copy-start | bytes 393220
  0.6 9.1 %copy-start.5 = (s32[1,8]{1,0:T(1,128)S(1)}, s32[1,8]{1,0:T(1,128)}, u32[]{:S(2)}) copy-start(s32[1,8]{1,0:T(1,128)} %param.9) | copy-start | bytes 100
  0.7 9.1 %copy-start.6 = (s32[1,8]{1,0:T(1,128)S(1)}, s32[1,8]{1,0:T(1,128)}, u32[]{:S(2)}) copy-start(s32[1,8]{1,0:T(1,128)} %param.10) | copy-start | bytes 100
  1.5 4.4 %collective-permute-start = (bf16[128,256]{1,0:T(8,128)(2,1)S(1)}, bf16[128,256]{1,0:T(8,128)(2,1)S(1)}, u32[]{:S(2)}, u32[]{:S(2)}) collective-permute-start(bf16[128,256]{1,0:T(8,128)(2,1)S(1)} %get-tuple-element.67.lead), channel_id=1, source_target_pairs={{0,2},{1,3},{2,0},{3,1},{4,6},{5,7},{6,4},{7,5},{8,10},{9,11},{10,... | collective-permute-start | bytes 196616 | tf_op jit(solution)/shard_map/ppermute | solution.py:28
  5.4 4.4 %copy-start.1 = (bf16[1,1024,2048]{2,1,0:T(8,128)(2,1)S(1)}, bf16[1,1024,2048]{2,1,0:T(8,128)(2,1)}, u32[]{:S(2)}) copy-start(bf16[1,1024,2048]{2,1,0:T(8,128)(2,1)} %param.8) | copy-start | bytes 12582916
  5.9 6.9 %collective-permute-start.3 = (bf16[2,128,256]{2,1,0:T(8,128)(2,1)S(1)}, bf16[2,128,256]{2,1,0:T(8,128)(2,1)S(1)}, u32[]{:S(2)}, u32[]{:S(2)}) collective-permute-start(bf16[2,128,256]{2,1,0:T(8,128)(2,1)S(1)} %pad_maximum_fusion.1), channel_id=1, source_target_pairs={{0,4},{1,5},{2,6},{3,7},{4,8},{5,9},{6,10},{7,11},{8,12},{9,13},{1... | collective-permute-start | bytes 393224 | tf_op jit(solution)/shard_map/ppermute | solution.py:28
  8.2 7.6 %collective-permute-start.2 = (bf16[2,128,256]{2,1,0:T(8,128)(2,1)S(1)}, bf16[2,128,256]{2,1,0:T(8,128)(2,1)S(1)}, u32[]{:S(2)}, u32[]{:S(2)}) collective-permute-start(bf16[2,128,256]{2,1,0:T(8,128)(2,1)S(1)} %pad_maximum_fusion.1), channel_id=1, source_target_pairs={{0,12},{1,13},{2,14},{3,15},{4,0},{5,1},{6,2},{7,3},{8,4},{9,5},{1... | collective-permute-start | bytes 393224 | tf_op jit(solution)/shard_map/ppermute | solution.py:28
  8.2 7.6 %collective-permute-start.1 = (bf16[2,128,256]{2,1,0:T(8,128)(2,1)S(1)}, bf16[2,128,256]{2,1,0:T(8,128)(2,1)S(1)}, u32[]{:S(2)}, u32[]{:S(2)}) collective-permute-start(bf16[2,128,256]{2,1,0:T(8,128)(2,1)S(1)} %pad_maximum_fusion.1), channel_id=1, source_target_pairs={{0,8},{1,9},{2,10},{3,11},{4,12},{5,13},{6,14},{7,15},{8,0},{9,1},... | collective-permute-start | bytes 393224 | tf_op jit(solution)/shard_map/ppermute | solution.py:28
  15.9 2.0 %collective-permute-start.4 = (bf16[8,128,256]{2,1,0:T(8,128)(2,1)S(1)}, bf16[8,128,256]{2,1,0:T(8,128)(2,1)S(1)}, u32[]{:S(2)}, u32[]{:S(2)}) collective-permute-start(bf16[8,128,256]{2,1,0:T(8,128)(2,1)S(1)} %pad_maximum_fusion.own), channel_id=1, source_target_pairs={{0,1},{1,0},{2,3},{3,2},{4,5},{5,4},{6,7},{7,6},{8,9},{9,8},{10,11... | collective-permute-start | bytes 1572872 | tf_op jit(solution)/shard_map/ppermute | solution.py:28
  18.4 12.2 %collective-permute-start.8 = (bf16[1024,128]{1,0:T(8,128)(2,1)S(1)}, bf16[1024,128]{1,0:T(8,128)(2,1)S(1)}, u32[]{:S(2)}, u32[]{:S(2)}) collective-permute-start(bf16[1024,128]{1,0:T(8,128)(2,1)S(1)} %get-tuple-element.47.after), channel_id=1, source_target_pairs={{0,16},{1,17},{2,18},{3,19},{4,20},{5,21},{6,22},{7,23},{8,24},{9,... | collective-permute-start | bytes 786440 | tf_op jit(solution)/shard_map/ppermute | solution.py:28
  20.5 15.8 %collective-permute-start.11 = (bf16[1024,128]{1,0:T(8,128)(2,1)S(1)}, bf16[1024,128]{1,0:T(8,128)(2,1)S(1)}, u32[]{:S(2)}, u32[]{:S(2)}) collective-permute-start(bf16[1024,128]{1,0:T(8,128)(2,1)S(1)} %get-tuple-element.48.after), channel_id=1, source_target_pairs={{0,16},{1,17},{2,18},{3,19},{4,20},{5,21},{6,22},{7,23},{8,24},{9,... | collective-permute-start | bytes 786440 | tf_op jit(solution)/shard_map/ppermute | solution.py:28
  22.5 8.8 %collective-permute-start.5 = (bf16[1024,128]{1,0:T(8,128)(2,1)S(1)}, bf16[1024,128]{1,0:T(8,128)(2,1)S(1)}, u32[]{:S(2)}, u32[]{:S(2)}) collective-permute-start(bf16[1024,128]{1,0:T(8,128)(2,1)S(1)} %get-tuple-element.50), channel_id=1, source_target_pairs={{0,112},{1,113},{2,114},{3,115},{4,116},{5,117},{6,118},{7,119},{8... | collective-permute-start | bytes 786440 | tf_op jit(solution)/shard_map/ppermute | solution.py:28
  24.6 25.0 %collective-permute-start.6 = (bf16[2,1024,128]{2,1,0:T(8,128)(2,1)S(1)}, bf16[2,1024,128]{2,1,0:T(8,128)(2,1)S(1)}, u32[]{:S(2)}, u32[]{:S(2)}) collective-permute-start(bf16[2,1024,128]{2,1,0:T(8,128)(2,1)S(1)} %get-tuple-element.53), channel_id=1, source_target_pairs={{0,128},{1,129},{2,130},{3,131},{4,132},{5,133},{6,134},{7,135},{8... | collective-permute-start | bytes 1572872 | tf_op jit(solution)/shard_map/ppermute | solution.py:28
  27.5 10.9 %collective-permute-start.14 = (bf16[1024,128]{1,0:T(8,128)(2,1)S(1)}, bf16[1024,128]{1,0:T(8,128)(2,1)S(1)}, u32[]{:S(2)}, u32[]{:S(2)}) collective-permute-start(bf16[1024,128]{1,0:T(8,128)(2,1)S(1)} %get-tuple-element.62), channel_id=1, source_target_pairs={{0,112},{1,113},{2,114},{3,115},{4,116},{5,117},{6,118},{7,119},{8... | collective-permute-start | bytes 786440 | tf_op jit(solution)/shard_map/ppermute | solution.py:28
  30.7 11.6 %collective-permute-start.9 = (bf16[1024,128]{1,0:T(8,128)(2,1)S(1)}, bf16[1024,128]{1,0:T(8,128)(2,1)S(1)}, u32[]{:S(2)}, u32[]{:S(2)}) collective-permute-start(bf16[1024,128]{1,0:T(8,128)(2,1)S(1)} %add_convert_fusion.4), channel_id=1, source_target_pairs={{0,16},{1,17},{2,18},{3,19},{4,20},{5,21},{6,22},{7,23},{8,24},{9,... | collective-permute-start | bytes 786440 | tf_op jit(solution)/shard_map/ppermute | solution.py:28
  31.4 11.2 %collective-permute-start.16 = (bf16[1024,128]{1,0:T(8,128)(2,1)S(1)}, bf16[1024,128]{1,0:T(8,128)(2,1)S(1)}, u32[]{:S(2)}, u32[]{:S(2)}) collective-permute-start(bf16[1024,128]{1,0:T(8,128)(2,1)S(1)} %add_convert_fusion.5.after), channel_id=1, source_target_pairs={{0,112},{1,113},{2,114},{3,115},{4,116},{5,117},{6,118},{7,119},{8... | collective-permute-start | bytes 786440 | tf_op jit(solution)/shard_map/ppermute | solution.py:28
  36.3 13.7 %collective-permute-start.12 = (bf16[1024,128]{1,0:T(8,128)(2,1)S(1)}, bf16[1024,128]{1,0:T(8,128)(2,1)S(1)}, u32[]{:S(2)}, u32[]{:S(2)}) collective-permute-start(bf16[1024,128]{1,0:T(8,128)(2,1)S(1)} %add_convert_fusion.2), channel_id=1, source_target_pairs={{0,144},{1,145},{2,146},{3,147},{4,148},{5,149},{6,150},{7,151},{8... | collective-permute-start | bytes 786440 | tf_op jit(solution)/shard_map/ppermute | solution.py:28
  38.6 11.5 %collective-permute-start.15 = (bf16[1024,128]{1,0:T(8,128)(2,1)S(1)}, bf16[1024,128]{1,0:T(8,128)(2,1)S(1)}, u32[]{:S(2)}, u32[]{:S(2)}) collective-permute-start(bf16[1024,128]{1,0:T(8,128)(2,1)S(1)} %add_convert_fusion.1), channel_id=1, source_target_pairs={{0,112},{1,113},{2,114},{3,115},{4,116},{5,117},{6,118},{7,119},{8... | collective-permute-start | bytes 786440 | tf_op jit(solution)/shard_map/ppermute | solution.py:28
  42.4 10.7 %collective-permute-start.10 = (bf16[1024,128]{1,0:T(8,128)(2,1)S(1)}, bf16[1024,128]{1,0:T(8,128)(2,1)S(1)}, u32[]{:S(2)}, u32[]{:S(2)}) collective-permute-start(bf16[1024,128]{1,0:T(8,128)(2,1)S(1)} %add_convert_fusion.3), channel_id=1, source_target_pairs={{0,16},{1,17},{2,18},{3,19},{4,20},{5,21},{6,22},{7,23},{8,24},{9,... | collective-permute-start | bytes 786440 | tf_op jit(solution)/shard_map/ppermute | solution.py:28
  42.6 25.3 %copy-start.4 = (f32[1024,128]{1,0:T(8,128)S(1)}, f32[1024,128]{1,0:T(8,128)}, u32[]{:S(2)}) copy-start(f32[1024,128]{1,0:T(8,128)} %param.11) | copy-start | bytes 1572868
  42.6 12.8 %collective-permute-start.17 = (bf16[1024,128]{1,0:T(8,128)(2,1)S(1)}, bf16[1024,128]{1,0:T(8,128)(2,1)S(1)}, u32[]{:S(2)}, u32[]{:S(2)}) collective-permute-start(bf16[1024,128]{1,0:T(8,128)(2,1)S(1)} %add_convert_fusion), channel_id=1, source_target_pairs={{0,240},{1,241},{2,242},{3,243},{4,244},{5,245},{6,246},{7,247},{8... | collective-permute-start | bytes 786440 | tf_op jit(solution)/shard_map/ppermute | solution.py:28
  49.6 11.3 %collective-permute-start.7 = (bf16[1024,128]{1,0:T(8,128)(2,1)S(1)}, bf16[1024,128]{1,0:T(8,128)(2,1)S(1)}, u32[]{:S(2)}, u32[]{:S(2)}) collective-permute-start(bf16[1024,128]{1,0:T(8,128)(2,1)S(1)} %get-tuple-element.55), channel_id=1, source_target_pairs={{0,128},{1,129},{2,130},{3,131},{4,132},{5,133},{6,134},{7,135},{8... | collective-permute-start | bytes 786440 | tf_op jit(solution)/shard_map/ppermute | solution.py:28
  55.7 8.8 %collective-permute-start.18 = (bf16[1024,128]{1,0:T(8,128)(2,1)S(1)}, bf16[1024,128]{1,0:T(8,128)(2,1)S(1)}, u32[]{:S(2)}, u32[]{:S(2)}) collective-permute-start(bf16[1024,128]{1,0:T(8,128)(2,1)S(1)} %get-tuple-element.65), channel_id=1, source_target_pairs={{0,112},{1,113},{2,114},{3,115},{4,116},{5,117},{6,118},{7,119},{8... | collective-permute-start | bytes 786440 | tf_op jit(solution)/shard_map/ppermute | solution.py:28
  59.5 8.4 %collective-permute-start.13 = (bf16[1024,128]{1,0:T(8,128)(2,1)S(1)}, bf16[1024,128]{1,0:T(8,128)(2,1)S(1)}, u32[]{:S(2)}, u32[]{:S(2)}) collective-permute-start(bf16[1024,128]{1,0:T(8,128)(2,1)S(1)} %get-tuple-element.64), channel_id=1, source_target_pairs={{0,16},{1,17},{2,18},{3,19},{4,20},{5,21},{6,22},{7,23},{8,24},{9,... | collective-permute-start | bytes 786440 | tf_op jit(solution)/shard_map/ppermute | solution.py:28
  (2 other events, 3.2 us)

commit v4 on v3

--- a/solution.py
+++ b/solution.py
@@ -188,11 +188,13 @@
 
     far, far_y = run([(4, 0, 0, ()), (4, 1, 1, ())], [one, one], brought)
     up4, down4_y = along(far, 1), along(far_y, -1)
-    near1, up3_y, down3 = run(
-        [(3, 1, 1, ()), (-3, 0, 2, ()), (1, 1, 0, (0,)), (-1, 1, 0, (1,))], [two, one, one], far
-    )
-    up3, down3_y, near0 = run([(3, 0, 0, ()), (-3, 1, 1, ()), (0, 1, 2, ())], [one] * 3, up3_y)
-    up3_y, down3 = along(up3_y, 1), along(down3, -1)
+    next_y, next_ = run([(3, 1, 0, ()), (-3, 0, 1, ())], [one, one], far)
+    up3_y, down3 = along(next_y, 1), along(next_, -1)
+    near1, near0, up3, down3_y = run(
+        [(1, 1, 0, (0,)), (-1, 1, 0, (1,)), (3, 0, 2, ()), (-3, 1, 3, ()), (0, 1, 1, ())],
+        [two, one, one, one],
+        next_y,
+    )
     near1 = across_y(near1)
     up = along(bf16(up3, up4), 1)
     down3_y = bf16(down3_y, down4_y)
@@ -205,9 +207,10 @@
     up1, down1, own0 = run([(1, 0, 0, ()), (-1, 0, 1, ()), (0, 0, 2, ())], [one] * 3, up2)
     up = along(bf16(up2, up), 1)
     down_y = along_y(bf16(down2_y, down_y), -1)
-    near1, near0 = lax.optimization_barrier((near1, near0))
+    up_y, near0 = lax.optimization_barrier((up_y, near0))
     near0 = across_y(near0)
-    up = along(bf16(up1, up, up_y, near1[0]), 1)
+    up, down1 = lax.optimization_barrier((bf16(up1, up, up_y, near1[0]), down1))
+    up = along(up, 1)
     down = along(bf16(down1, down, down_y, near1[1]), -1)
     arrivals = add(own0, near0, up, down)
     return (l21[None], parent_in + arrivals)

time: 69.1 us -> 68.5 us (level)
  the two profiles are of different devices: /device:TPU:6 before, /device:TPU:16 now
where the time goes in v4:
time: 68.5 us; the launch traced here: 68.3 us
  starting transfers between devices  31.2 us (46%)
  waiting for transfers between devices  24.4 us (36%)
  Pallas kernels  5.91 us (9%)
  local copies, waits for them, and re-layouts  4.14 us (6%)
  other arithmetic  1.8 us (3%)
  between operations  0.82 us (1%)
    ppermute x19, starting transfers between devices, place(): return lax.ppermute(value, AXES, pairs)  31.2 us
    ppermute x19, waiting for transfers between devices, place(): return lax.ppermute(value, AXES, pairs)  24.4 us
    pallas_call x5, Pallas kernels, contributions(): pl.pallas_call(body, out_shape=[jax.ShapeDtypeStruct(shape, BF16) for sha...  4 us
    unnamed x14, local copies, waits for them, and re-layouts  3.25 us
    pallas_call x1, Pallas kernels, prepare(): pl.pallas_call(prepare_kernel, out_shape=like + [jax.ShapeDtypeStruct((TI...  1.9 us
  transfers between devices with their start and end apart: 19, of which 11 were waited for; matrix products, arithmetic and copies ran while one was open for 1% of the time, Pallas kernels for 8%

profile of v4, /device:TPU:16, one launch (start us, length us, event | category | flops | bytes accessed | tf_op | source)
XLA Modules:
  0.0 68.3 jit_solution(2384548764586083187)
XLA Ops:
  1.5 1.4 %collective-permute-start = (bf16[128,256]{1,0:T(8,128)(2,1)S(1)}, bf16[128,256]{1,0:T(8,128)(2,1)S(1)}, u32[]{:S(2)}, u32[]{:S(2)}) collective-permute-start(bf16[128,256]{1,0:T(8,128)(2,1)S(1)} %get-tuple-element.69.lead), channel_id=1, source_target_pairs={{0,2},{1,3},{2,0},{3,1},{4,6},{5,7},{6,4},{7,5},{8,10},{9,11},{10,... | collective-permute-start | bytes 196616 | tf_op jit(solution)/shard_map/ppermute | solution.py:28
  2.9 2.2 %copy-done = bf16[1,1024,2048]{2,1,0:T(8,128)(2,1)S(1)} copy-done((bf16[1,1024,2048]{2,1,0:T(8,128)(2,1)S(1)}, bf16[1,1024,2048]{2,1,0:T(8,128)(2,1)}, u32[]{:S(2)}) %copy-start) | copy-done | bytes 4194328
  5.9 1.6 %collective-permute-start.3 = (bf16[2,128,256]{2,1,0:T(8,128)(2,1)S(1)}, bf16[2,128,256]{2,1,0:T(8,128)(2,1)S(1)}, u32[]{:S(2)}, u32[]{:S(2)}) collective-permute-start(bf16[2,128,256]{2,1,0:T(8,128)(2,1)S(1)} %pad_maximum_fusion.1), channel_id=1, source_target_pairs={{0,4},{1,5},{2,6},{3,7},{4,8},{5,9},{6,10},{7,11},{8,12},{9,13},{1... | collective-permute-start | bytes 393224 | tf_op jit(solution)/shard_map/ppermute | solution.py:28
  7.5 1.7 %collective-permute-start.2 = (bf16[2,128,256]{2,1,0:T(8,128)(2,1)S(1)}, bf16[2,128,256]{2,1,0:T(8,128)(2,1)S(1)}, u32[]{:S(2)}, u32[]{:S(2)}) collective-permute-start(bf16[2,128,256]{2,1,0:T(8,128)(2,1)S(1)} %pad_maximum_fusion.1), channel_id=1, source_target_pairs={{0,12},{1,13},{2,14},{3,15},{4,0},{5,1},{6,2},{7,3},{8,4},{9,5},{1... | collective-permute-start | bytes 393224 | tf_op jit(solution)/shard_map/ppermute | solution.py:28
  9.2 1.8 %collective-permute-start.1 = (bf16[2,128,256]{2,1,0:T(8,128)(2,1)S(1)}, bf16[2,128,256]{2,1,0:T(8,128)(2,1)S(1)}, u32[]{:S(2)}, u32[]{:S(2)}) collective-permute-start(bf16[2,128,256]{2,1,0:T(8,128)(2,1)S(1)} %pad_maximum_fusion.1), channel_id=1, source_target_pairs={{0,8},{1,9},{2,10},{3,11},{4,12},{5,13},{6,14},{7,15},{8,0},{9,1},... | collective-permute-start | bytes 393224 | tf_op jit(solution)/shard_map/ppermute | solution.py:28
  11.1 1.0 %copy-done.2 = bf16[1,1024,256]{2,1,0:T(8,128)(2,1)S(1)} copy-done((bf16[1,1024,256]{2,1,0:T(8,128)(2,1)S(1)}, bf16[1,1024,256]{2,1,0:T(8,128)(2,1)}, u32[]{:S(2)}) %copy-start.2) | copy-done | bytes 524312
  12.2 1.9 %shard_map.78 = (bf16[1024,256]{1,0:T(8,128)(2,1)}, bf16[1024,256]{1,0:T(8,128)(2,1)S(1)}, bf16[1024,2048]{1,0:T(8,128)(2,1)S(1)}, s32[8,128]{1,0:T(8,128)S(1)}, bf16[256,256]{1,0:T(8,128)(2,1)S(1)}) custom-call(s32[1,16]{1,0:T(1,128)S(1)} %pad_add_fusion.maps, bf16[1024,256]{1,0:T(8,128)(2,1)S(1)} %bitcast.19, bf16[256,256]{1,0:T(8,128)(2,1)S(1)} %bitcast.20, ...), custom_call_target="tpu_custom_call" | custom-call | flops 134217728 | bytes 8388608 | tf_op jit(solution)/shard_map/pallas_call | solution.py:127
  14.1 1.7 %collective-permute-done.1 = bf16[2,128,256]{2,1,0:T(8,128)(2,1)S(1)} collective-permute-done((bf16[2,128,256]{2,1,0:T(8,128)(2,1)S(1)}, bf16[2,128,256]{2,1,0:T(8,128)(2,1)S(1)}, u32[]{:S(2)}, u32[]{:S(2)}) %collective-permute-start.1) | collective-permute-done | bytes 131104 | tf_op jit(solution)/shard_map/ppermute | solution.py:28
  15.9 1.9 %collective-permute-done.4.far = bf16[8,128,256]{2,1,0:T(8,128)(2,1)S(1)} collective-permute-done((bf16[8,128,256]{2,1,0:T(8,128)(2,1)S(1)}, bf16[8,128,256]{2,1,0:T(8,128)(2,1)S(1)}, u32[]{:S(2)}, u32[]{:S(2)}) %collective-permute-start.4) | collective-permute-done | bytes 524320 | tf_op jit(solution)/shard_map/ppermute | solution.py:28
  18.4 5.9 %collective-permute-start.5 = (bf16[1024,128]{1,0:T(8,128)(2,1)S(1)}, bf16[1024,128]{1,0:T(8,128)(2,1)S(1)}, u32[]{:S(2)}, u32[]{:S(2)}) collective-permute-start(bf16[1024,128]{1,0:T(8,128)(2,1)S(1)} %get-tuple-element.52), channel_id=1, source_target_pairs={{0,112},{1,113},{2,114},{3,115},{4,116},{5,117},{6,118},{7,119},{8... | collective-permute-start | bytes 786440 | tf_op jit(solution)/shard_map/ppermute | solution.py:28
  24.9 3.3 %collective-permute-start.14 = (bf16[1024,128]{1,0:T(8,128)(2,1)S(1)}, bf16[1024,128]{1,0:T(8,128)(2,1)S(1)}, u32[]{:S(2)}, u32[]{:S(2)}) collective-permute-start(bf16[1024,128]{1,0:T(8,128)(2,1)S(1)} %get-tuple-element.66), channel_id=1, source_target_pairs={{0,112},{1,113},{2,114},{3,115},{4,116},{5,117},{6,118},{7,119},{8... | collective-permute-start | bytes 786440 | tf_op jit(solution)/shard_map/ppermute | solution.py:28
  28.2 1.2 %shard_map.81 = (bf16[2,1024,128]{2,1,0:T(8,128)(2,1)S(1)}, bf16[1024,128]{1,0:T(8,128)(2,1)S(1)}, bf16[1024,128]{1,0:T(8,128)(2,1)S(1)}, bf16[1024,128]{1,0:T(8,128)(2,1)S(1)}) custom-call(bf16[1024,256]{1,0:T(8,128)(2,1)S(1)} %get-tuple-element.43.factor, bf16[1024,2048]{1,0:T(8,128)(2,1)S(1)} %get-tuple-element.44.trailing, ...), custom_call_target="tpu_custom_call" | custom-call | flops 335544320 | bytes 3145728 | tf_op jit(solution)/shard_map/pallas_call | solution.py:97
  30.0 1.0 %collective-permute-done.5 = bf16[1024,128]{1,0:T(8,128)(2,1)S(1)} collective-permute-done((bf16[1024,128]{1,0:T(8,128)(2,1)S(1)}, bf16[1024,128]{1,0:T(8,128)(2,1)S(1)}, u32[]{:S(2)}, u32[]{:S(2)}) %collective-permute-start.5) | collective-permute-done | bytes 262176 | tf_op jit(solution)/shard_map/ppermute | solution.py:28
  31.1 3.8 %collective-permute-start.16 = (bf16[1024,128]{1,0:T(8,128)(2,1)S(1)}, bf16[1024,128]{1,0:T(8,128)(2,1)S(1)}, u32[]{:S(2)}, u32[]{:S(2)}) collective-permute-start(bf16[1024,128]{1,0:T(8,128)(2,1)S(1)} %add_convert_fusion.5.after), channel_id=1, source_target_pairs={{0,112},{1,113},{2,114},{3,115},{4,116},{5,117},{6,118},{7,119},{8... | collective-permute-start | bytes 786440 | tf_op jit(solution)/shard_map/ppermute | solution.py:28
  36.7 3.9 %collective-permute-start.15 = (bf16[1024,128]{1,0:T(8,128)(2,1)S(1)}, bf16[1024,128]{1,0:T(8,128)(2,1)S(1)}, u32[]{:S(2)}, u32[]{:S(2)}) collective-permute-start(bf16[1024,128]{1,0:T(8,128)(2,1)S(1)} %add_convert_fusion.1), channel_id=1, source_target_pairs={{0,112},{1,113},{2,114},{3,115},{4,116},{5,117},{6,118},{7,119},{8... | collective-permute-start | bytes 786440 | tf_op jit(solution)/shard_map/ppermute | solution.py:28
  40.8 5.2 %collective-permute-done.10 = bf16[1024,128]{1,0:T(8,128)(2,1)S(1)} collective-permute-done((bf16[1024,128]{1,0:T(8,128)(2,1)S(1)}, bf16[1024,128]{1,0:T(8,128)(2,1)S(1)}, u32[]{:S(2)}, u32[]{:S(2)}) %collective-permute-start.10) | collective-permute-done | bytes 262176 | tf_op jit(solution)/shard_map/ppermute | solution.py:28
  46.2 2.1 %collective-permute-start.17 = (bf16[1024,128]{1,0:T(8,128)(2,1)S(1)}, bf16[1024,128]{1,0:T(8,128)(2,1)S(1)}, u32[]{:S(2)}, u32[]{:S(2)}) collective-permute-start(bf16[1024,128]{1,0:T(8,128)(2,1)S(1)} %add_convert_fusion), channel_id=1, source_target_pairs={{0,240},{1,241},{2,242},{3,243},{4,244},{5,245},{6,246},{7,247},{8... | collective-permute-start | bytes 786440 | tf_op jit(solution)/shard_map/ppermute | solution.py:28
  49.2 5.3 %collective-permute-done.7 = bf16[1024,128]{1,0:T(8,128)(2,1)S(1)} collective-permute-done((bf16[1024,128]{1,0:T(8,128)(2,1)S(1)}, bf16[1024,128]{1,0:T(8,128)(2,1)S(1)}, u32[]{:S(2)}, u32[]{:S(2)}) %collective-permute-start.7) | collective-permute-done | bytes 262176 | tf_op jit(solution)/shard_map/ppermute | solution.py:28
  54.5 2.1 %collective-permute-start.8 = (bf16[1024,128]{1,0:T(8,128)(2,1)S(1)}, bf16[1024,128]{1,0:T(8,128)(2,1)S(1)}, u32[]{:S(2)}, u32[]{:S(2)}) collective-permute-start(bf16[1024,128]{1,0:T(8,128)(2,1)S(1)} %get-tuple-element.57), channel_id=1, source_target_pairs={{0,128},{1,129},{2,130},{3,131},{4,132},{5,133},{6,134},{7,135},{8... | collective-permute-start | bytes 786440 | tf_op jit(solution)/shard_map/ppermute | solution.py:28
  57.3 2.5 %collective-permute-start.18 = (bf16[1024,128]{1,0:T(8,128)(2,1)S(1)}, bf16[1024,128]{1,0:T(8,128)(2,1)S(1)}, u32[]{:S(2)}, u32[]{:S(2)}) collective-permute-start(bf16[1024,128]{1,0:T(8,128)(2,1)S(1)} %fusion), channel_id=1, source_target_pairs={{0,112},{1,113},{2,114},{3,115},{4,116},{5,117},{6,118},{7,119},{8... | collective-permute-start | bytes 786440 | tf_op jit(solution)/shard_map/ppermute | solution.py:28
  59.8 2.8 %collective-permute-done.8 = bf16[1024,128]{1,0:T(8,128)(2,1)S(1)} collective-permute-done((bf16[1024,128]{1,0:T(8,128)(2,1)S(1)}, bf16[1024,128]{1,0:T(8,128)(2,1)S(1)}, u32[]{:S(2)}, u32[]{:S(2)}) %collective-permute-start.8) | collective-permute-done | bytes 262176 | tf_op jit(solution)/shard_map/ppermute | solution.py:28
  62.6 1.9 %collective-permute-done.18 = bf16[1024,128]{1,0:T(8,128)(2,1)S(1)} collective-permute-done((bf16[1024,128]{1,0:T(8,128)(2,1)S(1)}, bf16[1024,128]{1,0:T(8,128)(2,1)S(1)}, u32[]{:S(2)}, u32[]{:S(2)}) %collective-permute-start.18) | collective-permute-done | bytes 262176 | tf_op jit(solution)/shard_map/ppermute | solution.py:28
  64.6 2.8 %collective-permute-done.13 = bf16[1024,128]{1,0:T(8,128)(2,1)S(1)} collective-permute-done((bf16[1024,128]{1,0:T(8,128)(2,1)S(1)}, bf16[1024,128]{1,0:T(8,128)(2,1)S(1)}, u32[]{:S(2)}, u32[]{:S(2)}) %collective-permute-start.13) | collective-permute-done | bytes 262176 | tf_op jit(solution)/shard_map/ppermute | solution.py:28
  67.4 0.9 %add_add_fusion = f32[1024,128]{1,0:T(8,128)} fusion(f32[1024,128]{1,0:T(8,128)S(1)} %copy-done.4, bf16[1024,128]{1,0:T(8,128)(2,1)S(1)} %collective-permute-done.18, bf16[1024,128]{1,0:T(8,128)(2,1)S(1)} %collective-permute-done.13, bf16[1024,128]{1,0:T(8,128)(2,1)S(1)} %collective-permute-done.8, bf16[1024,128]{1,0:T(8,128)(2,1)S(1)} %get-tuple-element.54), kind=kLoop, calls=%fused_computation.5 | loop fusion | flops 1048576 | bytes 2097152 | tf_op jit(solution)/shard_map/add | solution.py:216
  (48 shorter events, 7.4 us)
Async XLA Ops:
  0.6 10.5 %copy-start.3 = (bf16[1,256,256]{2,1,0:T(8,128)(2,1)S(1)}, bf16[1,256,256]{2,1,0:T(8,128)(2,1)}, u32[]{:S(2)}) copy-start(bf16[1,256,256]{2,1,0:T(8,128)(2,1)} %param.7) | copy-start | bytes 393220
  0.6 10.4 %copy-start.5 = (s32[1,8]{1,0:T(1,128)S(1)}, s32[1,8]{1,0:T(1,128)}, u32[]{:S(2)}) copy-start(s32[1,8]{1,0:T(1,128)} %param.9) | copy-start | bytes 100
  0.7 10.4 %copy-start.6 = (s32[1,8]{1,0:T(1,128)S(1)}, s32[1,8]{1,0:T(1,128)}, u32[]{:S(2)}) copy-start(s32[1,8]{1,0:T(1,128)} %param.10) | copy-start | bytes 100
  1.5 4.4 %collective-permute-start = (bf16[128,256]{1,0:T(8,128)(2,1)S(1)}, bf16[128,256]{1,0:T(8,128)(2,1)S(1)}, u32[]{:S(2)}, u32[]{:S(2)}) collective-permute-start(bf16[128,256]{1,0:T(8,128)(2,1)S(1)} %get-tuple-element.69.lead), channel_id=1, source_target_pairs={{0,2},{1,3},{2,0},{3,1},{4,6},{5,7},{6,4},{7,5},{8,10},{9,11},{10,... | collective-permute-start | bytes 196616 | tf_op jit(solution)/shard_map/ppermute | solution.py:28
  5.1 6.0 %copy-start.1 = (bf16[1,1024,2048]{2,1,0:T(8,128)(2,1)S(1)}, bf16[1,1024,2048]{2,1,0:T(8,128)(2,1)}, u32[]{:S(2)}) copy-start(bf16[1,1024,2048]{2,1,0:T(8,128)(2,1)} %param.8) | copy-start | bytes 12582916
  5.9 8.2 %collective-permute-start.3 = (bf16[2,128,256]{2,1,0:T(8,128)(2,1)S(1)}, bf16[2,128,256]{2,1,0:T(8,128)(2,1)S(1)}, u32[]{:S(2)}, u32[]{:S(2)}) collective-permute-start(bf16[2,128,256]{2,1,0:T(8,128)(2,1)S(1)} %pad_maximum_fusion.1), channel_id=1, source_target_pairs={{0,4},{1,5},{2,6},{3,7},{4,8},{5,9},{6,10},{7,11},{8,12},{9,13},{1... | collective-permute-start | bytes 393224 | tf_op jit(solution)/shard_map/ppermute | solution.py:28
  7.5 6.6 %collective-permute-start.2 = (bf16[2,128,256]{2,1,0:T(8,128)(2,1)S(1)}, bf16[2,128,256]{2,1,0:T(8,128)(2,1)S(1)}, u32[]{:S(2)}, u32[]{:S(2)}) collective-permute-start(bf16[2,128,256]{2,1,0:T(8,128)(2,1)S(1)} %pad_maximum_fusion.1), channel_id=1, source_target_pairs={{0,12},{1,13},{2,14},{3,15},{4,0},{5,1},{6,2},{7,3},{8,4},{9,5},{1... | collective-permute-start | bytes 393224 | tf_op jit(solution)/shard_map/ppermute | solution.py:28
  9.2 6.5 %collective-permute-start.1 = (bf16[2,128,256]{2,1,0:T(8,128)(2,1)S(1)}, bf16[2,128,256]{2,1,0:T(8,128)(2,1)S(1)}, u32[]{:S(2)}, u32[]{:S(2)}) collective-permute-start(bf16[2,128,256]{2,1,0:T(8,128)(2,1)S(1)} %pad_maximum_fusion.1), channel_id=1, source_target_pairs={{0,8},{1,9},{2,10},{3,11},{4,12},{5,13},{6,14},{7,15},{8,0},{9,1},... | collective-permute-start | bytes 393224 | tf_op jit(solution)/shard_map/ppermute | solution.py:28
  15.8 2.0 %collective-permute-start.4 = (bf16[8,128,256]{2,1,0:T(8,128)(2,1)S(1)}, bf16[8,128,256]{2,1,0:T(8,128)(2,1)S(1)}, u32[]{:S(2)}, u32[]{:S(2)}) collective-permute-start(bf16[8,128,256]{2,1,0:T(8,128)(2,1)S(1)} %pad_maximum_fusion.own), channel_id=1, source_target_pairs={{0,1},{1,0},{2,3},{3,2},{4,5},{5,4},{6,7},{7,6},{8,9},{9,8},{10,11... | collective-permute-start | bytes 1572872 | tf_op jit(solution)/shard_map/ppermute | solution.py:28
  18.4 12.6 %collective-permute-start.5 = (bf16[1024,128]{1,0:T(8,128)(2,1)S(1)}, bf16[1024,128]{1,0:T(8,128)(2,1)S(1)}, u32[]{:S(2)}, u32[]{:S(2)}) collective-permute-start(bf16[1024,128]{1,0:T(8,128)(2,1)S(1)} %get-tuple-element.52), channel_id=1, source_target_pairs={{0,112},{1,113},{2,114},{3,115},{4,116},{5,117},{6,118},{7,119},{8... | collective-permute-start | bytes 786440 | tf_op jit(solution)/shard_map/ppermute | solution.py:28
  24.3 10.5 %collective-permute-start.9 = (bf16[1024,128]{1,0:T(8,128)(2,1)S(1)}, bf16[1024,128]{1,0:T(8,128)(2,1)S(1)}, u32[]{:S(2)}, u32[]{:S(2)}) collective-permute-start(bf16[1024,128]{1,0:T(8,128)(2,1)S(1)} %get-tuple-element.49.after), channel_id=1, source_target_pairs={{0,16},{1,17},{2,18},{3,19},{4,20},{5,21},{6,22},{7,23},{8,24},{9,... | collective-permute-start | bytes 786440 | tf_op jit(solution)/shard_map/ppermute | solution.py:28
  24.9 11.7 %collective-permute-start.14 = (bf16[1024,128]{1,0:T(8,128)(2,1)S(1)}, bf16[1024,128]{1,0:T(8,128)(2,1)S(1)}, u32[]{:S(2)}, u32[]{:S(2)}) collective-permute-start(bf16[1024,128]{1,0:T(8,128)(2,1)S(1)} %get-tuple-element.66), channel_id=1, source_target_pairs={{0,112},{1,113},{2,114},{3,115},{4,116},{5,117},{6,118},{7,119},{8... | collective-permute-start | bytes 786440 | tf_op jit(solution)/shard_map/ppermute | solution.py:28
  28.2 12.5 %collective-permute-start.6 = (bf16[1024,128]{1,0:T(8,128)(2,1)S(1)}, bf16[1024,128]{1,0:T(8,128)(2,1)S(1)}, u32[]{:S(2)}, u32[]{:S(2)}) collective-permute-start(bf16[1024,128]{1,0:T(8,128)(2,1)S(1)} %get-tuple-element.50.after), channel_id=1, source_target_pairs={{0,16},{1,17},{2,18},{3,19},{4,20},{5,21},{6,22},{7,23},{8,24},{9,... | collective-permute-start | bytes 786440 | tf_op jit(solution)/shard_map/ppermute | solution.py:28
  29.4 27.3 %collective-permute-start.12 = (bf16[2,1024,128]{2,1,0:T(8,128)(2,1)S(1)}, bf16[2,1024,128]{2,1,0:T(8,128)(2,1)S(1)}, u32[]{:S(2)}, u32[]{:S(2)}) collective-permute-start(bf16[2,1024,128]{2,1,0:T(8,128)(2,1)S(1)} %get-tuple-element.61), channel_id=1, source_target_pairs={{0,128},{1,129},{2,130},{3,131},{4,132},{5,133},{6,134},{7,135},{8... | collective-permute-start | bytes 1572872 | tf_op jit(solution)/shard_map/ppermute | solution.py:28
  31.1 15.1 %collective-permute-start.16 = (bf16[1024,128]{1,0:T(8,128)(2,1)S(1)}, bf16[1024,128]{1,0:T(8,128)(2,1)S(1)}, u32[]{:S(2)}, u32[]{:S(2)}) collective-permute-start(bf16[1024,128]{1,0:T(8,128)(2,1)S(1)} %add_convert_fusion.5.after), channel_id=1, source_target_pairs={{0,112},{1,113},{2,114},{3,115},{4,116},{5,117},{6,118},{7,119},{8... | collective-permute-start | bytes 786440 | tf_op jit(solution)/shard_map/ppermute | solution.py:28
  34.9 11.0 %collective-permute-start.10 = (bf16[1024,128]{1,0:T(8,128)(2,1)S(1)}, bf16[1024,128]{1,0:T(8,128)(2,1)S(1)}, u32[]{:S(2)}, u32[]{:S(2)}) collective-permute-start(bf16[1024,128]{1,0:T(8,128)(2,1)S(1)} %add_convert_fusion.3), channel_id=1, source_target_pairs={{0,16},{1,17},{2,18},{3,19},{4,20},{5,21},{6,22},{7,23},{8,24},{9,... | collective-permute-start | bytes 786440 | tf_op jit(solution)/shard_map/ppermute | solution.py:28
  36.7 20.5 %collective-permute-start.15 = (bf16[1024,128]{1,0:T(8,128)(2,1)S(1)}, bf16[1024,128]{1,0:T(8,128)(2,1)S(1)}, u32[]{:S(2)}, u32[]{:S(2)}) collective-permute-start(bf16[1024,128]{1,0:T(8,128)(2,1)S(1)} %add_convert_fusion.1), channel_id=1, source_target_pairs={{0,112},{1,113},{2,114},{3,115},{4,116},{5,117},{6,118},{7,119},{8... | collective-permute-start | bytes 786440 | tf_op jit(solution)/shard_map/ppermute | solution.py:28
  40.7 13.8 %collective-permute-start.7 = (bf16[1024,128]{1,0:T(8,128)(2,1)S(1)}, bf16[1024,128]{1,0:T(8,128)(2,1)S(1)}, u32[]{:S(2)}, u32[]{:S(2)}) collective-permute-start(bf16[1024,128]{1,0:T(8,128)(2,1)S(1)} %add_convert_fusion.4), channel_id=1, source_target_pairs={{0,144},{1,145},{2,146},{3,147},{4,148},{5,149},{6,150},{7,151},{8... | collective-permute-start | bytes 786440 | tf_op jit(solution)/shard_map/ppermute | solution.py:28
  46.0 11.0 %collective-permute-start.11 = (bf16[1024,128]{1,0:T(8,128)(2,1)S(1)}, bf16[1024,128]{1,0:T(8,128)(2,1)S(1)}, u32[]{:S(2)}, u32[]{:S(2)}) collective-permute-start(bf16[1024,128]{1,0:T(8,128)(2,1)S(1)} %add_convert_fusion.2), channel_id=1, source_target_pairs={{0,16},{1,17},{2,18},{3,19},{4,20},{5,21},{6,22},{7,23},{8,24},{9,... | collective-permute-start | bytes 786440 | tf_op jit(solution)/shard_map/ppermute | solution.py:28
  46.2 21.2 %copy-start.4 = (f32[1024,128]{1,0:T(8,128)S(1)}, f32[1024,128]{1,0:T(8,128)}, u32[]{:S(2)}) copy-start(f32[1024,128]{1,0:T(8,128)} %param.11) | copy-start | bytes 1572868
  46.2 10.9 %collective-permute-start.17 = (bf16[1024,128]{1,0:T(8,128)(2,1)S(1)}, bf16[1024,128]{1,0:T(8,128)(2,1)S(1)}, u32[]{:S(2)}, u32[]{:S(2)}) collective-permute-start(bf16[1024,128]{1,0:T(8,128)(2,1)S(1)} %add_convert_fusion), channel_id=1, source_target_pairs={{0,240},{1,241},{2,242},{3,243},{4,244},{5,245},{6,246},{7,247},{8... | collective-permute-start | bytes 786440 | tf_op jit(solution)/shard_map/ppermute | solution.py:28
  54.5 8.1 %collective-permute-start.8 = (bf16[1024,128]{1,0:T(8,128)(2,1)S(1)}, bf16[1024,128]{1,0:T(8,128)(2,1)S(1)}, u32[]{:S(2)}, u32[]{:S(2)}) collective-permute-start(bf16[1024,128]{1,0:T(8,128)(2,1)S(1)} %get-tuple-element.57), channel_id=1, source_target_pairs={{0,128},{1,129},{2,130},{3,131},{4,132},{5,133},{6,134},{7,135},{8... | collective-permute-start | bytes 786440 | tf_op jit(solution)/shard_map/ppermute | solution.py:28
  57.3 7.3 %collective-permute-start.18 = (bf16[1024,128]{1,0:T(8,128)(2,1)S(1)}, bf16[1024,128]{1,0:T(8,128)(2,1)S(1)}, u32[]{:S(2)}, u32[]{:S(2)}) collective-permute-start(bf16[1024,128]{1,0:T(8,128)(2,1)S(1)} %fusion), channel_id=1, source_target_pairs={{0,112},{1,113},{2,114},{3,115},{4,116},{5,117},{6,118},{7,119},{8... | collective-permute-start | bytes 786440 | tf_op jit(solution)/shard_map/ppermute | solution.py:28
  59.8 7.6 %collective-permute-start.13 = (bf16[1024,128]{1,0:T(8,128)(2,1)S(1)}, bf16[1024,128]{1,0:T(8,128)(2,1)S(1)}, u32[]{:S(2)}, u32[]{:S(2)}) collective-permute-start(bf16[1024,128]{1,0:T(8,128)(2,1)S(1)} %fusion.1), channel_id=1, source_target_pairs={{0,16},{1,17},{2,18},{3,19},{4,20},{5,21},{6,22},{7,23},{8,24},{9,... | collective-permute-start | bytes 786440 | tf_op jit(solution)/shard_map/ppermute | solution.py:28
  (2 other events, 3.2 us)

commit v5 on v4

--- a/solution.py
+++ b/solution.py
@@ -53,26 +53,36 @@
     return ((leaf // 8) ^ other) * 8 + (leaf + step + 8) % 8
 
 
-def window_slot(step, other):
-    tile = destination(step, other)
+def window_piece(tile, head, rest, far):
     panel = position()[1]
+    core = panel % 2
     ahead = (tile // 4 - panel // 4 + 4) % 4
-    slot = jnp.where(ahead == 0, 0, jnp.where(ahead == 2, 1, jnp.where(ahead == 1, 2, 3)))
-    return slot * 2 + ((tile // 2) % 2 ^ (panel // 2) % 2)
+    low = (tile // 2) % 2 ^ (panel // 2) % 2
+    mine = (tile % 2) == core
+    holder = jnp.where(ahead == 0, tile % 2, jnp.where(ahead == 1, 1 - low, low))
+    first = jnp.where(ahead == 2, 3, 1 + 4 * low)
+    place_in = jnp.where(ahead == 0, 0, first + jnp.where(tile % 2 == holder, 0, 1))
+    received = jnp.where(holder == core, rest[place_in], far[place_in])
+    return jnp.where((ahead == 0) & (low == 0), head[jnp.where(mine, 0, 1)], received)
+
+
+def gather_window(lead, head):
+    beside = place(lead, lambda y, z, x, low, core: (y, z, x, 1 - low, core))
+    sides = place(head, lambda y, z, x, low, core: (y, z, x + 1 - 2 * core, low, core))
+    opposite = place(head, lambda y, z, x, low, core: (y, z, x + 2, low ^ core, core))
+    corners = place(head, lambda y, z, x, low, core: (y, z, x - 1 + 2 * core, 1 - low, core))
+    return jnp.concatenate([beside[None], sides, opposite, corners])
 
 
 def contributions(items, out_shapes, prepared, window, after):
-    def body(factor, trailing, limits, inverse, own, far, after, *outs):
-        core = position()[1] % 2
+    def body(factor, trailing, limits, inverse, head, rest, far, after, *outs):
         for first in range(0, len(items), 2):
             group = items[first : first + 2]
             tiles = [destination(step, other) for step, other, _, _ in group]
             columns = [pl.ds(pl.multiple_of(tile * TILE, TILE), TILE) for tile in tiles]
             weights = []
-            for tile, (step, other, _, _) in zip(tiles, group):
-                mine = (tile % 2) == core
-                slot = window_slot(step, other)
-                rows = jnp.where(mine, own[slot], far[slot])
+            for tile in tiles:
+                rows = window_piece(tile, head, rest, far)
                 weights.append(
                     lax.dot_general(
                         rows, inverse[...], (((1,), (1,)), ((), ())), preferred_element_type=F32
@@ -97,7 +107,7 @@
     return pl.pallas_call(
         body,
         out_shape=[jax.ShapeDtypeStruct(shape, BF16) for shape in out_shapes],
-        in_specs=[here] * 7,
+        in_specs=[here] * 8,
         out_specs=[here] * len(out_shapes),
         compiler_params=pltpu.CompilerParams(vmem_limit_bytes=VMEM_LIMIT),
         cost_estimate=pl.CostEstimate(
@@ -108,51 +118,48 @@
     )(*prepared, *window, after)
 
 
-def prepare_kernel(maps, a21, inverse, trailing, out, factor, ordered, limits, kept):
+def order_kernel(maps, trailing, ordered, limits):
+    for t in range(TILES_DEV):
+        target = pl.ds(pl.multiple_of(maps[0, t] * TILE, TILE), TILE)
+        ordered[target, :] = trailing[t * TILE : (t + 1) * TILE, :]
+        limits[pl.ds(maps[0, t], 1), :] = jnp.full((1, TILE), maps[0, TILES_DEV + t], jnp.int32)
+
+
+def solve_kernel(maps, a21, inverse, out, factor, kept):
     out[...] = lax.dot_general(
         a21[...], inverse[...], (((1,), (1,)), ((), ())), preferred_element_type=F32
     ).astype(BF16)
     kept[...] = inverse[...]
     for t in range(TILES_DEV):
-        rows = slice(t * TILE, (t + 1) * TILE)
         target = pl.ds(pl.multiple_of(maps[0, t] * TILE, TILE), TILE)
-        factor[target, :] = out[rows, :]
-        ordered[target, :] = trailing[rows, :]
-        limits[pl.ds(maps[0, t], 1), :] = jnp.full((1, TILE), maps[0, TILES_DEV + t], jnp.int32)
-
-
-def prepare(maps, a21, inverse, trailing):
+        factor[target, :] = out[t * TILE : (t + 1) * TILE, :]
+
+
+def in_vmem(kernel, flops, out_shape, maps, *operands):
     here = pl.BlockSpec(memory_space=pltpu.VMEM)
-    like = [jax.ShapeDtypeStruct(value.shape, BF16) for value in (a21, a21, trailing)]
     return pl.pallas_call(
-        prepare_kernel,
-        out_shape=like
-        + [
-            jax.ShapeDtypeStruct((TILES_DEV, TILE), jnp.int32),
-            jax.ShapeDtypeStruct(inverse.shape, BF16),
-        ],
-        in_specs=[pl.BlockSpec(memory_space=pltpu.SMEM)] + [here] * 3,
-        out_specs=[here] * 5,
+        kernel,
+        out_shape=out_shape,
+        in_specs=[pl.BlockSpec(memory_space=pltpu.SMEM)] + [here] * len(operands),
+        out_specs=[here] * len(out_shape),
         compiler_params=pltpu.CompilerParams(vmem_limit_bytes=VMEM_LIMIT),
         cost_estimate=pl.CostEstimate(
-            flops=2 * ROWS_DEV * PW * PW, bytes_accessed=8 * 1024 * 1024, transcendentals=0
+            flops=flops, bytes_accessed=4 * 1024 * 1024, transcendentals=0
         ),
-    )(maps, a21, inverse, trailing)
-
-
-def bring_kernel(trailing, lead, out):
-    out[...] = trailing[:TILE, :TILE] + lead[:, :TILE]
-
-
-def bring(trailing, lead):
-    here = pl.BlockSpec(memory_space=pltpu.VMEM)
-    return pl.pallas_call(
-        bring_kernel,
-        out_shape=jax.ShapeDtypeStruct((TILE, TILE), BF16),
-        in_specs=[here] * 2,
-        out_specs=here,
-        compiler_params=pltpu.CompilerParams(vmem_limit_bytes=VMEM_LIMIT),
-    )(trailing, lead)
+    )(maps, *operands)
+
+
+def order(maps, trailing):
+    shapes = [
+        jax.ShapeDtypeStruct(trailing.shape, BF16),
+        jax.ShapeDtypeStruct((TILES_DEV, TILE), jnp.int32),
+    ]
+    return in_vmem(order_kernel, 0, shapes, maps, trailing)
+
+
+def solve(maps, a21, inverse):
+    shapes = [jax.ShapeDtypeStruct(value.shape, BF16) for value in (a21, a21, inverse)]
+    return in_vmem(solve_kernel, 2 * ROWS_DEV * PW * PW, shapes, maps, a21, inverse)
 
 
 def add(*terms):
@@ -165,19 +172,14 @@
 def on_device(a21, l11_inv, a22, tasks, emap, parent_in):
     a21, l11_inv, a22 = a21[0], l11_inv[0], a22[0]
     lead = a21[:TILE]
-    pair = jnp.stack([lead, place(lead, lambda y, z, x, low, core: (y, z, x, 1 - low, core))])
-    pair, brought, a21, l11_inv = lax.optimization_barrier((pair, bring(a22, lead), a21, l11_inv))
-    own = jnp.concatenate(
-        [pair]
-        + [
-            place(pair, lambda y, z, x, low, core, dx=dx: (y, z, x + dx, low, core))
-            for dx in (2, -1, 1)
-        ]
-    )
     maps = jnp.concatenate([emap, tasks], axis=1)
-    l21, *prepared = prepare(maps, a21, l11_inv, a22)
-    own, prepared = lax.optimization_barrier((own, prepared))
-    window = (own, to_sibling(own))
+    head, maps, a22 = lax.optimization_barrier((jnp.stack([lead, to_sibling(lead)]), maps, a22))
+    rest = gather_window(lead, head)
+    ordered, limits = order(maps, a22)
+    rest, ordered, a21, l11_inv = lax.optimization_barrier((rest, ordered, a21, l11_inv))
+    l21, factor, inverse = solve(maps, a21, l11_inv)
+    prepared = factor, ordered, limits, inverse
+    window = (head, rest, to_sibling(rest))
 
     def run(items, shapes, after):
         return contributions(items, shapes, prepared, window, after)
@@ -186,7 +188,7 @@
     def bf16(*terms):
         return add(*terms).astype(BF16)
 
-    far, far_y = run([(4, 0, 0, ()), (4, 1, 1, ())], [one, one], brought)
+    far, far_y = run([(4, 0, 0, ()), (4, 1, 1, ())], [one, one], prepared[0])
     up4, down4_y = along(far, 1), along(far_y, -1)
     next_y, next_ = run([(3, 1, 0, ()), (-3, 0, 1, ())], [one, one], far)
     up3_y, down3 = along(next_y, 1), along(next_, -1)

time: 68.5 us -> 66.8 us (0.975)
  the two profiles are of different devices: /device:TPU:16 before, /device:TPU:6 now
where the time goes in v5:
time: 66.8 us; the launch traced here: 65.9 us
  starting transfers between devices  37.3 us (56%)
  waiting for transfers between devices  15.8 us (24%)
  Pallas kernels  6.46 us (10%)
  local copies, waits for them, and re-layouts  3.09 us (5%)
  other arithmetic  2.48 us (4%)
  between operations  0.81 us (1%)
    ppermute x20, starting transfers between devices, place(): return lax.ppermute(value, AXES, pairs)  37.3 us
    ppermute x20, waiting for transfers between devices, place(): return lax.ppermute(value, AXES, pairs)  15.8 us
    pallas_call x5, Pallas kernels, contributions(): pl.pallas_call(body, out_shape=[jax.ShapeDtypeStruct(shape, BF16) for sha...  3.98 us
    pallas_call x2, Pallas kernels, in_vmem(): pl.pallas_call(kernel, out_shape=out_shape, in_specs=[pl.BlockSpec(memory...  2.48 us
    unnamed x8, local copies, waits for them, and re-layouts  2.2 us
  transfers between devices with their start and end apart: 20, of which 8 were waited for; matrix products, arithmetic and copies ran while one was open for 2% of the time, Pallas kernels for 9%

profile of v5, /device:TPU:6, one launch (start us, length us, event | category | flops | bytes accessed | tf_op | source)
XLA Modules:
  0.0 65.9 jit_solution(14291449093522114055)
XLA Ops:
  2.9 1.9 %collective-permute-start.4 = (bf16[2,128,256]{2,1,0:T(8,128)(2,1)S(1)}, bf16[2,128,256]{2,1,0:T(8,128)(2,1)S(1)}, u32[]{:S(2)}, u32[]{:S(2)}) collective-permute-start(bf16[2,128,256]{2,1,0:T(8,128)(2,1)S(1)} %pad_maximum_fusion.1.head), channel_id=1, source_target_pairs={{0,14},{1,7},{2,12},{3,5},{4,2},{5,11},{6,0},{7,9},{8,6},{9,15},{1... | collective-permute-start | bytes 393224 | tf_op jit(solution)/shard_map/ppermute | solution.py:28
  4.8 1.1 %collective-permute-start.3 = (bf16[2,128,256]{2,1,0:T(8,128)(2,1)S(1)}, bf16[2,128,256]{2,1,0:T(8,128)(2,1)S(1)}, u32[]{:S(2)}, u32[]{:S(2)}) collective-permute-start(bf16[2,128,256]{2,1,0:T(8,128)(2,1)S(1)} %pad_maximum_fusion.1.head), channel_id=1, source_target_pairs={{0,8},{1,11},{2,10},{3,9},{4,12},{5,15},{6,14},{7,13},{8,0},{9,3},... | collective-permute-start | bytes 393224 | tf_op jit(solution)/shard_map/ppermute | solution.py:28
  5.9 2.1 %collective-permute-start.2 = (bf16[2,128,256]{2,1,0:T(8,128)(2,1)S(1)}, bf16[2,128,256]{2,1,0:T(8,128)(2,1)S(1)}, u32[]{:S(2)}, u32[]{:S(2)}) collective-permute-start(bf16[2,128,256]{2,1,0:T(8,128)(2,1)S(1)} %pad_maximum_fusion.1.head), channel_id=1, source_target_pairs={{0,4},{1,13},{2,6},{3,15},{4,8},{5,1},{6,10},{7,3},{8,12},{9,5},{1... | collective-permute-start | bytes 393224 | tf_op jit(solution)/shard_map/ppermute | solution.py:28
  8.5 2.2 %copy-done = bf16[1,1024,2048]{2,1,0:T(8,128)(2,1)S(1)} copy-done((bf16[1,1024,2048]{2,1,0:T(8,128)(2,1)S(1)}, bf16[1,1024,2048]{2,1,0:T(8,128)(2,1)}, u32[]{:S(2)}) %copy-start) | copy-done | bytes 4194328
  11.5 1.4 %collective-permute-done.1 = bf16[128,256]{1,0:T(8,128)(2,1)S(1)} collective-permute-done((bf16[128,256]{1,0:T(8,128)(2,1)S(1)}, bf16[128,256]{1,0:T(8,128)(2,1)S(1)}, u32[]{:S(2)}, u32[]{:S(2)}) %collective-permute-start.1) | collective-permute-done | bytes 65568 | tf_op jit(solution)/shard_map/ppermute | solution.py:28
  12.9 1.4 %collective-permute-start.5 = (bf16[7,128,256]{2,1,0:T(8,128)(2,1)S(1)}, bf16[7,128,256]{2,1,0:T(8,128)(2,1)S(1)}, u32[]{:S(2)}, u32[]{:S(2)}) collective-permute-start(bf16[7,128,256]{2,1,0:T(8,128)(2,1)S(1)} %pad_maximum_fusion.rest), channel_id=1, source_target_pairs={{0,1},{1,0},{2,3},{3,2},{4,5},{5,4},{6,7},{7,6},{8,9},{9,8},{10,11... | collective-permute-start | bytes 1376264 | tf_op jit(solution)/shard_map/ppermute | solution.py:28
  14.3 1.7 %shard_map.78 = (bf16[1024,256]{1,0:T(8,128)(2,1)}, bf16[1024,256]{1,0:T(8,128)(2,1)S(1)}, bf16[256,256]{1,0:T(8,128)(2,1)S(1)}) custom-call(s32[1,16]{1,0:T(1,128)S(1)} %pad_add_fusion.maps, bf16[1024,256]{1,0:T(8,128)(2,1)S(1)} %bitcast.19, bf16[256,256]{1,0:T(8,128)(2,1)S(1)} %bitcast.20), custom_call_target="tpu_custom_call" | custom-call | flops 134217728 | bytes 4194304 | tf_op jit(solution)/shard_map/pallas_call | solution.py:140
  16.5 5.7 %collective-permute-start.6 = (bf16[1024,128]{1,0:T(8,128)(2,1)S(1)}, bf16[1024,128]{1,0:T(8,128)(2,1)S(1)}, u32[]{:S(2)}, u32[]{:S(2)}) collective-permute-start(bf16[1024,128]{1,0:T(8,128)(2,1)S(1)} %get-tuple-element.48), channel_id=1, source_target_pairs={{0,112},{1,113},{2,114},{3,115},{4,116},{5,117},{6,118},{7,119},{8... | collective-permute-start | bytes 786440 | tf_op jit(solution)/shard_map/ppermute | solution.py:28
  22.8 3.3 %collective-permute-start.15 = (bf16[1024,128]{1,0:T(8,128)(2,1)S(1)}, bf16[1024,128]{1,0:T(8,128)(2,1)S(1)}, u32[]{:S(2)}, u32[]{:S(2)}) collective-permute-start(bf16[1024,128]{1,0:T(8,128)(2,1)S(1)} %get-tuple-element.62), channel_id=1, source_target_pairs={{0,112},{1,113},{2,114},{3,115},{4,116},{5,117},{6,118},{7,119},{8... | collective-permute-start | bytes 786440 | tf_op jit(solution)/shard_map/ppermute | solution.py:28
  26.1 1.2 %shard_map.81 = (bf16[2,1024,128]{2,1,0:T(8,128)(2,1)S(1)}, bf16[1024,128]{1,0:T(8,128)(2,1)S(1)}, bf16[1024,128]{1,0:T(8,128)(2,1)S(1)}, bf16[1024,128]{1,0:T(8,128)(2,1)S(1)}) custom-call(bf16[1024,256]{1,0:T(8,128)(2,1)S(1)} %get-tuple-element.40.factor.after, bf16[1024,2048]{1,0:T(8,128)(2,1)S(1)} %get-tuple-element.41.trailing, ...), custom_call_target="tpu_custom_call" | custom-call | flops 335544320 | bytes 3145728 | tf_op jit(solution)/shard_map/pallas_call | solution.py:107
  27.3 3.2 %collective-permute-start.13 = (bf16[2,1024,128]{2,1,0:T(8,128)(2,1)S(1)}, bf16[2,1024,128]{2,1,0:T(8,128)(2,1)S(1)}, u32[]{:S(2)}, u32[]{:S(2)}) collective-permute-start(bf16[2,1024,128]{2,1,0:T(8,128)(2,1)S(1)} %get-tuple-element.57), channel_id=1, source_target_pairs={{0,128},{1,129},{2,130},{3,131},{4,132},{5,133},{6,134},{7,135},{8... | collective-permute-start | bytes 1572872 | tf_op jit(solution)/shard_map/ppermute | solution.py:28
  30.6 3.3 %collective-permute-start.17 = (bf16[1024,128]{1,0:T(8,128)(2,1)S(1)}, bf16[1024,128]{1,0:T(8,128)(2,1)S(1)}, u32[]{:S(2)}, u32[]{:S(2)}) collective-permute-start(bf16[1024,128]{1,0:T(8,128)(2,1)S(1)} %add_convert_fusion.5.after), channel_id=1, source_target_pairs={{0,112},{1,113},{2,114},{3,115},{4,116},{5,117},{6,118},{7,119},{8... | collective-permute-start | bytes 786440 | tf_op jit(solution)/shard_map/ppermute | solution.py:28
  35.0 3.5 %collective-permute-start.16 = (bf16[1024,128]{1,0:T(8,128)(2,1)S(1)}, bf16[1024,128]{1,0:T(8,128)(2,1)S(1)}, u32[]{:S(2)}, u32[]{:S(2)}) collective-permute-start(bf16[1024,128]{1,0:T(8,128)(2,1)S(1)} %add_convert_fusion.1), channel_id=1, source_target_pairs={{0,112},{1,113},{2,114},{3,115},{4,116},{5,117},{6,118},{7,119},{8... | collective-permute-start | bytes 786440 | tf_op jit(solution)/shard_map/ppermute | solution.py:28
  38.6 1.0 %collective-permute-start.8 = (bf16[1024,128]{1,0:T(8,128)(2,1)S(1)}, bf16[1024,128]{1,0:T(8,128)(2,1)S(1)}, u32[]{:S(2)}, u32[]{:S(2)}) collective-permute-start(bf16[1024,128]{1,0:T(8,128)(2,1)S(1)} %add_convert_fusion.4), channel_id=1, source_target_pairs={{0,144},{1,145},{2,146},{3,147},{4,148},{5,149},{6,150},{7,151},{8... | collective-permute-start | bytes 786440 | tf_op jit(solution)/shard_map/ppermute | solution.py:28
  39.7 3.1 %collective-permute-done.11 = bf16[1024,128]{1,0:T(8,128)(2,1)S(1)} collective-permute-done((bf16[1024,128]{1,0:T(8,128)(2,1)S(1)}, bf16[1024,128]{1,0:T(8,128)(2,1)S(1)}, u32[]{:S(2)}, u32[]{:S(2)}) %collective-permute-start.11) | collective-permute-done | bytes 262176 | tf_op jit(solution)/shard_map/ppermute | solution.py:28
  43.1 6.9 %collective-permute-start.18 = (bf16[1024,128]{1,0:T(8,128)(2,1)S(1)}, bf16[1024,128]{1,0:T(8,128)(2,1)S(1)}, u32[]{:S(2)}, u32[]{:S(2)}) collective-permute-start(bf16[1024,128]{1,0:T(8,128)(2,1)S(1)} %add_convert_fusion), channel_id=1, source_target_pairs={{0,240},{1,241},{2,242},{3,243},{4,244},{5,245},{6,246},{7,247},{8... | collective-permute-start | bytes 786440 | tf_op jit(solution)/shard_map/ppermute | solution.py:28
  50.8 3.7 %collective-permute-done.8 = bf16[1024,128]{1,0:T(8,128)(2,1)S(1)} collective-permute-done((bf16[1024,128]{1,0:T(8,128)(2,1)S(1)}, bf16[1024,128]{1,0:T(8,128)(2,1)S(1)}, u32[]{:S(2)}, u32[]{:S(2)}) %collective-permute-start.8) | collective-permute-done | bytes 262176 | tf_op jit(solution)/shard_map/ppermute | solution.py:28
  54.5 1.0 %collective-permute-start.9 = (bf16[1024,128]{1,0:T(8,128)(2,1)S(1)}, bf16[1024,128]{1,0:T(8,128)(2,1)S(1)}, u32[]{:S(2)}, u32[]{:S(2)}) collective-permute-start(bf16[1024,128]{1,0:T(8,128)(2,1)S(1)} %get-tuple-element.53), channel_id=1, source_target_pairs={{0,128},{1,129},{2,130},{3,131},{4,132},{5,133},{6,134},{7,135},{8... | collective-permute-start | bytes 786440 | tf_op jit(solution)/shard_map/ppermute | solution.py:28
  55.7 1.1 %collective-permute-done.18 = bf16[1024,128]{1,0:T(8,128)(2,1)S(1)} collective-permute-done((bf16[1024,128]{1,0:T(8,128)(2,1)S(1)}, bf16[1024,128]{1,0:T(8,128)(2,1)S(1)}, u32[]{:S(2)}, u32[]{:S(2)}) %collective-permute-start.18) | collective-permute-done | bytes 262176 | tf_op jit(solution)/shard_map/ppermute | solution.py:28
  57.4 1.6 %collective-permute-start.14 = (bf16[1024,128]{1,0:T(8,128)(2,1)S(1)}, bf16[1024,128]{1,0:T(8,128)(2,1)S(1)}, u32[]{:S(2)}, u32[]{:S(2)}) collective-permute-start(bf16[1024,128]{1,0:T(8,128)(2,1)S(1)} %fusion.1), channel_id=1, source_target_pairs={{0,16},{1,17},{2,18},{3,19},{4,20},{5,21},{6,22},{7,23},{8,24},{9,... | collective-permute-start | bytes 786440 | tf_op jit(solution)/shard_map/ppermute | solution.py:28
  59.0 3.5 %collective-permute-done.9 = bf16[1024,128]{1,0:T(8,128)(2,1)S(1)} collective-permute-done((bf16[1024,128]{1,0:T(8,128)(2,1)S(1)}, bf16[1024,128]{1,0:T(8,128)(2,1)S(1)}, u32[]{:S(2)}, u32[]{:S(2)}) %collective-permute-start.9) | collective-permute-done | bytes 262176 | tf_op jit(solution)/shard_map/ppermute | solution.py:28
  62.5 0.9 %collective-permute-done.19 = bf16[1024,128]{1,0:T(8,128)(2,1)S(1)} collective-permute-done((bf16[1024,128]{1,0:T(8,128)(2,1)S(1)}, bf16[1024,128]{1,0:T(8,128)(2,1)S(1)}, u32[]{:S(2)}, u32[]{:S(2)}) %collective-permute-start.19) | collective-permute-done | bytes 262176 | tf_op jit(solution)/shard_map/ppermute | solution.py:28
  63.3 1.6 %collective-permute-done.14 = bf16[1024,128]{1,0:T(8,128)(2,1)S(1)} collective-permute-done((bf16[1024,128]{1,0:T(8,128)(2,1)S(1)}, bf16[1024,128]{1,0:T(8,128)(2,1)S(1)}, u32[]{:S(2)}, u32[]{:S(2)}) %collective-permute-start.14) | collective-permute-done | bytes 262176 | tf_op jit(solution)/shard_map/ppermute | solution.py:28
  64.9 0.9 %add_add_fusion = f32[1024,128]{1,0:T(8,128)} fusion(f32[1024,128]{1,0:T(8,128)S(1)} %copy-done.3, bf16[1024,128]{1,0:T(8,128)(2,1)S(1)} %collective-permute-done.19, bf16[1024,128]{1,0:T(8,128)(2,1)S(1)} %collective-permute-done.14, bf16[1024,128]{1,0:T(8,128)(2,1)S(1)} %collective-permute-done.9, bf16[1024,128]{1,0:T(8,128)(2,1)S(1)} %get-tuple-element.50), kind=kLoop, calls=%fused_computation.4 | loop fusion | flops 1048576 | bytes 2097152 | tf_op jit(solution)/shard_map/add | solution.py:218
  (44 shorter events, 7.7 us)
Async XLA Ops:
  0.6 13.7 %copy-start.2 = (bf16[1,256,256]{2,1,0:T(8,128)(2,1)S(1)}, bf16[1,256,256]{2,1,0:T(8,128)(2,1)}, u32[]{:S(2)}) copy-start(bf16[1,256,256]{2,1,0:T(8,128)(2,1)} %param.7) | copy-start | bytes 393220
  1.5 1.3 %collective-permute-start = (bf16[128,256]{1,0:T(8,128)(2,1)S(1)}, bf16[128,256]{1,0:T(8,128)(2,1)S(1)}, u32[]{:S(2)}, u32[]{:S(2)}) collective-permute-start(bf16[128,256]{1,0:T(8,128)(2,1)S(1)} %get-tuple-element.65), channel_id=1, source_target_pairs={{0,1},{1,0},{2,3},{3,2},{4,5},{5,4},{6,7},{7,6},{8,9},{9,8},{10,11... | collective-permute-start | bytes 196616 | tf_op jit(solution)/shard_map/ppermute | solution.py:28
  2.9 10.0 %collective-permute-start.4 = (bf16[2,128,256]{2,1,0:T(8,128)(2,1)S(1)}, bf16[2,128,256]{2,1,0:T(8,128)(2,1)S(1)}, u32[]{:S(2)}, u32[]{:S(2)}) collective-permute-start(bf16[2,128,256]{2,1,0:T(8,128)(2,1)S(1)} %pad_maximum_fusion.1.head), channel_id=1, source_target_pairs={{0,14},{1,7},{2,12},{3,5},{4,2},{5,11},{6,0},{7,9},{8,6},{9,15},{1... | collective-permute-start | bytes 393224 | tf_op jit(solution)/shard_map/ppermute | solution.py:28
  4.8 8.1 %collective-permute-start.3 = (bf16[2,128,256]{2,1,0:T(8,128)(2,1)S(1)}, bf16[2,128,256]{2,1,0:T(8,128)(2,1)S(1)}, u32[]{:S(2)}, u32[]{:S(2)}) collective-permute-start(bf16[2,128,256]{2,1,0:T(8,128)(2,1)S(1)} %pad_maximum_fusion.1.head), channel_id=1, source_target_pairs={{0,8},{1,11},{2,10},{3,9},{4,12},{5,15},{6,14},{7,13},{8,0},{9,3},... | collective-permute-start | bytes 393224 | tf_op jit(solution)/shard_map/ppermute | solution.py:28
  5.9 6.9 %collective-permute-start.2 = (bf16[2,128,256]{2,1,0:T(8,128)(2,1)S(1)}, bf16[2,128,256]{2,1,0:T(8,128)(2,1)S(1)}, u32[]{:S(2)}, u32[]{:S(2)}) collective-permute-start(bf16[2,128,256]{2,1,0:T(8,128)(2,1)S(1)} %pad_maximum_fusion.1.head), channel_id=1, source_target_pairs={{0,4},{1,13},{2,6},{3,15},{4,8},{5,1},{6,10},{7,3},{8,12},{9,5},{1... | collective-permute-start | bytes 393224 | tf_op jit(solution)/shard_map/ppermute | solution.py:28
  8.0 4.8 %collective-permute-start.1 = (bf16[128,256]{1,0:T(8,128)(2,1)S(1)}, bf16[128,256]{1,0:T(8,128)(2,1)S(1)}, u32[]{:S(2)}, u32[]{:S(2)}) collective-permute-start(bf16[128,256]{1,0:T(8,128)(2,1)S(1)} %get-tuple-element.65), channel_id=1, source_target_pairs={{0,2},{1,3},{2,0},{3,1},{4,6},{5,7},{6,4},{7,5},{8,10},{9,11},{10,... | collective-permute-start | bytes 196616 | tf_op jit(solution)/shard_map/ppermute | solution.py:28
  8.5 2.2 %copy-start = (bf16[1,1024,2048]{2,1,0:T(8,128)(2,1)S(1)}, bf16[1,1024,2048]{2,1,0:T(8,128)(2,1)}, u32[]{:S(2)}) copy-start(bf16[1,1024,2048]{2,1,0:T(8,128)(2,1)} %param.8) | copy-start | bytes 12582916
  10.7 3.7 %copy-start.1 = (bf16[1,1024,256]{2,1,0:T(8,128)(2,1)S(1)}, bf16[1,1024,256]{2,1,0:T(8,128)(2,1)}, u32[]{:S(2)}) copy-start(bf16[1,1024,256]{2,1,0:T(8,128)(2,1)} %param.6) | copy-start | bytes 1572868
  12.9 3.1 %collective-permute-start.5 = (bf16[7,128,256]{2,1,0:T(8,128)(2,1)S(1)}, bf16[7,128,256]{2,1,0:T(8,128)(2,1)S(1)}, u32[]{:S(2)}, u32[]{:S(2)}) collective-permute-start(bf16[7,128,256]{2,1,0:T(8,128)(2,1)S(1)} %pad_maximum_fusion.rest), channel_id=1, source_target_pairs={{0,1},{1,0},{2,3},{3,2},{4,5},{5,4},{6,7},{7,6},{8,9},{9,8},{10,11... | collective-permute-start | bytes 1376264 | tf_op jit(solution)/shard_map/ppermute | solution.py:28
  16.5 14.0 %collective-permute-start.6 = (bf16[1024,128]{1,0:T(8,128)(2,1)S(1)}, bf16[1024,128]{1,0:T(8,128)(2,1)S(1)}, u32[]{:S(2)}, u32[]{:S(2)}) collective-permute-start(bf16[1024,128]{1,0:T(8,128)(2,1)S(1)} %get-tuple-element.48), channel_id=1, source_target_pairs={{0,112},{1,113},{2,114},{3,115},{4,116},{5,117},{6,118},{7,119},{8... | collective-permute-start | bytes 786440 | tf_op jit(solution)/shard_map/ppermute | solution.py:28
  22.3 11.6 %collective-permute-start.10 = (bf16[1024,128]{1,0:T(8,128)(2,1)S(1)}, bf16[1024,128]{1,0:T(8,128)(2,1)S(1)}, u32[]{:S(2)}, u32[]{:S(2)}) collective-permute-start(bf16[1024,128]{1,0:T(8,128)(2,1)S(1)} %get-tuple-element.45.after), channel_id=1, source_target_pairs={{0,16},{1,17},{2,18},{3,19},{4,20},{5,21},{6,22},{7,23},{8,24},{9,... | collective-permute-start | bytes 786440 | tf_op jit(solution)/shard_map/ppermute | solution.py:28
  22.8 12.1 %collective-permute-start.15 = (bf16[1024,128]{1,0:T(8,128)(2,1)S(1)}, bf16[1024,128]{1,0:T(8,128)(2,1)S(1)}, u32[]{:S(2)}, u32[]{:S(2)}) collective-permute-start(bf16[1024,128]{1,0:T(8,128)(2,1)S(1)} %get-tuple-element.62), channel_id=1, source_target_pairs={{0,112},{1,113},{2,114},{3,115},{4,116},{5,117},{6,118},{7,119},{8... | collective-permute-start | bytes 786440 | tf_op jit(solution)/shard_map/ppermute | solution.py:28
  26.1 12.5 %collective-permute-start.7 = (bf16[1024,128]{1,0:T(8,128)(2,1)S(1)}, bf16[1024,128]{1,0:T(8,128)(2,1)S(1)}, u32[]{:S(2)}, u32[]{:S(2)}) collective-permute-start(bf16[1024,128]{1,0:T(8,128)(2,1)S(1)} %get-tuple-element.46.after), channel_id=1, source_target_pairs={{0,16},{1,17},{2,18},{3,19},{4,20},{5,21},{6,22},{7,23},{8,24},{9,... | collective-permute-start | bytes 786440 | tf_op jit(solution)/shard_map/ppermute | solution.py:28
  27.3 28.2 %collective-permute-start.13 = (bf16[2,1024,128]{2,1,0:T(8,128)(2,1)S(1)}, bf16[2,1024,128]{2,1,0:T(8,128)(2,1)S(1)}, u32[]{:S(2)}, u32[]{:S(2)}) collective-permute-start(bf16[2,1024,128]{2,1,0:T(8,128)(2,1)S(1)} %get-tuple-element.57), channel_id=1, source_target_pairs={{0,128},{1,129},{2,130},{3,131},{4,132},{5,133},{6,134},{7,135},{8... | collective-permute-start | bytes 1572872 | tf_op jit(solution)/shard_map/ppermute | solution.py:28
  30.6 12.4 %collective-permute-start.17 = (bf16[1024,128]{1,0:T(8,128)(2,1)S(1)}, bf16[1024,128]{1,0:T(8,128)(2,1)S(1)}, u32[]{:S(2)}, u32[]{:S(2)}) collective-permute-start(bf16[1024,128]{1,0:T(8,128)(2,1)S(1)} %add_convert_fusion.5.after), channel_id=1, source_target_pairs={{0,112},{1,113},{2,114},{3,115},{4,116},{5,117},{6,118},{7,119},{8... | collective-permute-start | bytes 786440 | tf_op jit(solution)/shard_map/ppermute | solution.py:28
  34.0 8.8 %collective-permute-start.11 = (bf16[1024,128]{1,0:T(8,128)(2,1)S(1)}, bf16[1024,128]{1,0:T(8,128)(2,1)S(1)}, u32[]{:S(2)}, u32[]{:S(2)}) collective-permute-start(bf16[1024,128]{1,0:T(8,128)(2,1)S(1)} %add_convert_fusion.3), channel_id=1, source_target_pairs={{0,16},{1,17},{2,18},{3,19},{4,20},{5,21},{6,22},{7,23},{8,24},{9,... | collective-permute-start | bytes 786440 | tf_op jit(solution)/shard_map/ppermute | solution.py:28
  35.0 20.6 %collective-permute-start.16 = (bf16[1024,128]{1,0:T(8,128)(2,1)S(1)}, bf16[1024,128]{1,0:T(8,128)(2,1)S(1)}, u32[]{:S(2)}, u32[]{:S(2)}) collective-permute-start(bf16[1024,128]{1,0:T(8,128)(2,1)S(1)} %add_convert_fusion.1), channel_id=1, source_target_pairs={{0,112},{1,113},{2,114},{3,115},{4,116},{5,117},{6,118},{7,119},{8... | collective-permute-start | bytes 786440 | tf_op jit(solution)/shard_map/ppermute | solution.py:28
  38.6 15.9 %collective-permute-start.8 = (bf16[1024,128]{1,0:T(8,128)(2,1)S(1)}, bf16[1024,128]{1,0:T(8,128)(2,1)S(1)}, u32[]{:S(2)}, u32[]{:S(2)}) collective-permute-start(bf16[1024,128]{1,0:T(8,128)(2,1)S(1)} %add_convert_fusion.4), channel_id=1, source_target_pairs={{0,144},{1,145},{2,146},{3,147},{4,148},{5,149},{6,150},{7,151},{8... | collective-permute-start | bytes 786440 | tf_op jit(solution)/shard_map/ppermute | solution.py:28
  42.9 12.7 %collective-permute-start.12 = (bf16[1024,128]{1,0:T(8,128)(2,1)S(1)}, bf16[1024,128]{1,0:T(8,128)(2,1)S(1)}, u32[]{:S(2)}, u32[]{:S(2)}) collective-permute-start(bf16[1024,128]{1,0:T(8,128)(2,1)S(1)} %add_convert_fusion.2), channel_id=1, source_target_pairs={{0,16},{1,17},{2,18},{3,19},{4,20},{5,21},{6,22},{7,23},{8,24},{9,... | collective-permute-start | bytes 786440 | tf_op jit(solution)/shard_map/ppermute | solution.py:28
  43.0 21.9 %copy-start.3 = (f32[1024,128]{1,0:T(8,128)S(1)}, f32[1024,128]{1,0:T(8,128)}, u32[]{:S(2)}) copy-start(f32[1024,128]{1,0:T(8,128)} %param.11) | copy-start | bytes 1572868
  43.1 13.7 %collective-permute-start.18 = (bf16[1024,128]{1,0:T(8,128)(2,1)S(1)}, bf16[1024,128]{1,0:T(8,128)(2,1)S(1)}, u32[]{:S(2)}, u32[]{:S(2)}) collective-permute-start(bf16[1024,128]{1,0:T(8,128)(2,1)S(1)} %add_convert_fusion), channel_id=1, source_target_pairs={{0,240},{1,241},{2,242},{3,243},{4,244},{5,245},{6,246},{7,247},{8... | collective-permute-start | bytes 786440 | tf_op jit(solution)/shard_map/ppermute | solution.py:28
  54.5 7.9 %collective-permute-start.9 = (bf16[1024,128]{1,0:T(8,128)(2,1)S(1)}, bf16[1024,128]{1,0:T(8,128)(2,1)S(1)}, u32[]{:S(2)}, u32[]{:S(2)}) collective-permute-start(bf16[1024,128]{1,0:T(8,128)(2,1)S(1)} %get-tuple-element.53), channel_id=1, source_target_pairs={{0,128},{1,129},{2,130},{3,131},{4,132},{5,133},{6,134},{7,135},{8... | collective-permute-start | bytes 786440 | tf_op jit(solution)/shard_map/ppermute | solution.py:28
  56.9 6.5 %collective-permute-start.19 = (bf16[1024,128]{1,0:T(8,128)(2,1)S(1)}, bf16[1024,128]{1,0:T(8,128)(2,1)S(1)}, u32[]{:S(2)}, u32[]{:S(2)}) collective-permute-start(bf16[1024,128]{1,0:T(8,128)(2,1)S(1)} %fusion), channel_id=1, source_target_pairs={{0,112},{1,113},{2,114},{3,115},{4,116},{5,117},{6,118},{7,119},{8... | collective-permute-start | bytes 786440 | tf_op jit(solution)/shard_map/ppermute | solution.py:28
  57.4 7.6 %collective-permute-start.14 = (bf16[1024,128]{1,0:T(8,128)(2,1)S(1)}, bf16[1024,128]{1,0:T(8,128)(2,1)S(1)}, u32[]{:S(2)}, u32[]{:S(2)}) collective-permute-start(bf16[1024,128]{1,0:T(8,128)(2,1)S(1)} %fusion.1), channel_id=1, source_target_pairs={{0,16},{1,17},{2,18},{3,19},{4,20},{5,21},{6,22},{7,23},{8,24},{9,... | collective-permute-start | bytes 786440 | tf_op jit(solution)/shard_map/ppermute | solution.py:28

commit v6 on v5

--- a/solution.py
+++ b/solution.py
@@ -206,13 +206,13 @@
     )
     up_y = along_y(bf16(up2_y, up3_y), 1)
     down = along(bf16(down2, down3), -1)
-    up1, down1, own0 = run([(1, 0, 0, ()), (-1, 0, 1, ()), (0, 0, 2, ())], [one] * 3, up2)
+    up1, own0 = run([(1, 0, 0, ()), (0, 0, 1, ())], [one] * 2, up2)
     up = along(bf16(up2, up), 1)
     down_y = along_y(bf16(down2_y, down_y), -1)
     up_y, near0 = lax.optimization_barrier((up_y, near0))
     near0 = across_y(near0)
-    up, down1 = lax.optimization_barrier((bf16(up1, up, up_y, near1[0]), down1))
-    up = along(up, 1)
+    up = along(bf16(up1, up, up_y, near1[0]), 1)
+    (down1,) = run([(-1, 0, 0, ())], [one], down_y)
     down = along(bf16(down1, down, down_y, near1[1]), -1)
     arrivals = add(own0, near0, up, down)
     return (l21[None], parent_in + arrivals)

time: 66.8 us -> 66.4 us (level); the launches traced: 65.9 us -> 66.3 us
  waiting for transfers between devices: 15.8 us -> 18.3 us
  starting transfers between devices: 37.3 us -> 35 us
    ppermute x20, waiting for transfers between devices: 15.8 us -> 18.3 us  [place(): return lax.ppermute(value, AXES, pairs)]
    ppermute x20, starting transfers between devices: 37.3 us -> 35 us  [place(): return lax.ppermute(value, AXES, pairs)]
    pallas_call x5 -> x6, Pallas kernels: 3.98 us -> 4.19 us  [contributions(): pl.pallas_call(body, out_shape=[jax.ShapeDtypeStruct(shape, BF16) for sha...]
  transfers between devices with their start and end apart: 20 -> 20, of which waited for: 8 -> 7; matrix products, arithmetic and copies ran while one was open for 2% -> 2% of each run, Pallas kernels for 9% -> 9%
where the time goes in v6:
time: 66.4 us; the launch traced here: 66.3 us
  starting transfers between devices  35 us (53%)
  waiting for transfers between devices  18.3 us (28%)
  Pallas kernels  6.67 us (10%)
  local copies, waits for them, and re-layouts  3.09 us (5%)
  other arithmetic  2.46 us (4%)
  between operations  0.8 us (1%)
    ppermute x20, starting transfers between devices, place(): return lax.ppermute(value, AXES, pairs)  35 us
    ppermute x20, waiting for transfers between devices, place(): return lax.ppermute(value, AXES, pairs)  18.3 us
    pallas_call x6, Pallas kernels, contributions(): pl.pallas_call(body, out_shape=[jax.ShapeDtypeStruct(shape, BF16) for sha...  4.19 us
    pallas_call x2, Pallas kernels, in_vmem(): pl.pallas_call(kernel, out_shape=out_shape, in_specs=[pl.BlockSpec(memory...  2.48 us
    unnamed x8, local copies, waits for them, and re-layouts  2.2 us
  transfers between devices with their start and end apart: 20, of which 7 were waited for; matrix products, arithmetic and copies ran while one was open for 2% of the time, Pallas kernels for 9%

profile of v6, /device:TPU:6, one launch (start us, length us, event | category | flops | bytes accessed | tf_op | source)
XLA Modules:
  0.0 66.3 jit_solution(17713286351489358731)
XLA Ops:
  0.6 0.9 %fusion.2 = (bf16[1,128,256]{2,1,0:T(8,128)(2,1)S(1)}, bf16[128,256]{1,0:T(8,128)(2,1)S(1)}) fusion(bf16[1,1024,256]{2,1,0:T(8,128)(2,1)} %param.6), kind=kLoop, calls=%fused_computation.17 | loop fusion | bytes 196608 | tf_op jit(solution)/shard_map/slice | solution.py:174
  2.9 1.9 %collective-permute-start.4 = (bf16[2,128,256]{2,1,0:T(8,128)(2,1)S(1)}, bf16[2,128,256]{2,1,0:T(8,128)(2,1)S(1)}, u32[]{:S(2)}, u32[]{:S(2)}) collective-permute-start(bf16[2,128,256]{2,1,0:T(8,128)(2,1)S(1)} %pad_maximum_fusion.1.head), channel_id=1, source_target_pairs={{0,14},{1,7},{2,12},{3,5},{4,2},{5,11},{6,0},{7,9},{8,6},{9,15},{1... | collective-permute-start | bytes 393224 | tf_op jit(solution)/shard_map/ppermute | solution.py:28
  4.8 1.1 %collective-permute-start.3 = (bf16[2,128,256]{2,1,0:T(8,128)(2,1)S(1)}, bf16[2,128,256]{2,1,0:T(8,128)(2,1)S(1)}, u32[]{:S(2)}, u32[]{:S(2)}) collective-permute-start(bf16[2,128,256]{2,1,0:T(8,128)(2,1)S(1)} %pad_maximum_fusion.1.head), channel_id=1, source_target_pairs={{0,8},{1,11},{2,10},{3,9},{4,12},{5,15},{6,14},{7,13},{8,0},{9,3},... | collective-permute-start | bytes 393224 | tf_op jit(solution)/shard_map/ppermute | solution.py:28
  5.9 2.1 %collective-permute-start.2 = (bf16[2,128,256]{2,1,0:T(8,128)(2,1)S(1)}, bf16[2,128,256]{2,1,0:T(8,128)(2,1)S(1)}, u32[]{:S(2)}, u32[]{:S(2)}) collective-permute-start(bf16[2,128,256]{2,1,0:T(8,128)(2,1)S(1)} %pad_maximum_fusion.1.head), channel_id=1, source_target_pairs={{0,4},{1,13},{2,6},{3,15},{4,8},{5,1},{6,10},{7,3},{8,12},{9,5},{1... | collective-permute-start | bytes 393224 | tf_op jit(solution)/shard_map/ppermute | solution.py:28
  8.5 2.2 %copy-done = bf16[1,1024,2048]{2,1,0:T(8,128)(2,1)S(1)} copy-done((bf16[1,1024,2048]{2,1,0:T(8,128)(2,1)S(1)}, bf16[1,1024,2048]{2,1,0:T(8,128)(2,1)}, u32[]{:S(2)}) %copy-start) | copy-done | bytes 4194328
  11.5 1.4 %collective-permute-done.1 = bf16[128,256]{1,0:T(8,128)(2,1)S(1)} collective-permute-done((bf16[128,256]{1,0:T(8,128)(2,1)S(1)}, bf16[128,256]{1,0:T(8,128)(2,1)S(1)}, u32[]{:S(2)}, u32[]{:S(2)}) %collective-permute-start.1) | collective-permute-done | bytes 65568 | tf_op jit(solution)/shard_map/ppermute | solution.py:28
  12.9 1.4 %collective-permute-start.5 = (bf16[7,128,256]{2,1,0:T(8,128)(2,1)S(1)}, bf16[7,128,256]{2,1,0:T(8,128)(2,1)S(1)}, u32[]{:S(2)}, u32[]{:S(2)}) collective-permute-start(bf16[7,128,256]{2,1,0:T(8,128)(2,1)S(1)} %pad_maximum_fusion.rest), channel_id=1, source_target_pairs={{0,1},{1,0},{2,3},{3,2},{4,5},{5,4},{6,7},{7,6},{8,9},{9,8},{10,11... | collective-permute-start | bytes 1376264 | tf_op jit(solution)/shard_map/ppermute | solution.py:28
  14.3 1.7 %shard_map.78 = (bf16[1024,256]{1,0:T(8,128)(2,1)}, bf16[1024,256]{1,0:T(8,128)(2,1)S(1)}, bf16[256,256]{1,0:T(8,128)(2,1)S(1)}) custom-call(s32[1,16]{1,0:T(1,128)S(1)} %pad_add_fusion.maps, bf16[1024,256]{1,0:T(8,128)(2,1)S(1)} %bitcast.19, bf16[256,256]{1,0:T(8,128)(2,1)S(1)} %bitcast.20), custom_call_target="tpu_custom_call" | custom-call | flops 134217728 | bytes 4194304 | tf_op jit(solution)/shard_map/pallas_call | solution.py:140
  16.5 5.7 %collective-permute-start.6 = (bf16[1024,128]{1,0:T(8,128)(2,1)S(1)}, bf16[1024,128]{1,0:T(8,128)(2,1)S(1)}, u32[]{:S(2)}, u32[]{:S(2)}) collective-permute-start(bf16[1024,128]{1,0:T(8,128)(2,1)S(1)} %get-tuple-element.45), channel_id=1, source_target_pairs={{0,112},{1,113},{2,114},{3,115},{4,116},{5,117},{6,118},{7,119},{8... | collective-permute-start | bytes 786440 | tf_op jit(solution)/shard_map/ppermute | solution.py:28
  22.8 3.3 %collective-permute-start.17 = (bf16[1024,128]{1,0:T(8,128)(2,1)S(1)}, bf16[1024,128]{1,0:T(8,128)(2,1)S(1)}, u32[]{:S(2)}, u32[]{:S(2)}) collective-permute-start(bf16[1024,128]{1,0:T(8,128)(2,1)S(1)} %get-tuple-element.57), channel_id=1, source_target_pairs={{0,112},{1,113},{2,114},{3,115},{4,116},{5,117},{6,118},{7,119},{8... | collective-permute-start | bytes 786440 | tf_op jit(solution)/shard_map/ppermute | solution.py:28
  26.1 1.2 %shard_map.81 = (bf16[2,1024,128]{2,1,0:T(8,128)(2,1)S(1)}, bf16[1024,128]{1,0:T(8,128)(2,1)S(1)}, bf16[1024,128]{1,0:T(8,128)(2,1)S(1)}, bf16[1024,128]{1,0:T(8,128)(2,1)S(1)}) custom-call(bf16[1024,256]{1,0:T(8,128)(2,1)S(1)} %get-tuple-element.37.factor.after, bf16[1024,2048]{1,0:T(8,128)(2,1)S(1)} %get-tuple-element.38.trailing, ...), custom_call_target="tpu_custom_call" | custom-call | flops 335544320 | bytes 3145728 | tf_op jit(solution)/shard_map/pallas_call | solution.py:107
  27.3 3.2 %collective-permute-start.13 = (bf16[2,1024,128]{2,1,0:T(8,128)(2,1)S(1)}, bf16[2,1024,128]{2,1,0:T(8,128)(2,1)S(1)}, u32[]{:S(2)}, u32[]{:S(2)}) collective-permute-start(bf16[2,1024,128]{2,1,0:T(8,128)(2,1)S(1)} %get-tuple-element.54), channel_id=1, source_target_pairs={{0,128},{1,129},{2,130},{3,131},{4,132},{5,133},{6,134},{7,135},{8... | collective-permute-start | bytes 1572872 | tf_op jit(solution)/shard_map/ppermute | solution.py:28
  30.6 3.3 %collective-permute-start.15 = (bf16[1024,128]{1,0:T(8,128)(2,1)S(1)}, bf16[1024,128]{1,0:T(8,128)(2,1)S(1)}, u32[]{:S(2)}, u32[]{:S(2)}) collective-permute-start(bf16[1024,128]{1,0:T(8,128)(2,1)S(1)} %add_convert_fusion.5.after), channel_id=1, source_target_pairs={{0,112},{1,113},{2,114},{3,115},{4,116},{5,117},{6,118},{7,119},{8... | collective-permute-start | bytes 786440 | tf_op jit(solution)/shard_map/ppermute | solution.py:28
  34.0 0.9 %shard_map.82 = (bf16[1024,128]{1,0:T(8,128)(2,1)S(1)}, bf16[1024,128]{1,0:T(8,128)(2,1)S(1)}, bf16[1024,128]{1,0:T(8,128)(2,1)S(1)}, bf16[1024,128]{1,0:T(8,128)(2,1)S(1)}) custom-call(bf16[1024,256]{1,0:T(8,128)(2,1)S(1)} %get-tuple-element.37.factor.after, bf16[1024,2048]{1,0:T(8,128)(2,1)S(1)} %get-tuple-element.38.trailing, ...), custom_call_target="tpu_custom_call" | custom-call | flops 268435456 | bytes 2621440 | tf_op jit(solution)/shard_map/pallas_call | solution.py:107
  34.9 2.8 %collective-permute-done.7 = bf16[1024,128]{1,0:T(8,128)(2,1)S(1)} collective-permute-done((bf16[1024,128]{1,0:T(8,128)(2,1)S(1)}, bf16[1024,128]{1,0:T(8,128)(2,1)S(1)}, u32[]{:S(2)}, u32[]{:S(2)}) %collective-permute-start.7) | collective-permute-done | bytes 262176 | tf_op jit(solution)/shard_map/ppermute | solution.py:28
  37.8 2.0 %collective-permute-start.8 = (bf16[1024,128]{1,0:T(8,128)(2,1)S(1)}, bf16[1024,128]{1,0:T(8,128)(2,1)S(1)}, u32[]{:S(2)}, u32[]{:S(2)}) collective-permute-start(bf16[1024,128]{1,0:T(8,128)(2,1)S(1)} %add_convert_fusion.4), channel_id=1, source_target_pairs={{0,144},{1,145},{2,146},{3,147},{4,148},{5,149},{6,150},{7,151},{8... | collective-permute-start | bytes 786440 | tf_op jit(solution)/shard_map/ppermute | solution.py:28
  39.9 4.6 %collective-permute-start.18 = (bf16[1024,128]{1,0:T(8,128)(2,1)S(1)}, bf16[1024,128]{1,0:T(8,128)(2,1)S(1)}, u32[]{:S(2)}, u32[]{:S(2)}) collective-permute-start(bf16[1024,128]{1,0:T(8,128)(2,1)S(1)} %add_convert_fusion), channel_id=1, source_target_pairs={{0,112},{1,113},{2,114},{3,115},{4,116},{5,117},{6,118},{7,119},{8... | collective-permute-start | bytes 786440 | tf_op jit(solution)/shard_map/ppermute | solution.py:28
  44.6 1.4 %collective-permute-start.16 = (bf16[1024,128]{1,0:T(8,128)(2,1)S(1)}, bf16[1024,128]{1,0:T(8,128)(2,1)S(1)}, u32[]{:S(2)}, u32[]{:S(2)}) collective-permute-start(bf16[1024,128]{1,0:T(8,128)(2,1)S(1)} %add_convert_fusion.1), channel_id=1, source_target_pairs={{0,240},{1,241},{2,242},{3,243},{4,244},{5,245},{6,246},{7,247},{8... | collective-permute-start | bytes 786440 | tf_op jit(solution)/shard_map/ppermute | solution.py:28
  46.8 6.8 %collective-permute-done.8 = bf16[1024,128]{1,0:T(8,128)(2,1)S(1)} collective-permute-done((bf16[1024,128]{1,0:T(8,128)(2,1)S(1)}, bf16[1024,128]{1,0:T(8,128)(2,1)S(1)}, u32[]{:S(2)}, u32[]{:S(2)}) %collective-permute-start.8) | collective-permute-done | bytes 262176 | tf_op jit(solution)/shard_map/ppermute | solution.py:28
  54.4 2.4 %collective-permute-done.16.after = bf16[1024,128]{1,0:T(8,128)(2,1)S(1)} collective-permute-done((bf16[1024,128]{1,0:T(8,128)(2,1)S(1)}, bf16[1024,128]{1,0:T(8,128)(2,1)S(1)}, u32[]{:S(2)}, u32[]{:S(2)}) %collective-permute-start.16) | collective-permute-done | bytes 262176 | tf_op jit(solution)/shard_map/ppermute | solution.py:28
  57.8 3.2 %collective-permute-start.19 = (bf16[1024,128]{1,0:T(8,128)(2,1)S(1)}, bf16[1024,128]{1,0:T(8,128)(2,1)S(1)}, u32[]{:S(2)}, u32[]{:S(2)}) collective-permute-start(bf16[1024,128]{1,0:T(8,128)(2,1)S(1)} %get-tuple-element.59), channel_id=1, source_target_pairs={{0,112},{1,113},{2,114},{3,115},{4,116},{5,117},{6,118},{7,119},{8... | collective-permute-start | bytes 786440 | tf_op jit(solution)/shard_map/ppermute | solution.py:28
  61.0 1.4 %collective-permute-done.9 = bf16[1024,128]{1,0:T(8,128)(2,1)S(1)} collective-permute-done((bf16[1024,128]{1,0:T(8,128)(2,1)S(1)}, bf16[1024,128]{1,0:T(8,128)(2,1)S(1)}, u32[]{:S(2)}, u32[]{:S(2)}) %collective-permute-start.9) | collective-permute-done | bytes 262176 | tf_op jit(solution)/shard_map/ppermute | solution.py:28
  62.4 3.0 %collective-permute-done.14 = bf16[1024,128]{1,0:T(8,128)(2,1)S(1)} collective-permute-done((bf16[1024,128]{1,0:T(8,128)(2,1)S(1)}, bf16[1024,128]{1,0:T(8,128)(2,1)S(1)}, u32[]{:S(2)}, u32[]{:S(2)}) %collective-permute-start.14) | collective-permute-done | bytes 262176 | tf_op jit(solution)/shard_map/ppermute | solution.py:28
  65.3 0.9 %add_add_fusion = f32[1024,128]{1,0:T(8,128)} fusion(f32[1024,128]{1,0:T(8,128)S(1)} %copy-done.3, bf16[1024,128]{1,0:T(8,128)(2,1)S(1)} %collective-permute-done.19, bf16[1024,128]{1,0:T(8,128)(2,1)S(1)} %collective-permute-done.14, bf16[1024,128]{1,0:T(8,128)(2,1)S(1)} %collective-permute-done.9, bf16[1024,128]{1,0:T(8,128)(2,1)S(1)} %get-tuple-element.47), kind=kLoop, calls=%fused_computation.4 | loop fusion | flops 1048576 | bytes 2097152 | tf_op jit(solution)/shard_map/add | solution.py:218
  (44 shorter events, 6.7 us)
Async XLA Ops:
  0.6 13.7 %copy-start.2 = (bf16[1,256,256]{2,1,0:T(8,128)(2,1)S(1)}, bf16[1,256,256]{2,1,0:T(8,128)(2,1)}, u32[]{:S(2)}) copy-start(bf16[1,256,256]{2,1,0:T(8,128)(2,1)} %param.7) | copy-start | bytes 393220
  1.5 1.3 %collective-permute-start = (bf16[128,256]{1,0:T(8,128)(2,1)S(1)}, bf16[128,256]{1,0:T(8,128)(2,1)S(1)}, u32[]{:S(2)}, u32[]{:S(2)}) collective-permute-start(bf16[128,256]{1,0:T(8,128)(2,1)S(1)} %get-tuple-element.61), channel_id=1, source_target_pairs={{0,1},{1,0},{2,3},{3,2},{4,5},{5,4},{6,7},{7,6},{8,9},{9,8},{10,11... | collective-permute-start | bytes 196616 | tf_op jit(solution)/shard_map/ppermute | solution.py:28
  2.9 10.0 %collective-permute-start.4 = (bf16[2,128,256]{2,1,0:T(8,128)(2,1)S(1)}, bf16[2,128,256]{2,1,0:T(8,128)(2,1)S(1)}, u32[]{:S(2)}, u32[]{:S(2)}) collective-permute-start(bf16[2,128,256]{2,1,0:T(8,128)(2,1)S(1)} %pad_maximum_fusion.1.head), channel_id=1, source_target_pairs={{0,14},{1,7},{2,12},{3,5},{4,2},{5,11},{6,0},{7,9},{8,6},{9,15},{1... | collective-permute-start | bytes 393224 | tf_op jit(solution)/shard_map/ppermute | solution.py:28
  4.8 8.1 %collective-permute-start.3 = (bf16[2,128,256]{2,1,0:T(8,128)(2,1)S(1)}, bf16[2,128,256]{2,1,0:T(8,128)(2,1)S(1)}, u32[]{:S(2)}, u32[]{:S(2)}) collective-permute-start(bf16[2,128,256]{2,1,0:T(8,128)(2,1)S(1)} %pad_maximum_fusion.1.head), channel_id=1, source_target_pairs={{0,8},{1,11},{2,10},{3,9},{4,12},{5,15},{6,14},{7,13},{8,0},{9,3},... | collective-permute-start | bytes 393224 | tf_op jit(solution)/shard_map/ppermute | solution.py:28
  5.9 6.9 %collective-permute-start.2 = (bf16[2,128,256]{2,1,0:T(8,128)(2,1)S(1)}, bf16[2,128,256]{2,1,0:T(8,128)(2,1)S(1)}, u32[]{:S(2)}, u32[]{:S(2)}) collective-permute-start(bf16[2,128,256]{2,1,0:T(8,128)(2,1)S(1)} %pad_maximum_fusion.1.head), channel_id=1, source_target_pairs={{0,4},{1,13},{2,6},{3,15},{4,8},{5,1},{6,10},{7,3},{8,12},{9,5},{1... | collective-permute-start | bytes 393224 | tf_op jit(solution)/shard_map/ppermute | solution.py:28
  8.0 4.8 %collective-permute-start.1 = (bf16[128,256]{1,0:T(8,128)(2,1)S(1)}, bf16[128,256]{1,0:T(8,128)(2,1)S(1)}, u32[]{:S(2)}, u32[]{:S(2)}) collective-permute-start(bf16[128,256]{1,0:T(8,128)(2,1)S(1)} %get-tuple-element.61), channel_id=1, source_target_pairs={{0,2},{1,3},{2,0},{3,1},{4,6},{5,7},{6,4},{7,5},{8,10},{9,11},{10,... | collective-permute-start | bytes 196616 | tf_op jit(solution)/shard_map/ppermute | solution.py:28
  8.5 2.2 %copy-start = (bf16[1,1024,2048]{2,1,0:T(8,128)(2,1)S(1)}, bf16[1,1024,2048]{2,1,0:T(8,128)(2,1)}, u32[]{:S(2)}) copy-start(bf16[1,1024,2048]{2,1,0:T(8,128)(2,1)} %param.8) | copy-start | bytes 12582916
  10.7 3.7 %copy-start.1 = (bf16[1,1024,256]{2,1,0:T(8,128)(2,1)S(1)}, bf16[1,1024,256]{2,1,0:T(8,128)(2,1)}, u32[]{:S(2)}) copy-start(bf16[1,1024,256]{2,1,0:T(8,128)(2,1)} %param.6) | copy-start | bytes 1572868
  12.9 3.1 %collective-permute-start.5 = (bf16[7,128,256]{2,1,0:T(8,128)(2,1)S(1)}, bf16[7,128,256]{2,1,0:T(8,128)(2,1)S(1)}, u32[]{:S(2)}, u32[]{:S(2)}) collective-permute-start(bf16[7,128,256]{2,1,0:T(8,128)(2,1)S(1)} %pad_maximum_fusion.rest), channel_id=1, source_target_pairs={{0,1},{1,0},{2,3},{3,2},{4,5},{5,4},{6,7},{7,6},{8,9},{9,8},{10,11... | collective-permute-start | bytes 1376264 | tf_op jit(solution)/shard_map/ppermute | solution.py:28
  16.5 14.0 %collective-permute-start.6 = (bf16[1024,128]{1,0:T(8,128)(2,1)S(1)}, bf16[1024,128]{1,0:T(8,128)(2,1)S(1)}, u32[]{:S(2)}, u32[]{:S(2)}) collective-permute-start(bf16[1024,128]{1,0:T(8,128)(2,1)S(1)} %get-tuple-element.45), channel_id=1, source_target_pairs={{0,112},{1,113},{2,114},{3,115},{4,116},{5,117},{6,118},{7,119},{8... | collective-permute-start | bytes 786440 | tf_op jit(solution)/shard_map/ppermute | solution.py:28
  22.3 11.6 %collective-permute-start.10 = (bf16[1024,128]{1,0:T(8,128)(2,1)S(1)}, bf16[1024,128]{1,0:T(8,128)(2,1)S(1)}, u32[]{:S(2)}, u32[]{:S(2)}) collective-permute-start(bf16[1024,128]{1,0:T(8,128)(2,1)S(1)} %get-tuple-element.42.after), channel_id=1, source_target_pairs={{0,16},{1,17},{2,18},{3,19},{4,20},{5,21},{6,22},{7,23},{8,24},{9,... | collective-permute-start | bytes 786440 | tf_op jit(solution)/shard_map/ppermute | solution.py:28
  22.8 17.1 %collective-permute-start.17 = (bf16[1024,128]{1,0:T(8,128)(2,1)S(1)}, bf16[1024,128]{1,0:T(8,128)(2,1)S(1)}, u32[]{:S(2)}, u32[]{:S(2)}) collective-permute-start(bf16[1024,128]{1,0:T(8,128)(2,1)S(1)} %get-tuple-element.57), channel_id=1, source_target_pairs={{0,112},{1,113},{2,114},{3,115},{4,116},{5,117},{6,118},{7,119},{8... | collective-permute-start | bytes 786440 | tf_op jit(solution)/shard_map/ppermute | solution.py:28
  26.1 11.6 %collective-permute-start.7 = (bf16[1024,128]{1,0:T(8,128)(2,1)S(1)}, bf16[1024,128]{1,0:T(8,128)(2,1)S(1)}, u32[]{:S(2)}, u32[]{:S(2)}) collective-permute-start(bf16[1024,128]{1,0:T(8,128)(2,1)S(1)} %get-tuple-element.43.after), channel_id=1, source_target_pairs={{0,16},{1,17},{2,18},{3,19},{4,20},{5,21},{6,22},{7,23},{8,24},{9,... | collective-permute-start | bytes 786440 | tf_op jit(solution)/shard_map/ppermute | solution.py:28
  27.3 30.0 %collective-permute-start.13 = (bf16[2,1024,128]{2,1,0:T(8,128)(2,1)S(1)}, bf16[2,1024,128]{2,1,0:T(8,128)(2,1)S(1)}, u32[]{:S(2)}, u32[]{:S(2)}) collective-permute-start(bf16[2,1024,128]{2,1,0:T(8,128)(2,1)S(1)} %get-tuple-element.54), channel_id=1, source_target_pairs={{0,128},{1,129},{2,130},{3,131},{4,132},{5,133},{6,134},{7,135},{8... | collective-permute-start | bytes 1572872 | tf_op jit(solution)/shard_map/ppermute | solution.py:28
  30.6 13.9 %collective-permute-start.15 = (bf16[1024,128]{1,0:T(8,128)(2,1)S(1)}, bf16[1024,128]{1,0:T(8,128)(2,1)S(1)}, u32[]{:S(2)}, u32[]{:S(2)}) collective-permute-start(bf16[1024,128]{1,0:T(8,128)(2,1)S(1)} %add_convert_fusion.5.after), channel_id=1, source_target_pairs={{0,112},{1,113},{2,114},{3,115},{4,116},{5,117},{6,118},{7,119},{8... | collective-permute-start | bytes 786440 | tf_op jit(solution)/shard_map/ppermute | solution.py:28
  34.0 12.0 %collective-permute-start.11 = (bf16[1024,128]{1,0:T(8,128)(2,1)S(1)}, bf16[1024,128]{1,0:T(8,128)(2,1)S(1)}, u32[]{:S(2)}, u32[]{:S(2)}) collective-permute-start(bf16[1024,128]{1,0:T(8,128)(2,1)S(1)} %add_convert_fusion.3), channel_id=1, source_target_pairs={{0,16},{1,17},{2,18},{3,19},{4,20},{5,21},{6,22},{7,23},{8,24},{9,... | collective-permute-start | bytes 786440 | tf_op jit(solution)/shard_map/ppermute | solution.py:28
  37.8 15.8 %collective-permute-start.8 = (bf16[1024,128]{1,0:T(8,128)(2,1)S(1)}, bf16[1024,128]{1,0:T(8,128)(2,1)S(1)}, u32[]{:S(2)}, u32[]{:S(2)}) collective-permute-start(bf16[1024,128]{1,0:T(8,128)(2,1)S(1)} %add_convert_fusion.4), channel_id=1, source_target_pairs={{0,144},{1,145},{2,146},{3,147},{4,148},{5,149},{6,150},{7,151},{8... | collective-permute-start | bytes 786440 | tf_op jit(solution)/shard_map/ppermute | solution.py:28
  39.9 17.4 %collective-permute-start.18 = (bf16[1024,128]{1,0:T(8,128)(2,1)S(1)}, bf16[1024,128]{1,0:T(8,128)(2,1)S(1)}, u32[]{:S(2)}, u32[]{:S(2)}) collective-permute-start(bf16[1024,128]{1,0:T(8,128)(2,1)S(1)} %add_convert_fusion), channel_id=1, source_target_pairs={{0,112},{1,113},{2,114},{3,115},{4,116},{5,117},{6,118},{7,119},{8... | collective-permute-start | bytes 786440 | tf_op jit(solution)/shard_map/ppermute | solution.py:28
  44.6 12.3 %collective-permute-start.16 = (bf16[1024,128]{1,0:T(8,128)(2,1)S(1)}, bf16[1024,128]{1,0:T(8,128)(2,1)S(1)}, u32[]{:S(2)}, u32[]{:S(2)}) collective-permute-start(bf16[1024,128]{1,0:T(8,128)(2,1)S(1)} %add_convert_fusion.1), channel_id=1, source_target_pairs={{0,240},{1,241},{2,242},{3,243},{4,244},{5,245},{6,246},{7,247},{8... | collective-permute-start | bytes 786440 | tf_op jit(solution)/shard_map/ppermute | solution.py:28
  46.0 11.4 %collective-permute-start.12 = (bf16[1024,128]{1,0:T(8,128)(2,1)S(1)}, bf16[1024,128]{1,0:T(8,128)(2,1)S(1)}, u32[]{:S(2)}, u32[]{:S(2)}) collective-permute-start(bf16[1024,128]{1,0:T(8,128)(2,1)S(1)} %add_convert_fusion.2), channel_id=1, source_target_pairs={{0,16},{1,17},{2,18},{3,19},{4,20},{5,21},{6,22},{7,23},{8,24},{9,... | collective-permute-start | bytes 786440 | tf_op jit(solution)/shard_map/ppermute | solution.py:28
  53.6 11.8 %copy-start.3 = (f32[1024,128]{1,0:T(8,128)S(1)}, f32[1024,128]{1,0:T(8,128)}, u32[]{:S(2)}) copy-start(f32[1024,128]{1,0:T(8,128)} %param.11) | copy-start | bytes 1572868
  53.6 8.8 %collective-permute-start.9 = (bf16[1024,128]{1,0:T(8,128)(2,1)S(1)}, bf16[1024,128]{1,0:T(8,128)(2,1)S(1)}, u32[]{:S(2)}, u32[]{:S(2)}) collective-permute-start(bf16[1024,128]{1,0:T(8,128)(2,1)S(1)} %get-tuple-element.50), channel_id=1, source_target_pairs={{0,128},{1,129},{2,130},{3,131},{4,132},{5,133},{6,134},{7,135},{8... | collective-permute-start | bytes 786440 | tf_op jit(solution)/shard_map/ppermute | solution.py:28
  57.7 7.7 %collective-permute-start.14 = (bf16[1024,128]{1,0:T(8,128)(2,1)S(1)}, bf16[1024,128]{1,0:T(8,128)(2,1)S(1)}, u32[]{:S(2)}, u32[]{:S(2)}) collective-permute-start(bf16[1024,128]{1,0:T(8,128)(2,1)S(1)} %get-tuple-element.58), channel_id=1, source_target_pairs={{0,16},{1,17},{2,18},{3,19},{4,20},{5,21},{6,22},{7,23},{8,24},{9,... | collective-permute-start | bytes 786440 | tf_op jit(solution)/shard_map/ppermute | solution.py:28
  57.8 7.6 %collective-permute-start.19 = (bf16[1024,128]{1,0:T(8,128)(2,1)S(1)}, bf16[1024,128]{1,0:T(8,128)(2,1)S(1)}, u32[]{:S(2)}, u32[]{:S(2)}) collective-permute-start(bf16[1024,128]{1,0:T(8,128)(2,1)S(1)} %get-tuple-element.59), channel_id=1, source_target_pairs={{0,112},{1,113},{2,114},{3,115},{4,116},{5,117},{6,118},{7,119},{8... | collective-permute-start | bytes 786440 | tf_op jit(solution)/shard_map/ppermute | solution.py:28

commit v7 on v6

--- a/solution.py
+++ b/solution.py
@@ -190,14 +190,11 @@
 
     far, far_y = run([(4, 0, 0, ()), (4, 1, 1, ())], [one, one], prepared[0])
     up4, down4_y = along(far, 1), along(far_y, -1)
-    next_y, next_ = run([(3, 1, 0, ()), (-3, 0, 1, ())], [one, one], far)
+    (near1,) = run([(1, 1, 0, (0,)), (-1, 1, 0, (1,))], [two], far)
+    next_y, next_ = run([(3, 1, 0, ()), (-3, 0, 1, ())], [one, one], near1)
+    near1 = across_y(near1)
     up3_y, down3 = along(next_y, 1), along(next_, -1)
-    near1, near0, up3, down3_y = run(
-        [(1, 1, 0, (0,)), (-1, 1, 0, (1,)), (3, 0, 2, ()), (-3, 1, 3, ()), (0, 1, 1, ())],
-        [two, one, one, one],
-        next_y,
-    )
-    near1 = across_y(near1)
+    up3, down3_y, near0 = run([(3, 0, 0, ()), (-3, 1, 1, ()), (0, 1, 2, ())], [one] * 3, next_y)
     up = along(bf16(up3, up4), 1)
     down3_y = bf16(down3_y, down4_y)
     down_y = along(down3_y, -1)

time: 66.4 us -> 66.5 us (level)
  waiting for transfers between devices: 18.3 us -> 17.4 us
  starting transfers between devices: 35 us -> 35.7 us
    ppermute x20, waiting for transfers between devices: 18.3 us -> 17.4 us  [place(): return lax.ppermute(value, AXES, pairs)]
    ppermute x20, starting transfers between devices: 35 us -> 35.7 us  [place(): return lax.ppermute(value, AXES, pairs)]
    pallas_call x6 -> x7, Pallas kernels: 4.19 us -> 4.35 us  [contributions(): pl.pallas_call(body, out_shape=[jax.ShapeDtypeStruct(shape, BF16) for sha...]
where the time goes in v7:
time: 66.5 us; the launch traced here: 66.4 us
  starting transfers between devices  35.7 us (54%)
  waiting for transfers between devices  17.4 us (26%)
  Pallas kernels  6.83 us (10%)
  local copies, waits for them, and re-layouts  3.09 us (5%)
  other arithmetic  2.48 us (4%)
  between operations  0.84 us (1%)
    ppermute x20, starting transfers between devices, place(): return lax.ppermute(value, AXES, pairs)  35.7 us
    ppermute x20, waiting for transfers between devices, place(): return lax.ppermute(value, AXES, pairs)  17.4 us
    pallas_call x7, Pallas kernels, contributions(): pl.pallas_call(body, out_shape=[jax.ShapeDtypeStruct(shape, BF16) for sha...  4.35 us
    pallas_call x2, Pallas kernels, in_vmem(): pl.pallas_call(kernel, out_shape=out_shape, in_specs=[pl.BlockSpec(memory...  2.48 us
    unnamed x8, local copies, waits for them, and re-layouts  2.2 us
  transfers between devices with their start and end apart: 20, of which 7 were waited for; matrix products, arithmetic and copies ran while one was open for 2% of the time, Pallas kernels for 9%

profile of v7, /device:TPU:6, one launch (start us, length us, event | category | flops | bytes accessed | tf_op | source)
XLA Modules:
  0.0 66.4 jit_solution(12335241474122600180)
XLA Ops:
  0.6 0.9 %fusion.2 = (bf16[1,128,256]{2,1,0:T(8,128)(2,1)S(1)}, bf16[128,256]{1,0:T(8,128)(2,1)S(1)}) fusion(bf16[1,1024,256]{2,1,0:T(8,128)(2,1)} %param.6), kind=kLoop, calls=%fused_computation.17 | loop fusion | bytes 196608 | tf_op jit(solution)/shard_map/slice | solution.py:174
  2.9 1.9 %collective-permute-start.4 = (bf16[2,128,256]{2,1,0:T(8,128)(2,1)S(1)}, bf16[2,128,256]{2,1,0:T(8,128)(2,1)S(1)}, u32[]{:S(2)}, u32[]{:S(2)}) collective-permute-start(bf16[2,128,256]{2,1,0:T(8,128)(2,1)S(1)} %pad_maximum_fusion.1.head), channel_id=1, source_target_pairs={{0,14},{1,7},{2,12},{3,5},{4,2},{5,11},{6,0},{7,9},{8,6},{9,15},{1... | collective-permute-start | bytes 393224 | tf_op jit(solution)/shard_map/ppermute | solution.py:28
  4.8 1.1 %collective-permute-start.3 = (bf16[2,128,256]{2,1,0:T(8,128)(2,1)S(1)}, bf16[2,128,256]{2,1,0:T(8,128)(2,1)S(1)}, u32[]{:S(2)}, u32[]{:S(2)}) collective-permute-start(bf16[2,128,256]{2,1,0:T(8,128)(2,1)S(1)} %pad_maximum_fusion.1.head), channel_id=1, source_target_pairs={{0,8},{1,11},{2,10},{3,9},{4,12},{5,15},{6,14},{7,13},{8,0},{9,3},... | collective-permute-start | bytes 393224 | tf_op jit(solution)/shard_map/ppermute | solution.py:28
  5.9 2.1 %collective-permute-start.2 = (bf16[2,128,256]{2,1,0:T(8,128)(2,1)S(1)}, bf16[2,128,256]{2,1,0:T(8,128)(2,1)S(1)}, u32[]{:S(2)}, u32[]{:S(2)}) collective-permute-start(bf16[2,128,256]{2,1,0:T(8,128)(2,1)S(1)} %pad_maximum_fusion.1.head), channel_id=1, source_target_pairs={{0,4},{1,13},{2,6},{3,15},{4,8},{5,1},{6,10},{7,3},{8,12},{9,5},{1... | collective-permute-start | bytes 393224 | tf_op jit(solution)/shard_map/ppermute | solution.py:28
  8.5 2.2 %copy-done = bf16[1,1024,2048]{2,1,0:T(8,128)(2,1)S(1)} copy-done((bf16[1,1024,2048]{2,1,0:T(8,128)(2,1)S(1)}, bf16[1,1024,2048]{2,1,0:T(8,128)(2,1)}, u32[]{:S(2)}) %copy-start) | copy-done | bytes 4194328
  11.5 1.4 %collective-permute-done.1 = bf16[128,256]{1,0:T(8,128)(2,1)S(1)} collective-permute-done((bf16[128,256]{1,0:T(8,128)(2,1)S(1)}, bf16[128,256]{1,0:T(8,128)(2,1)S(1)}, u32[]{:S(2)}, u32[]{:S(2)}) %collective-permute-start.1) | collective-permute-done | bytes 65568 | tf_op jit(solution)/shard_map/ppermute | solution.py:28
  12.9 1.4 %collective-permute-start.5 = (bf16[7,128,256]{2,1,0:T(8,128)(2,1)S(1)}, bf16[7,128,256]{2,1,0:T(8,128)(2,1)S(1)}, u32[]{:S(2)}, u32[]{:S(2)}) collective-permute-start(bf16[7,128,256]{2,1,0:T(8,128)(2,1)S(1)} %pad_maximum_fusion.rest), channel_id=1, source_target_pairs={{0,1},{1,0},{2,3},{3,2},{4,5},{5,4},{6,7},{7,6},{8,9},{9,8},{10,11... | collective-permute-start | bytes 1376264 | tf_op jit(solution)/shard_map/ppermute | solution.py:28
  14.3 1.7 %shard_map.78 = (bf16[1024,256]{1,0:T(8,128)(2,1)}, bf16[1024,256]{1,0:T(8,128)(2,1)S(1)}, bf16[256,256]{1,0:T(8,128)(2,1)S(1)}) custom-call(s32[1,16]{1,0:T(1,128)S(1)} %pad_add_fusion.maps, bf16[1024,256]{1,0:T(8,128)(2,1)S(1)} %bitcast.19, bf16[256,256]{1,0:T(8,128)(2,1)S(1)} %bitcast.20), custom_call_target="tpu_custom_call" | custom-call | flops 134217728 | bytes 4194304 | tf_op jit(solution)/shard_map/pallas_call | solution.py:140
  16.5 5.7 %collective-permute-start.6 = (bf16[1024,128]{1,0:T(8,128)(2,1)S(1)}, bf16[1024,128]{1,0:T(8,128)(2,1)S(1)}, u32[]{:S(2)}, u32[]{:S(2)}) collective-permute-start(bf16[1024,128]{1,0:T(8,128)(2,1)S(1)} %get-tuple-element.44), channel_id=1, source_target_pairs={{0,112},{1,113},{2,114},{3,115},{4,116},{5,117},{6,118},{7,119},{8... | collective-permute-start | bytes 786440 | tf_op jit(solution)/shard_map/ppermute | solution.py:28
  22.8 3.2 %collective-permute-start.13 = (bf16[2,1024,128]{2,1,0:T(8,128)(2,1)S(1)}, bf16[2,1024,128]{2,1,0:T(8,128)(2,1)S(1)}, u32[]{:S(2)}, u32[]{:S(2)}) collective-permute-start(bf16[2,1024,128]{2,1,0:T(8,128)(2,1)S(1)} %shard_map.80.after), channel_id=1, source_target_pairs={{0,128},{1,129},{2,130},{3,131},{4,132},{5,133},{6,134},{7,135},{8... | collective-permute-start | bytes 1572872 | tf_op jit(solution)/shard_map/ppermute | solution.py:28
  26.5 3.3 %collective-permute-start.17 = (bf16[1024,128]{1,0:T(8,128)(2,1)S(1)}, bf16[1024,128]{1,0:T(8,128)(2,1)S(1)}, u32[]{:S(2)}, u32[]{:S(2)}) collective-permute-start(bf16[1024,128]{1,0:T(8,128)(2,1)S(1)} %get-tuple-element.55), channel_id=1, source_target_pairs={{0,112},{1,113},{2,114},{3,115},{4,116},{5,117},{6,118},{7,119},{8... | collective-permute-start | bytes 786440 | tf_op jit(solution)/shard_map/ppermute | solution.py:28
  30.8 3.3 %collective-permute-start.15 = (bf16[1024,128]{1,0:T(8,128)(2,1)S(1)}, bf16[1024,128]{1,0:T(8,128)(2,1)S(1)}, u32[]{:S(2)}, u32[]{:S(2)}) collective-permute-start(bf16[1024,128]{1,0:T(8,128)(2,1)S(1)} %add_convert_fusion.5.after), channel_id=1, source_target_pairs={{0,112},{1,113},{2,114},{3,115},{4,116},{5,117},{6,118},{7,119},{8... | collective-permute-start | bytes 786440 | tf_op jit(solution)/shard_map/ppermute | solution.py:28
  34.4 0.9 %shard_map.83 = (bf16[1024,128]{1,0:T(8,128)(2,1)S(1)}, bf16[1024,128]{1,0:T(8,128)(2,1)S(1)}, bf16[1024,128]{1,0:T(8,128)(2,1)S(1)}, bf16[1024,128]{1,0:T(8,128)(2,1)S(1)}) custom-call(bf16[1024,256]{1,0:T(8,128)(2,1)S(1)} %get-tuple-element.36.factor.after, bf16[1024,2048]{1,0:T(8,128)(2,1)S(1)} %get-tuple-element.37.trailing, ...), custom_call_target="tpu_custom_call" | custom-call | flops 268435456 | bytes 2621440 | tf_op jit(solution)/shard_map/pallas_call | solution.py:107
  35.3 4.7 %collective-permute-done.7 = bf16[1024,128]{1,0:T(8,128)(2,1)S(1)} collective-permute-done((bf16[1024,128]{1,0:T(8,128)(2,1)S(1)}, bf16[1024,128]{1,0:T(8,128)(2,1)S(1)}, u32[]{:S(2)}, u32[]{:S(2)}) %collective-permute-start.7) | collective-permute-done | bytes 262176 | tf_op jit(solution)/shard_map/ppermute | solution.py:28
  40.2 4.1 %collective-permute-start.18 = (bf16[1024,128]{1,0:T(8,128)(2,1)S(1)}, bf16[1024,128]{1,0:T(8,128)(2,1)S(1)}, u32[]{:S(2)}, u32[]{:S(2)}) collective-permute-start(bf16[1024,128]{1,0:T(8,128)(2,1)S(1)} %add_convert_fusion), channel_id=1, source_target_pairs={{0,112},{1,113},{2,114},{3,115},{4,116},{5,117},{6,118},{7,119},{8... | collective-permute-start | bytes 786440 | tf_op jit(solution)/shard_map/ppermute | solution.py:28
  44.4 1.7 %collective-permute-start.16 = (bf16[1024,128]{1,0:T(8,128)(2,1)S(1)}, bf16[1024,128]{1,0:T(8,128)(2,1)S(1)}, u32[]{:S(2)}, u32[]{:S(2)}) collective-permute-start(bf16[1024,128]{1,0:T(8,128)(2,1)S(1)} %add_convert_fusion.1), channel_id=1, source_target_pairs={{0,240},{1,241},{2,242},{3,243},{4,244},{5,245},{6,246},{7,247},{8... | collective-permute-start | bytes 786440 | tf_op jit(solution)/shard_map/ppermute | solution.py:28
  46.2 2.1 %collective-permute-start.12 = (bf16[1024,128]{1,0:T(8,128)(2,1)S(1)}, bf16[1024,128]{1,0:T(8,128)(2,1)S(1)}, u32[]{:S(2)}, u32[]{:S(2)}) collective-permute-start(bf16[1024,128]{1,0:T(8,128)(2,1)S(1)} %add_convert_fusion.2), channel_id=1, source_target_pairs={{0,16},{1,17},{2,18},{3,19},{4,20},{5,21},{6,22},{7,23},{8,24},{9,... | collective-permute-start | bytes 786440 | tf_op jit(solution)/shard_map/ppermute | solution.py:28
  48.8 5.2 %collective-permute-done.8 = bf16[1024,128]{1,0:T(8,128)(2,1)S(1)} collective-permute-done((bf16[1024,128]{1,0:T(8,128)(2,1)S(1)}, bf16[1024,128]{1,0:T(8,128)(2,1)S(1)}, u32[]{:S(2)}, u32[]{:S(2)}) %collective-permute-start.8) | collective-permute-done | bytes 262176 | tf_op jit(solution)/shard_map/ppermute | solution.py:28
  54.0 1.6 %collective-permute-start.9 = (bf16[1024,128]{1,0:T(8,128)(2,1)S(1)}, bf16[1024,128]{1,0:T(8,128)(2,1)S(1)}, u32[]{:S(2)}, u32[]{:S(2)}) collective-permute-start(bf16[1024,128]{1,0:T(8,128)(2,1)S(1)} %get-tuple-element.49), channel_id=1, source_target_pairs={{0,128},{1,129},{2,130},{3,131},{4,132},{5,133},{6,134},{7,135},{8... | collective-permute-start | bytes 786440 | tf_op jit(solution)/shard_map/ppermute | solution.py:28
  55.7 1.2 %collective-permute-done.16.after = bf16[1024,128]{1,0:T(8,128)(2,1)S(1)} collective-permute-done((bf16[1024,128]{1,0:T(8,128)(2,1)S(1)}, bf16[1024,128]{1,0:T(8,128)(2,1)S(1)}, u32[]{:S(2)}, u32[]{:S(2)}) %collective-permute-start.16) | collective-permute-done | bytes 262176 | tf_op jit(solution)/shard_map/ppermute | solution.py:28
  57.8 3.2 %collective-permute-start.19 = (bf16[1024,128]{1,0:T(8,128)(2,1)S(1)}, bf16[1024,128]{1,0:T(8,128)(2,1)S(1)}, u32[]{:S(2)}, u32[]{:S(2)}) collective-permute-start(bf16[1024,128]{1,0:T(8,128)(2,1)S(1)} %get-tuple-element.57), channel_id=1, source_target_pairs={{0,112},{1,113},{2,114},{3,115},{4,116},{5,117},{6,118},{7,119},{8... | collective-permute-start | bytes 786440 | tf_op jit(solution)/shard_map/ppermute | solution.py:28
  61.0 1.4 %collective-permute-done.9 = bf16[1024,128]{1,0:T(8,128)(2,1)S(1)} collective-permute-done((bf16[1024,128]{1,0:T(8,128)(2,1)S(1)}, bf16[1024,128]{1,0:T(8,128)(2,1)S(1)}, u32[]{:S(2)}, u32[]{:S(2)}) %collective-permute-start.9) | collective-permute-done | bytes 262176 | tf_op jit(solution)/shard_map/ppermute | solution.py:28
  62.4 3.0 %collective-permute-done.14 = bf16[1024,128]{1,0:T(8,128)(2,1)S(1)} collective-permute-done((bf16[1024,128]{1,0:T(8,128)(2,1)S(1)}, bf16[1024,128]{1,0:T(8,128)(2,1)S(1)}, u32[]{:S(2)}, u32[]{:S(2)}) %collective-permute-start.14) | collective-permute-done | bytes 262176 | tf_op jit(solution)/shard_map/ppermute | solution.py:28
  65.4 1.0 %add_add_fusion = f32[1024,128]{1,0:T(8,128)} fusion(f32[1024,128]{1,0:T(8,128)S(1)} %copy-done.3, bf16[1024,128]{1,0:T(8,128)(2,1)S(1)} %collective-permute-done.19, bf16[1024,128]{1,0:T(8,128)(2,1)S(1)} %collective-permute-done.14, bf16[1024,128]{1,0:T(8,128)(2,1)S(1)} %collective-permute-done.9, bf16[1024,128]{1,0:T(8,128)(2,1)S(1)} %get-tuple-element.46), kind=kLoop, calls=%fused_computation.4 | loop fusion | flops 1048576 | bytes 2097152 | tf_op jit(solution)/shard_map/add | solution.py:215
  (45 shorter events, 7.3 us)
Async XLA Ops:
  0.6 13.7 %copy-start.2 = (bf16[1,256,256]{2,1,0:T(8,128)(2,1)S(1)}, bf16[1,256,256]{2,1,0:T(8,128)(2,1)}, u32[]{:S(2)}) copy-start(bf16[1,256,256]{2,1,0:T(8,128)(2,1)} %param.7) | copy-start | bytes 393220
  1.5 1.3 %collective-permute-start = (bf16[128,256]{1,0:T(8,128)(2,1)S(1)}, bf16[128,256]{1,0:T(8,128)(2,1)S(1)}, u32[]{:S(2)}, u32[]{:S(2)}) collective-permute-start(bf16[128,256]{1,0:T(8,128)(2,1)S(1)} %get-tuple-element.59), channel_id=1, source_target_pairs={{0,1},{1,0},{2,3},{3,2},{4,5},{5,4},{6,7},{7,6},{8,9},{9,8},{10,11... | collective-permute-start | bytes 196616 | tf_op jit(solution)/shard_map/ppermute | solution.py:28
  2.9 10.0 %collective-permute-start.4 = (bf16[2,128,256]{2,1,0:T(8,128)(2,1)S(1)}, bf16[2,128,256]{2,1,0:T(8,128)(2,1)S(1)}, u32[]{:S(2)}, u32[]{:S(2)}) collective-permute-start(bf16[2,128,256]{2,1,0:T(8,128)(2,1)S(1)} %pad_maximum_fusion.1.head), channel_id=1, source_target_pairs={{0,14},{1,7},{2,12},{3,5},{4,2},{5,11},{6,0},{7,9},{8,6},{9,15},{1... | collective-permute-start | bytes 393224 | tf_op jit(solution)/shard_map/ppermute | solution.py:28
  4.8 8.1 %collective-permute-start.3 = (bf16[2,128,256]{2,1,0:T(8,128)(2,1)S(1)}, bf16[2,128,256]{2,1,0:T(8,128)(2,1)S(1)}, u32[]{:S(2)}, u32[]{:S(2)}) collective-permute-start(bf16[2,128,256]{2,1,0:T(8,128)(2,1)S(1)} %pad_maximum_fusion.1.head), channel_id=1, source_target_pairs={{0,8},{1,11},{2,10},{3,9},{4,12},{5,15},{6,14},{7,13},{8,0},{9,3},... | collective-permute-start | bytes 393224 | tf_op jit(solution)/shard_map/ppermute | solution.py:28
  5.9 6.9 %collective-permute-start.2 = (bf16[2,128,256]{2,1,0:T(8,128)(2,1)S(1)}, bf16[2,128,256]{2,1,0:T(8,128)(2,1)S(1)}, u32[]{:S(2)}, u32[]{:S(2)}) collective-permute-start(bf16[2,128,256]{2,1,0:T(8,128)(2,1)S(1)} %pad_maximum_fusion.1.head), channel_id=1, source_target_pairs={{0,4},{1,13},{2,6},{3,15},{4,8},{5,1},{6,10},{7,3},{8,12},{9,5},{1... | collective-permute-start | bytes 393224 | tf_op jit(solution)/shard_map/ppermute | solution.py:28
  8.0 4.8 %collective-permute-start.1 = (bf16[128,256]{1,0:T(8,128)(2,1)S(1)}, bf16[128,256]{1,0:T(8,128)(2,1)S(1)}, u32[]{:S(2)}, u32[]{:S(2)}) collective-permute-start(bf16[128,256]{1,0:T(8,128)(2,1)S(1)} %get-tuple-element.59), channel_id=1, source_target_pairs={{0,2},{1,3},{2,0},{3,1},{4,6},{5,7},{6,4},{7,5},{8,10},{9,11},{10,... | collective-permute-start | bytes 196616 | tf_op jit(solution)/shard_map/ppermute | solution.py:28
  8.5 2.2 %copy-start = (bf16[1,1024,2048]{2,1,0:T(8,128)(2,1)S(1)}, bf16[1,1024,2048]{2,1,0:T(8,128)(2,1)}, u32[]{:S(2)}) copy-start(bf16[1,1024,2048]{2,1,0:T(8,128)(2,1)} %param.8) | copy-start | bytes 12582916
  10.7 3.7 %copy-start.1 = (bf16[1,1024,256]{2,1,0:T(8,128)(2,1)S(1)}, bf16[1,1024,256]{2,1,0:T(8,128)(2,1)}, u32[]{:S(2)}) copy-start(bf16[1,1024,256]{2,1,0:T(8,128)(2,1)} %param.6) | copy-start | bytes 1572868
  12.9 3.1 %collective-permute-start.5 = (bf16[7,128,256]{2,1,0:T(8,128)(2,1)S(1)}, bf16[7,128,256]{2,1,0:T(8,128)(2,1)S(1)}, u32[]{:S(2)}, u32[]{:S(2)}) collective-permute-start(bf16[7,128,256]{2,1,0:T(8,128)(2,1)S(1)} %pad_maximum_fusion.rest), channel_id=1, source_target_pairs={{0,1},{1,0},{2,3},{3,2},{4,5},{5,4},{6,7},{7,6},{8,9},{9,8},{10,11... | collective-permute-start | bytes 1376264 | tf_op jit(solution)/shard_map/ppermute | solution.py:28
  16.5 14.1 %collective-permute-start.6 = (bf16[1024,128]{1,0:T(8,128)(2,1)S(1)}, bf16[1024,128]{1,0:T(8,128)(2,1)S(1)}, u32[]{:S(2)}, u32[]{:S(2)}) collective-permute-start(bf16[1024,128]{1,0:T(8,128)(2,1)S(1)} %get-tuple-element.44), channel_id=1, source_target_pairs={{0,112},{1,113},{2,114},{3,115},{4,116},{5,117},{6,118},{7,119},{8... | collective-permute-start | bytes 786440 | tf_op jit(solution)/shard_map/ppermute | solution.py:28
  22.3 11.8 %collective-permute-start.10 = (bf16[1024,128]{1,0:T(8,128)(2,1)S(1)}, bf16[1024,128]{1,0:T(8,128)(2,1)S(1)}, u32[]{:S(2)}, u32[]{:S(2)}) collective-permute-start(bf16[1024,128]{1,0:T(8,128)(2,1)S(1)} %get-tuple-element.41.after), channel_id=1, source_target_pairs={{0,16},{1,17},{2,18},{3,19},{4,20},{5,21},{6,22},{7,23},{8,24},{9,... | collective-permute-start | bytes 786440 | tf_op jit(solution)/shard_map/ppermute | solution.py:28
  22.8 34.6 %collective-permute-start.13 = (bf16[2,1024,128]{2,1,0:T(8,128)(2,1)S(1)}, bf16[2,1024,128]{2,1,0:T(8,128)(2,1)S(1)}, u32[]{:S(2)}, u32[]{:S(2)}) collective-permute-start(bf16[2,1024,128]{2,1,0:T(8,128)(2,1)S(1)} %shard_map.80.after), channel_id=1, source_target_pairs={{0,128},{1,129},{2,130},{3,131},{4,132},{5,133},{6,134},{7,135},{8... | collective-permute-start | bytes 1572872 | tf_op jit(solution)/shard_map/ppermute | solution.py:28
  26.5 13.7 %collective-permute-start.17 = (bf16[1024,128]{1,0:T(8,128)(2,1)S(1)}, bf16[1024,128]{1,0:T(8,128)(2,1)S(1)}, u32[]{:S(2)}, u32[]{:S(2)}) collective-permute-start(bf16[1024,128]{1,0:T(8,128)(2,1)S(1)} %get-tuple-element.55), channel_id=1, source_target_pairs={{0,112},{1,113},{2,114},{3,115},{4,116},{5,117},{6,118},{7,119},{8... | collective-permute-start | bytes 786440 | tf_op jit(solution)/shard_map/ppermute | solution.py:28
  29.8 10.2 %collective-permute-start.7 = (bf16[1024,128]{1,0:T(8,128)(2,1)S(1)}, bf16[1024,128]{1,0:T(8,128)(2,1)S(1)}, u32[]{:S(2)}, u32[]{:S(2)}) collective-permute-start(bf16[1024,128]{1,0:T(8,128)(2,1)S(1)} %get-tuple-element.42.after), channel_id=1, source_target_pairs={{0,16},{1,17},{2,18},{3,19},{4,20},{5,21},{6,22},{7,23},{8,24},{9,... | collective-permute-start | bytes 786440 | tf_op jit(solution)/shard_map/ppermute | solution.py:28
  30.8 13.6 %collective-permute-start.15 = (bf16[1024,128]{1,0:T(8,128)(2,1)S(1)}, bf16[1024,128]{1,0:T(8,128)(2,1)S(1)}, u32[]{:S(2)}, u32[]{:S(2)}) collective-permute-start(bf16[1024,128]{1,0:T(8,128)(2,1)S(1)} %add_convert_fusion.5.after), channel_id=1, source_target_pairs={{0,112},{1,113},{2,114},{3,115},{4,116},{5,117},{6,118},{7,119},{8... | collective-permute-start | bytes 786440 | tf_op jit(solution)/shard_map/ppermute | solution.py:28
  34.1 12.0 %collective-permute-start.11 = (bf16[1024,128]{1,0:T(8,128)(2,1)S(1)}, bf16[1024,128]{1,0:T(8,128)(2,1)S(1)}, u32[]{:S(2)}, u32[]{:S(2)}) collective-permute-start(bf16[1024,128]{1,0:T(8,128)(2,1)S(1)} %add_convert_fusion.3), channel_id=1, source_target_pairs={{0,16},{1,17},{2,18},{3,19},{4,20},{5,21},{6,22},{7,23},{8,24},{9,... | collective-permute-start | bytes 786440 | tf_op jit(solution)/shard_map/ppermute | solution.py:28
  40.1 14.0 %collective-permute-start.8 = (bf16[1024,128]{1,0:T(8,128)(2,1)S(1)}, bf16[1024,128]{1,0:T(8,128)(2,1)S(1)}, u32[]{:S(2)}, u32[]{:S(2)}) collective-permute-start(bf16[1024,128]{1,0:T(8,128)(2,1)S(1)} %add_convert_fusion.4), channel_id=1, source_target_pairs={{0,144},{1,145},{2,146},{3,147},{4,148},{5,149},{6,150},{7,151},{8... | collective-permute-start | bytes 786440 | tf_op jit(solution)/shard_map/ppermute | solution.py:28
  40.2 17.1 %collective-permute-start.18 = (bf16[1024,128]{1,0:T(8,128)(2,1)S(1)}, bf16[1024,128]{1,0:T(8,128)(2,1)S(1)}, u32[]{:S(2)}, u32[]{:S(2)}) collective-permute-start(bf16[1024,128]{1,0:T(8,128)(2,1)S(1)} %add_convert_fusion), channel_id=1, source_target_pairs={{0,112},{1,113},{2,114},{3,115},{4,116},{5,117},{6,118},{7,119},{8... | collective-permute-start | bytes 786440 | tf_op jit(solution)/shard_map/ppermute | solution.py:28
  44.4 12.5 %collective-permute-start.16 = (bf16[1024,128]{1,0:T(8,128)(2,1)S(1)}, bf16[1024,128]{1,0:T(8,128)(2,1)S(1)}, u32[]{:S(2)}, u32[]{:S(2)}) collective-permute-start(bf16[1024,128]{1,0:T(8,128)(2,1)S(1)} %add_convert_fusion.1), channel_id=1, source_target_pairs={{0,240},{1,241},{2,242},{3,243},{4,244},{5,245},{6,246},{7,247},{8... | collective-permute-start | bytes 786440 | tf_op jit(solution)/shard_map/ppermute | solution.py:28
  46.2 11.2 %collective-permute-start.12 = (bf16[1024,128]{1,0:T(8,128)(2,1)S(1)}, bf16[1024,128]{1,0:T(8,128)(2,1)S(1)}, u32[]{:S(2)}, u32[]{:S(2)}) collective-permute-start(bf16[1024,128]{1,0:T(8,128)(2,1)S(1)} %add_convert_fusion.2), channel_id=1, source_target_pairs={{0,16},{1,17},{2,18},{3,19},{4,20},{5,21},{6,22},{7,23},{8,24},{9,... | collective-permute-start | bytes 786440 | tf_op jit(solution)/shard_map/ppermute | solution.py:28
  54.0 11.4 %copy-start.3 = (f32[1024,128]{1,0:T(8,128)S(1)}, f32[1024,128]{1,0:T(8,128)}, u32[]{:S(2)}) copy-start(f32[1024,128]{1,0:T(8,128)} %param.11) | copy-start | bytes 1572868
  54.0 8.3 %collective-permute-start.9 = (bf16[1024,128]{1,0:T(8,128)(2,1)S(1)}, bf16[1024,128]{1,0:T(8,128)(2,1)S(1)}, u32[]{:S(2)}, u32[]{:S(2)}) collective-permute-start(bf16[1024,128]{1,0:T(8,128)(2,1)S(1)} %get-tuple-element.49), channel_id=1, source_target_pairs={{0,128},{1,129},{2,130},{3,131},{4,132},{5,133},{6,134},{7,135},{8... | collective-permute-start | bytes 786440 | tf_op jit(solution)/shard_map/ppermute | solution.py:28
  57.7 7.7 %collective-permute-start.14 = (bf16[1024,128]{1,0:T(8,128)(2,1)S(1)}, bf16[1024,128]{1,0:T(8,128)(2,1)S(1)}, u32[]{:S(2)}, u32[]{:S(2)}) collective-permute-start(bf16[1024,128]{1,0:T(8,128)(2,1)S(1)} %get-tuple-element.56), channel_id=1, source_target_pairs={{0,16},{1,17},{2,18},{3,19},{4,20},{5,21},{6,22},{7,23},{8,24},{9,... | collective-permute-start | bytes 786440 | tf_op jit(solution)/shard_map/ppermute | solution.py:28
  57.8 7.6 %collective-permute-start.19 = (bf16[1024,128]{1,0:T(8,128)(2,1)S(1)}, bf16[1024,128]{1,0:T(8,128)(2,1)S(1)}, u32[]{:S(2)}, u32[]{:S(2)}) collective-permute-start(bf16[1024,128]{1,0:T(8,128)(2,1)S(1)} %get-tuple-element.57), channel_id=1, source_target_pairs={{0,112},{1,113},{2,114},{3,115},{4,116},{5,117},{6,118},{7,119},{8... | collective-permute-start | bytes 786440 | tf_op jit(solution)/shard_map/ppermute | solution.py:28
